TPU v7x, 512 devices: a whole 4x8x8 slice. The times are simulated.
512 devices in a mesh: pack: 32 (over x, z), seq: 16 (over y, core).
Axes of the slice: x: 4, y: 8, z: 8, core: 2. Of those that a mesh axis runs over, the one named last changes fastest.
Arguments:
- source: bfloat16 [16, 6144, 1152], P('seq', 'pack')
- destination: int32 [16, 6144], P('seq', 'pack'), may hold values from 0 to 6143, as said below
- doc_ids: int32 [32, 3072], P('pack'), may hold values from 0 to 23, as said below
- w_qkv: bfloat16 [3, 1152, 1152], P(None, None, 'seq')
- w_out: bfloat16 [1152, 1152], P('seq'), may hold values from -0.1875 to 0.1875
Outputs:
- projected: bfloat16 [32, 3072, 1152], P('pack', 'seq')
Inputs may be any that keep to these rules, and one draw needn't show every extreme that they name: For every column s, destination[s] is a permutation of 0 to 6143. Of the 192 rows of one device, at most 12 have the same destination // 192, and in every column some device sends exactly 12 rows to one owner. doc_ids[p] starts at 0, never falls, rises by one at most from one position to the next and changes only at positions that are multiples of 128; some packed row reaches the largest value.
All inputs are finite; a program needn't handle non-finite values.
Results may differ from a plain program's by a relative error of at most 0.011.
Values may be sent and summed in bfloat16 or wider, within the bound.
No kernel may reach another device: no remote copies, remote signals or barrier semaphores. Data moves between devices by JAX's collectives and lax.ppermute only.
A program may use at most 64 MiB of HBM per device.

v0:
```python
import math

import jax
import jax.numpy as jnp
from jax import lax
from jax.sharding import PartitionSpec as P

HD = 72


def block_rows(length):
    best = 1
    for candidate in range(1, min(length, 512) + 1):
        if length % candidate == 0:
            best = candidate
    return best


def attend_head(queries, key_rows, value_rows, documents):
    length = queries.shape[0]
    height = block_rows(length)

    def one_block(number):
        query_blk = lax.dynamic_slice_in_dim(queries, number * height, height, 0)
        doc_blk = lax.dynamic_slice_in_dim(documents, number * height, height, 0)
        scores = jnp.einsum(
            "qc,kc->qk", query_blk, key_rows, preferred_element_type=jnp.float32
        ) / math.sqrt(HD)
        scores = jnp.where(doc_blk[:, None] == documents[None, :], scores, -jnp.inf)
        highest = jnp.max(scores, axis=1, keepdims=True)
        expo = jnp.exp(scores - highest)
        weights = (expo / jnp.sum(expo, axis=1, keepdims=True)).astype(jnp.bfloat16)
        return jnp.dot(weights, value_rows, preferred_element_type=jnp.float32).astype(jnp.bfloat16)

    blocks = lax.map(one_block, jnp.arange(length // height, dtype=jnp.int32))
    return blocks.reshape(length, queries.shape[1])


def body(source, destination, doc_ids, w_qkv, w_out):
    pack_count = lax.axis_size("pack")
    tok_dev = source.shape[1]
    width = source.shape[2]
    capacity = 2 * tok_dev // pack_count
    my_rows = source[0]
    targets = destination[0]
    owners = targets // tok_dev
    places = targets % tok_dev
    matches = owners[:, None] == jnp.arange(pack_count, dtype=jnp.int32)[None, :]
    counted = jnp.cumsum(matches.astype(jnp.int32), axis=0)
    slots = jnp.sum(jnp.where(matches, counted, 0), axis=1) - 1
    flat_slot = owners * capacity + slots
    outbox = jnp.zeros((pack_count * capacity, width), jnp.bfloat16).at[flat_slot].set(my_rows)
    labels = jnp.full((pack_count * capacity,), tok_dev, jnp.int32).at[flat_slot].set(places)
    inbox, arrived = (
        lax.all_to_all(
            outbox.reshape(pack_count, capacity, width),
            "pack",
            split_axis=0,
            concat_axis=0,
            tiled=True,
        ),
        lax.all_to_all(
            labels.reshape(pack_count, capacity), "pack", split_axis=0, concat_axis=0, tiled=True
        ),
    )
    packed = (
        jnp.zeros((tok_dev, width), jnp.bfloat16)
        .at[arrived.reshape(-1)]
        .set(inbox.reshape(-1, width), mode="drop")
    )
    local_qkv = jnp.einsum(
        "td,jdc->jtc",
        packed,
        lax.all_gather(w_qkv, "seq", axis=2, tiled=True),
        preferred_element_type=jnp.float32,
    ).astype(jnp.bfloat16)
    heads_qkv = lax.all_to_all(local_qkv, "seq", split_axis=2, concat_axis=1, tiled=True)
    documents = doc_ids[0]
    attended_list = attend_head(
        heads_qkv[0, :, 0:HD], heads_qkv[1, :, 0:HD], heads_qkv[2, :, 0:HD], documents
    )
    token_major = lax.all_to_all(attended_list, "seq", split_axis=0, concat_axis=1, tiled=True)
    summed = jnp.dot(
        token_major,
        lax.all_gather(w_out, "seq", axis=0, tiled=True),
        preferred_element_type=jnp.float32,
    )
    return summed.astype(jnp.bfloat16)[None]


def solution(mesh):
    placed = (
        P("seq", "pack", None),
        P("seq", "pack"),
        P("pack", None),
        P(None, None, "seq"),
        P("seq", None),
    )
    return jax.shard_map(
        body, mesh=mesh, in_specs=placed, out_specs=P("pack", "seq", None), check_vma=False
    )
```

profile of v0, /device:TPU:7, one launch (start us, length us, event | category | flops | bytes accessed | tf_op | source)
XLA Modules:
  0.0 223.5 jit_solution(14568556036094130002)
XLA Ops:
  6.5 0.7 all-gather.3.cloned.1.call-update
  7.3 0.7 compare_reduce_fusion
  8.0 0.7 broadcast_remainder_fusion
  8.7 0.6 reduce-window.6
  9.6 0.7 compare_select_fusion.1
  10.3 1.2 scatter_custom_fusion
  11.5 0.7 all_to_all.34
  12.2 12.9 %all-to-all-start = ((s32[32,1,12]{2,1,0:T(1,128)}), s32[32,1,12]{2,1,0:T(1,128)S(1)}, u32[]{:S(2)}, u32[]{:S(2)}) async-start(s32[32,1,12]{2,1,0:T(1,128)} %bitcast.11), calls=%async_computation | async-start | bytes 32768 | tf_op jit(solution)/shard_map/all_to_all | solution.py:62
  25.2 1.7 scatter_custom_fusion.1
  26.9 1.3 reshape.163
  28.2 3.9 %all-to-all-done = s32[32,1,12]{2,1,0:T(1,128)S(1)} async-done(((s32[32,1,12]{2,1,0:T(1,128)}), s32[32,1,12]{2,1,0:T(1,128)S(1)}, u32[]{:S(2)}, u32[]{:S(2)}) %all-to-all-start) | async-done | bytes 1568 | tf_op jit(solution)/shard_map/all_to_all | solution.py:62
  32.1 5.5 %all-to-all-start.1 = ((bf16[32,12,1152]{2,1,0:T(8,128)(2,1)}), bf16[32,12,1152]{2,1,0:T(8,128)(2,1)S(1)}, u32[]{:S(2)}, u32[]{:S(2)}) async-start(bf16[32,12,1152]{2,1,0:T(8,128)(2,1)} %reshape.163), calls=%async_computation.1 | async-start | bytes 2359296 | tf_op jit(solution)/shard_map/all_to_all | solution.py:55
  38.2 0.7 reduce.9
  39.0 24.3 %all-to-all-done.1 = bf16[32,12,1152]{2,1,0:T(8,128)(2,1)S(1)} async-done(((bf16[32,12,1152]{2,1,0:T(8,128)(2,1)}), bf16[32,12,1152]{2,1,0:T(8,128)(2,1)S(1)}, u32[]{:S(2)}, u32[]{:S(2)}) %all-to-all-start.1) | async-done | bytes 884768 | tf_op jit(solution)/shard_map/all_to_all | solution.py:55
  63.5 2.2 %scatter_custom_fusion.2 = bf16[192,1152]{1,0:T(8,128)(2,1)S(1)} fusion(s32[384]{0:T(512)S(1)} %fusion.16, bf16[384,1152]{1,0:T(8,128)(2,1)S(1)} %reshape.186, bf16[]{:T(256)} %constant.52.clone.1), kind=kCustom, calls=%fused_computation.21 | custom fusion | bytes 442370 | tf_op jit(solution)/shard_map/scatter | solution.py:69
  65.7 5.0 %all-gather.3.cloned.1.call-done = bf16[3,1152,1152]{1,2,0:T(8,128)(2,1)} async-done(((bf16[3,1152,72]{1,2,0:T(8,128)(2,1)}), bf16[3,1152,1152]{1,2,0:T(8,128)(2,1)}) %all-gather.3.cloned.1.call-update) | async-done | bytes 7962640 | tf_op jit(solution)/shard_map/all_gather | solution.py:74
  70.7 5.8 %fusion.7 = bf16[3,192,1152]{2,1,0:T(8,128)(2,1)S(1)} fusion(bf16[3,1152,1152]{1,2,0:T(8,128)(2,1)} %all-gather.3.cloned.1.call-done, bf16[192,1152]{1,0:T(8,128)(2,1)S(1)} %scatter_custom_fusion.2), kind=kOutput, calls=%fused_computation.14 | convolution fusion | flops 1529487360 | bytes 9732096 | tf_op jit(solution)/shard_map/td,jdc->jtc/dot_general | solution.py:71
  76.5 3.2 %copy.28 = bf16[3,192,1152]{1,0,2:T(4,128)(2,1)} copy(bf16[3,192,1152]{2,1,0:T(8,128)(2,1)S(1)} %fusion.7) | data formatting | bytes 2654208 | tf_op jit(solution)/shard_map/convert_element_type | solution.py:76
  79.7 7.0 %all-to-all-start.2 = ((bf16[3,192,1152]{1,0,2:T(4,128)(2,1)}), bf16[3,192,1152]{1,0,2:T(4,128)(2,1)S(1)}, u32[]{:S(2)}, u32[]{:S(2)}) async-start(bf16[3,192,1152]{1,0,2:T(4,128)(2,1)} %copy.28), calls=%async_computation.2 | async-start | bytes 4718592 | tf_op jit(solution)/shard_map/all_to_all | solution.py:77
  87.4 64.9 %all-to-all-done.2 = bf16[3,192,1152]{1,0,2:T(4,128)(2,1)S(1)} async-done(((bf16[3,192,1152]{1,0,2:T(4,128)(2,1)}), bf16[3,192,1152]{1,0,2:T(4,128)(2,1)S(1)}, u32[]{:S(2)}, u32[]{:S(2)}) %all-to-all-start.2) | async-done | bytes 1327136 | tf_op jit(solution)/shard_map/all_to_all | solution.py:77
  153.8 33.3 %while.10 = (s32[]{:T(128)}, bf16[6,512,72]{1,2,0:T(8,128)(2,1)}, s32[6]{0:T(128)S(1)}, s32[3072]{0:T(1024)S(1)}, s32[1,3072]{1,0:T(1,128)S(1)}, /*index=5*/bf16...) while((s32[]{:T(128)}, bf16[6,512,72]{1,2,0:T(8,128)(2,1)}, ...), condition=%wide.region_9.10_spmd, body=%wide.region_6.9_spmd.sunk | while | flops 467176448 | bytes 20337336 | solution.py:35
  153.8 0.6 dynamic_slice.18
  155.1 1.2 fusion.33
  156.3 1.0 fusion.34
  157.3 2.1 fusion.35
  160.6 1.2 fusion.33
  161.8 1.0 fusion.34
  162.8 2.1 fusion.35
  166.2 1.2 fusion.33
  167.4 1.0 fusion.34
  168.4 2.1 fusion.35
  170.5 0.6 dynamic_slice.18
  171.7 1.2 fusion.33
  172.9 1.0 fusion.34
  173.9 2.1 fusion.35
  176.0 0.6 dynamic_slice.18
  177.3 1.2 fusion.33
  178.5 1.0 fusion.34
  179.5 2.1 fusion.35
  182.8 1.2 fusion.33
  184.0 1.0 fusion.34
  185.0 2.1 fusion.35
  187.1 1.1 copy.36
  188.3 0.7 all_to_all.40
  189.0 1.0 copy.37
  190.0 4.7 %all-to-all-start.3 = ((bf16[16,192,72]{1,2,0:T(8,128)(2,1)}), bf16[16,192,72]{1,2,0:T(8,128)(2,1)S(1)}, u32[]{:S(2)}, u32[]{:S(2)}) async-start(bf16[16,192,72]{1,2,0:T(8,128)(2,1)} %copy.37), calls=%async_computation.3 | async-start | bytes 1179648 | tf_op jit(solution)/shard_map/all_to_all | solution.py:82
  194.7 18.6 %all-to-all-done.3 = bf16[16,192,72]{1,2,0:T(8,128)(2,1)S(1)} async-done(((bf16[16,192,72]{1,2,0:T(8,128)(2,1)}), bf16[16,192,72]{1,2,0:T(8,128)(2,1)S(1)}, u32[]{:S(2)}, u32[]{:S(2)}) %all-to-all-start.3) | async-done | bytes 442400 | tf_op jit(solution)/shard_map/all_to_all | solution.py:82
  213.3 3.3 %fusion.8 = bf16[1,192,1152]{2,1,0:T(8,128)(2,1)} fusion(bf16[192,1152]{0,1:T(8,128)(2,1)S(1)} %bitcast.69, bf16[1152,1152]{1,0:T(8,128)(2,1)} %all-gather.5.cloned.1.call-done), kind=kOutput, calls=%fused_computation.16 | convolution fusion | flops 509829120 | bytes 3538944 | tf_op jit(solution)/shard_map/dot_general | solution.py:83
  (37 shorter events, 5.7 us)
Async XLA Ops:
  6.5 18.6 %copy-start = (bf16[1,192,1152]{2,1,0:T(8,128)(2,1)S(1)}, bf16[1,192,1152]{2,1,0:T(8,128)(2,1)}, u32[]{:S(2)}) copy-start(bf16[1,192,1152]{2,1,0:T(8,128)(2,1)} %param.7) | copy-start | bytes 1327108
  6.5 64.2 %all-gather.3.cloned.1.call-start = ((), (), s32[]{:S(2)}) async-start(), calls=%async_computation.4 | async-start | bytes 8460288 | tf_op jit(solution)/shard_map/all_gather | solution.py:74
  12.2 19.9 %all-to-all-start = ((s32[32,1,12]{2,1,0:T(1,128)}), s32[32,1,12]{2,1,0:T(1,128)S(1)}, u32[]{:S(2)}, u32[]{:S(2)}) async-start(s32[32,1,12]{2,1,0:T(1,128)} %bitcast.11), calls=%async_computation | async-start | bytes 32768 | tf_op jit(solution)/shard_map/all_to_all | solution.py:62
  32.1 31.2 %all-to-all-start.1 = ((bf16[32,12,1152]{2,1,0:T(8,128)(2,1)}), bf16[32,12,1152]{2,1,0:T(8,128)(2,1)S(1)}, u32[]{:S(2)}, u32[]{:S(2)}) async-start(bf16[32,12,1152]{2,1,0:T(8,128)(2,1)} %reshape.163), calls=%async_computation.1 | async-start | bytes 2359296 | tf_op jit(solution)/shard_map/all_to_all | solution.py:55
  79.7 72.6 %all-to-all-start.2 = ((bf16[3,192,1152]{1,0,2:T(4,128)(2,1)}), bf16[3,192,1152]{1,0,2:T(4,128)(2,1)S(1)}, u32[]{:S(2)}, u32[]{:S(2)}) async-start(bf16[3,192,1152]{1,0,2:T(4,128)(2,1)} %copy.28), calls=%async_computation.2 | async-start | bytes 4718592 | tf_op jit(solution)/shard_map/all_to_all | solution.py:77
  86.6 67.2 %copy-start.1 = (s32[1,3072]{1,0:T(1,128)S(1)}, s32[1,3072]{1,0:T(1,128)}, u32[]{:S(2)}) copy-start(s32[1,3072]{1,0:T(1,128)} %param.9) | copy-start | bytes 36868
  86.6 108.0 %all-gather.5.cloned.1.call-start = ((), (), s32[]{:S(2)}) async-start(), calls=%async_computation.5 | async-start | bytes 2820096 | tf_op jit(solution)/shard_map/all_gather | solution.py:85
  190.0 23.3 %all-to-all-start.3 = ((bf16[16,192,72]{1,2,0:T(8,128)(2,1)}), bf16[16,192,72]{1,2,0:T(8,128)(2,1)S(1)}, u32[]{:S(2)}, u32[]{:S(2)}) async-start(bf16[16,192,72]{1,2,0:T(8,128)(2,1)} %copy.37), calls=%async_computation.3 | async-start | bytes 1179648 | tf_op jit(solution)/shard_map/all_to_all | solution.py:82
Sparse Core Ops, SparseCore 0:
  9.4 61.2 all-gather.2
  89.6 65.8 all-gather.4
where the time goes:
time: 228 us; the launch traced here: 223 us
  waiting for transfers between devices  118 us (52%)
  starting transfers between devices  30.3 us (13%)
  matrix products  29.1 us (13%)
  local copies, waits for them, and re-layouts  19.6 us (9%)
  between operations  13.6 us (6%)
  other arithmetic  9.53 us (4%)
  loops' own time  3.45 us (2%)
    all_to_all x1, waiting for transfers between devices, body(): lax.all_to_all(local_qkv, 'seq', split_axis=2, concat_axis=1, tiled=True)  64.9 us
    all_to_all x1, waiting for transfers between devices, body(): lax.all_to_all(outbox.reshape(pack_count, capacity, width), 'pack', split...  24.3 us
    all_to_all x1, waiting for transfers between devices, body(): lax.all_to_all(attended_list, 'seq', split_axis=0, concat_axis=1, tiled=T...  18.6 us
    all_to_all x1, starting transfers between devices, body(): lax.all_to_all(labels.reshape(pack_count, capacity), 'pack', split_axis=0...  12.9 us
    dot_general x6, matrix products, one_block(): jnp.dot(weights, value_rows, preferred_element_type=jnp.float32)  12.8 us
    dot_general x6, matrix products, one_block(): jnp.einsum('qc,kc->qk', query_blk, key_rows, preferred_element_type=jnp.f...  7.18 us
    all_to_all x1, starting transfers between devices, body(): lax.all_to_all(local_qkv, 'seq', split_axis=2, concat_axis=1, tiled=True)  6.96 us
    reduce_sum x6, other arithmetic, one_block(): weights = (expo / jnp.sum(expo, axis=1, keepdims=True)).astype(jnp.bfloat16)  5.96 us
  transfers between devices with their start and end apart: 6, of which 5 were waited for; matrix products, arithmetic and copies ran while one was open for 20% of the time, Pallas kernels for 0%

commit v1 on v0

v1 whole, which is shorter than its diff:
```python
import functools
import math

import jax
import jax.numpy as jnp
from jax import lax
from jax.experimental import pallas as pl
from jax.experimental.pallas import tpu as pltpu
from jax.sharding import PartitionSpec as P

HD = 72
CAP = 12
LANES = 128
BLK = 128
BF = jnp.bfloat16
F32 = jnp.float32
NT = (((1,), (1,)), ((), ()))

SHIFTS = (
    (0, ((0, 0), (3, 4), (6, 8))),
    (-12, ((0, 1), (3, 5))),
    (4, ((1, 1), (4, 5))),
    (-8, ((1, 2), (4, 6))),
    (8, ((2, 2), (5, 6))),
    (-4, ((2, 3), (5, 7))),
)
TILES = 7


def iota(shape, dim):
    return lax.broadcasted_iota(jnp.int32, shape, dim)


def onehot(condition):
    return jnp.where(condition, 1.0, 0.0).astype(BF)


def pack_kernel(n_pack, dest_ref, rows_ref, out_ref):
    tok = rows_ref.shape[0]
    group = n_pack * 16
    dest = dest_ref[...]
    owner = ((dest >> 6) * 171) >> 9
    place = dest - owner * tok
    owned = iota((n_pack, tok), 0) == owner
    before = onehot(iota((tok, tok), 0) < iota((tok, tok), 1))
    counted = jnp.dot(onehot(owned), before, preferred_element_type=F32)
    slot = jnp.sum(jnp.where(owned, counted, 0.0), axis=0, keepdims=True).astype(jnp.int32)
    row = iota((group, tok), 0)
    parts = {}
    for shift, pairs in SHIFTS:
        at = slot - shift
        key = jnp.where((at >= 0) & (at < 16), owner * 16 + at, -1)
        picked = jnp.concatenate(
            [rows_ref[:, f * LANES : (f + 1) * LANES] for _, f in pairs], axis=1
        )
        moved = jnp.dot(onehot(row == key), picked, preferred_element_type=F32)
        for n, (tile, _) in enumerate(pairs):
            parts.setdefault(tile, []).append(moved[:, n * LANES : (n + 1) * LANES])
    tags = jnp.where(iota((LANES, tok), 0) == slot, (place + 1).astype(F32), 0.0).astype(BF)
    here = onehot(row == owner * 16 + CAP)
    parts[TILES - 1].append(lax.dot_general(here, tags, NT, preferred_element_type=F32))
    for tile in range(TILES):
        whole = functools.reduce(lambda a, b: a + b, parts[tile])
        out_ref[:, tile * 16 : (tile + 1) * 16, :] = whole.astype(BF).reshape(n_pack, 16, LANES)


def unpack_kernel(n_pack, in_ref, out_ref):
    tok = out_ref.shape[0]
    group = n_pack * 16
    tiles = [in_ref[:, t * 16 : (t + 1) * 16, :].reshape(group, LANES) for t in range(TILES)]
    col = iota((n_pack, group), 1)
    lead = iota((n_pack, group), 0) * 16
    labels = jnp.dot(onehot(col == lead + CAP), tiles[-1], preferred_element_type=F32).astype(BF)
    mine = (col >= lead) & (col < lead + 16)
    offset = iota((LANES, group), 0) - (iota((LANES, group), 1) & 15)
    place = iota((tok, group), 0) + 1
    parts = {}
    for shift, pairs in SHIFTS:
        spread = jnp.dot(labels, onehot(offset == shift), preferred_element_type=F32)
        label = jnp.sum(jnp.where(mine, spread, 0.0), axis=0, keepdims=True).astype(jnp.int32)
        picked = jnp.concatenate([tiles[t] for t, _ in pairs], axis=1)
        moved = jnp.dot(onehot(place == label), picked, preferred_element_type=F32)
        for n, (_, f) in enumerate(pairs):
            parts.setdefault(f, []).append(moved[:, n * LANES : (n + 1) * LANES])
    for f in sorted(parts):
        whole = functools.reduce(lambda a, b: a + b, parts[f])
        out_ref[:, f * LANES : (f + 1) * LANES] = whole.astype(BF)


TOKT = 256
QT = 256
KT = 512
AROWS = 112
NEG = -3e38
LIMIT = pltpu.CompilerParams(vmem_limit_bytes=56 * 2**20)


def attend_kernel(steps, n_seq, doc_ref, x_ref, w_ref, out_ref, q_s, k_s, v_s, o_s, bound_s):
    step = pl.program_id(0)
    rows = pl.ds(pl.multiple_of(step * TOKT, TOKT), TOKT)
    x = x_ref[...]
    qkv = [
        lax.dot_general(x, w_ref[j], NT, preferred_element_type=F32).astype(BF) for j in range(3)
    ]
    q_s[rows, :] = qkv[0]
    k_s[rows, :] = qkv[1]
    v_s[rows, 0:HD] = qkv[2]
    v_s[rows, HD:LANES] = jnp.where(iota((TOKT, LANES - HD), 1) == 0, 1.0, 0.0).astype(BF)

    @pl.when(step == steps - 1)
    def _():
        length = k_s.shape[0] - KT
        blocks = length // BLK
        scale = math.log2(math.e) / math.sqrt(HD)
        k_s[length:, :] = jnp.zeros((KT, HD), BF)
        v_s[length:, :] = jnp.zeros((KT, LANES), BF)
        first = jnp.int32(0)
        for b in range(blocks):
            if b:
                first = jnp.where(doc_ref[0, b * BLK] == doc_ref[0, (b - 1) * BLK], first, b)
            bound_s[0, b] = first
        last = jnp.int32(blocks)
        for b in reversed(range(blocks)):
            if b < blocks - 1:
                last = jnp.where(doc_ref[0, b * BLK] == doc_ref[0, (b + 1) * BLK], last, b + 1)
            bound_s[1, b] = last
        per = QT // BLK

        def one_tile(t, _):
            q = q_s[pl.ds(pl.multiple_of(t * QT, QT), QT), :]
            lo = bound_s[0, t * per]
            hi = bound_s[1, t * per + per - 1]
            chunks = (hi - lo + KT // BLK - 1) // (KT // BLK)

            def one_chunk(c, carry):
                high, total = carry
                begin = lo + c * (KT // BLK)
                keys = pl.ds(pl.multiple_of(begin * BLK, BLK), KT)
                scores = lax.dot_general(q, k_s[keys, :], NT, preferred_element_type=F32)
                block = begin + iota((1, KT), 1) // BLK
                halves = []
                for i in range(per):
                    keep = (block >= bound_s[0, t * per + i]) & (block < bound_s[1, t * per + i])
                    halves.append(
                        jnp.where(keep, scores[i * BLK : (i + 1) * BLK, :], -jnp.inf)
                    )
                scores = jnp.concatenate(halves, axis=0)
                newer = jnp.maximum(high, jnp.max(scores, axis=1, keepdims=True))
                expo = jnp.exp2((scores - newer) * scale).astype(BF)
                total = total * jnp.exp2((high - newer) * scale) + jnp.dot(
                    expo, v_s[keys, :], preferred_element_type=F32
                )
                return newer, total

            high = jnp.full((QT, 1), NEG, F32)
            total = jnp.zeros((QT, LANES), F32)
            _, total = lax.fori_loop(0, chunks, one_chunk, (high, total))
            done = total[:, 0:HD] / total[:, HD : HD + 1]
            o_s[pl.ds(pl.multiple_of(t * QT, QT), QT), 0:HD] = done
            return 0

        lax.fori_loop(0, length // QT, one_tile, 0)
        tok = length // n_seq
        for s in range(n_seq):
            turned = o_s[s * tok : (s + 1) * tok, :].T
            out_ref[s, 0:64, :] = turned[0:64, 0:LANES].astype(BF)
            out_ref[s, 64:96, :] = jnp.concatenate(
                [turned[0:32, LANES:tok], turned[32:64, LANES:tok]], axis=1
            ).astype(BF)
            out_ref[s, 96:112, :] = jnp.concatenate(
                [
                    turned[64:72, 0:LANES],
                    jnp.concatenate(
                        [turned[64:72, LANES:tok], jnp.zeros((8, 2 * LANES - tok), F32)], axis=1
                    ),
                ],
                axis=0,
            ).astype(BF)


def project_kernel(n_seq, in_ref, w_ref, out_ref):
    width = out_ref.shape[1]
    tok = out_ref.shape[0]
    rest = tok - LANES
    lo = in_ref[:, 0:32, :].reshape(n_seq * 32, LANES)
    hi = in_ref[:, 32:64, :].reshape(n_seq * 32, LANES)
    far = in_ref[:, 64:96, :].reshape(n_seq * 32, LANES)
    tail = in_ref[:, 96:112, :].reshape(n_seq * 16, LANES).astype(F32)
    upper = (iota(tail.shape, 0) & 15) < 8
    tail_near = jnp.where(upper, tail, 0.0).astype(BF)
    tail_far = jnp.where(upper, 0.0, tail).astype(BF)
    near = jnp.concatenate([lo, hi, tail_near], axis=0).T
    far_t = far.T
    distant = jnp.concatenate([far_t[0:rest], far_t[rest:LANES], tail_far.T[0:rest]], axis=1)
    left = jnp.concatenate([near, distant], axis=0)
    weights = jnp.concatenate(
        [
            w_ref[:, 0:32, :].reshape(n_seq * 32, width),
            w_ref[:, 32:64, :].reshape(n_seq * 32, width),
            w_ref[:, 64:80, :].reshape(n_seq * 16, width),
        ],
        axis=0,
    )
    out_ref[...] = jnp.dot(left, weights, preferred_element_type=F32).astype(BF)


def whole(*shape):
    return pl.BlockSpec(shape, lambda *_: (0,) * len(shape))


def attend_call(doc_ids, tokens, w_t, n_seq):
    length, width = tokens.shape
    steps = length // TOKT
    return pl.pallas_call(
        functools.partial(attend_kernel, steps, n_seq),
        grid=(steps,),
        out_shape=jax.ShapeDtypeStruct((n_seq, AROWS, LANES), BF),
        in_specs=[
            pl.BlockSpec(memory_space=pltpu.SMEM),
            pl.BlockSpec((TOKT, width), lambda i: (i, 0)),
            whole(3, HD, width),
        ],
        out_specs=whole(n_seq, AROWS, LANES),
        scratch_shapes=[
            pltpu.VMEM((length, HD), BF),
            pltpu.VMEM((length + KT, HD), BF),
            pltpu.VMEM((length + KT, LANES), BF),
            pltpu.VMEM((length, LANES), F32),
            pltpu.SMEM((2, length // BLK), jnp.int32),
        ],
        compiler_params=LIMIT,
        name="attend",
    )(doc_ids, tokens, w_t)


def body(source, destination, doc_ids, w_qkv, w_out):
    n_pack = lax.axis_size("pack")
    n_seq = lax.axis_size("seq")
    tok, width = source.shape[1:]
    spare = jnp.concatenate([w_out, w_out[64:HD]], axis=0)
    w_all = lax.all_gather(spare, "seq", axis=0, tiled=False)

    outbox = pl.pallas_call(
        functools.partial(pack_kernel, n_pack),
        out_shape=jax.ShapeDtypeStruct((n_pack, TILES * 16, LANES), BF),
        compiler_params=LIMIT,
        name="pack_rows",
    )(destination, source[0])
    inbox = lax.all_to_all(outbox, "pack", split_axis=0, concat_axis=0, tiled=True)
    packed = pl.pallas_call(
        functools.partial(unpack_kernel, n_pack),
        out_shape=jax.ShapeDtypeStruct((tok, width), BF),
        compiler_params=LIMIT,
        name="unpack_rows",
    )(inbox)
    tokens = lax.all_gather(packed, "seq", axis=0, tiled=True)

    attended = attend_call(doc_ids, tokens, jnp.transpose(w_qkv, (0, 2, 1)), n_seq)
    blocks = lax.all_to_all(attended, "seq", split_axis=0, concat_axis=0, tiled=True)

    out = pl.pallas_call(
        functools.partial(project_kernel, n_seq),
        out_shape=jax.ShapeDtypeStruct((tok, width), BF),
        compiler_params=LIMIT,
        name="project",
    )(blocks, w_all)
    return out[None]


def solution(mesh):
    placed = (
        P("seq", "pack", None),
        P("seq", "pack"),
        P("pack", None),
        P(None, None, "seq"),
        P("seq", None),
    )
    return jax.shard_map(
        body, mesh=mesh, in_specs=placed, out_specs=P("pack", "seq", None), check_vma=False
    )
```

time: 228 us -> 165 us (0.72)
  waiting for transfers between devices: 118 us -> 75.5 us
  blocking collectives: 0 us -> 33.9 us
  Pallas kernels: 0 us -> 31.8 us
  matrix products: 29.1 us -> 0 us
  starting transfers between devices: 30.3 us -> 4.78 us
  local copies, waits for them, and re-layouts: 19.6 us -> 1.5 us
  other arithmetic: 9.53 us -> 1.61 us
  loops' own time: 3.45 us -> 0 us
    all_to_all x4 -> x1, waiting for transfers between devices: 112 us -> 0.01 us  [body(): lax.all_to_all(attended, 'seq', split_axis=0, concat_axis=0, tiled=True)]
    all_gather x2, waiting for transfers between devices: 4.98 us -> 75.5 us  [the longest x1 51.9 us: body(): tokens = lax.all_gather(packed, 'seq', axis=0, tiled=True)]
    all_to_all x0 -> x1, blocking collectives: none -> 33.9 us  [body(): lax.all_to_all(outbox, 'pack', split_axis=0, concat_axis=0, tiled=True)]
    pallas_call x0 -> x4, Pallas kernels: none -> 31.8 us  [the longest x1 22.4 us: attend_call(): pl.pallas_call(functools.partial(attend_kernel, steps, n_seq), grid=(step...]
    dot_general x14 -> x0, matrix products: 29.1 us -> none  [the longest x6 12.8 us: one_block(): jnp.dot(weights, value_rows, preferred_element_type=jnp.float32)]
    all_to_all x4 -> x1, starting transfers between devices: 30.1 us -> 4.73 us  [body(): lax.all_to_all(attended, 'seq', split_axis=0, concat_axis=0, tiled=True)]
    reduce_sum x7 -> x0, other arithmetic: 6 us -> none  [the longest x6 5.96 us: one_block(): weights = (expo / jnp.sum(expo, axis=1, keepdims=True)).astype(jnp.bfloat16)]
    scatter x3 -> x0, local copies, waits for them, and re-layouts: 5.14 us -> none  [the longest x1 2.24 us: body(): packed = jnp.zeros((tok_dev, width), jnp.bfloat16).at[arrived.reshape(-1)...]
  transfers between devices with their start and end apart: 6 -> 3, of which waited for: 5 -> 2; matrix products, arithmetic and copies ran while one was open for 20% -> 1% of each run, Pallas kernels for 0% -> 14%
where the time goes in v1:
time: 165 us; the launch traced here: 163 us
  waiting for transfers between devices  75.5 us (46%)
  blocking collectives  33.9 us (21%)
  Pallas kernels  31.8 us (19%)
  between operations  13.4 us (8%)
  starting transfers between devices  4.78 us (3%)
    all_gather x1, waiting for transfers between devices, body(): tokens = lax.all_gather(packed, 'seq', axis=0, tiled=True)  51.9 us
    all_to_all x1, blocking collectives, body(): lax.all_to_all(outbox, 'pack', split_axis=0, concat_axis=0, tiled=True)  33.9 us
    all_gather x1, waiting for transfers between devices, body(): w_all = lax.all_gather(spare, 'seq', axis=0, tiled=False)  23.6 us
    pallas_call x1, Pallas kernels, attend_call(): pl.pallas_call(functools.partial(attend_kernel, steps, n_seq), grid=(step...  22.4 us
    all_to_all x1, starting transfers between devices, body(): lax.all_to_all(attended, 'seq', split_axis=0, concat_axis=0, tiled=True)  4.73 us
    pallas_call x1, Pallas kernels, body(): pl.pallas_call(functools.partial(project_kernel, n_seq), out_shape=jax.Sh...  3.59 us
  transfers between devices with their start and end apart: 3, of which 2 were waited for; matrix products, arithmetic and copies ran while one was open for 1% of the time, Pallas kernels for 14%

profile of v1, /device:TPU:7, one launch (start us, length us, event | category | flops | bytes accessed | tf_op | source)
XLA Modules:
  0.0 162.6 jit_solution(14782139405563921394)
XLA Ops:
  6.5 0.0 all-gather.4.cloned.1.call-start
  6.5 2.8 %pack_rows.1 = bf16[32,112,128]{2,1,0:T(8,128)(2,1)} custom-call(s32[1,192]{1,0:T(1,128)} %dest_ref.1, bf16[192,1152]{1,0:T(8,128)(2,1)} %bitcast.6), custom_call_target="tpu_custom_call" | custom-call | tf_op jit(solution)/shard_map/pack_rows/pallas_call | solution.py:243
  9.4 33.9 %all_to_all.10.in_ref = bf16[32,112,128]{2,1,0:T(8,128)(2,1)} all-to-all(bf16[32,112,128]{2,1,0:T(8,128)(2,1)} %pack_rows.1), channel_id=1, replica_groups=mesh['pack'=32,'seq'=16] {'pack'}, dimensions={0} | all-to-all | bytes 1835008 | tf_op jit(solution)/shard_map/all_to_all | solution.py:249
  43.3 3.1 %unpack_rows.1 = bf16[192,1152]{1,0:T(8,128)(2,1)} custom-call(bf16[32,112,128]{2,1,0:T(8,128)(2,1)} %all_to_all.10.in_ref), custom_call_target="tpu_custom_call" | custom-call | tf_op jit(solution)/shard_map/unpack_rows/pallas_call | solution.py:250
  46.4 0.0 all-gather.4.cloned.1.call-update
  46.4 0.0 all-gather.6.cloned.1.call-start
  46.4 0.7 slice.3
  47.2 1.6 pad_maximum_fusion
  48.8 0.0 all-gather.6.cloned.1.call-update
  48.8 51.9 %all-gather.4.cloned.1.call-done.x_ref = bf16[3072,1152]{1,0:T(8,128)(2,1)} async-done(((bf16[192,1152]{1,0:T(8,128)(2,1)}), bf16[3072,1152]{1,0:T(8,128)(2,1)}) %all-gather.4.cloned.1.call-update) | async-done | bytes 7077904 | tf_op jit(solution)/shard_map/all_gather | solution.py:256
  100.7 22.4 %attend.1 = bf16[16,112,128]{2,1,0:T(8,128)(2,1)} custom-call(s32[1,3072]{1,0:T(1,128)} %doc_ref.1, bf16[3072,1152]{1,0:T(8,128)(2,1)} %all-gather.4.cloned.1.call-done.x_ref, bf16[3,72,1152]{2,1,0:T(8,128)(2,1)} %bitcast.5), custom_call_target="tpu_custom_call" | custom-call | tf_op jit(solution)/shard_map/attend/pallas_call | solution.py:214
  123.0 4.7 %all-to-all-start.1 = ((bf16[16,112,128]{2,1,0:T(8,128)(2,1)}), bf16[16,112,128]{2,1,0:T(8,128)(2,1)S(1)}, u32[]{:S(2)}, u32[]{:S(2)}) async-start(bf16[16,112,128]{2,1,0:T(8,128)(2,1)} %attend.1), calls=%async_computation.1 | async-start | bytes 917504 | tf_op jit(solution)/shard_map/all_to_all | solution.py:259
  127.7 23.6 %all-gather.6.cloned.1.call-done = bf16[1280,1152]{1,0:T(8,128)(2,1)} async-done(((bf16[80,1152]{1,0:T(8,128)(2,1)}), bf16[1280,1152]{1,0:T(8,128)(2,1)}) %all-gather.6.cloned.1.call-update) | async-done | bytes 2949136 | tf_op jit(solution)/shard_map/all_gather | solution.py:241
  151.4 0.0 all-to-all-done.1.in_ref
  151.4 0.0 copy-start
  151.4 0.8 copy-done
  152.1 3.6 %project.1 = bf16[192,1152]{1,0:T(8,128)(2,1)} custom-call(bf16[16,112,128]{2,1,0:T(8,128)(2,1)} %copy-done, bf16[16,80,1152]{2,1,0:T(8,128)(2,1)} %bitcast.4), custom_call_target="tpu_custom_call" | custom-call | tf_op jit(solution)/shard_map/project/pallas_call | solution.py:261
Async XLA Ops:
  6.5 94.1 %all-gather.4.cloned.1.call-start = ((), (), s32[]{:S(2)}) async-start(), calls=%async_computation.2 | async-start | bytes 7520256 | tf_op jit(solution)/shard_map/all_gather | solution.py:256
  46.4 105.0 %all-gather.6.cloned.1.call-start = ((), (), s32[]{:S(2)}) async-start(), calls=%async_computation.3 | async-start | bytes 3133440 | tf_op jit(solution)/shard_map/all_gather | solution.py:241
  123.0 28.4 %all-to-all-start.1 = ((bf16[16,112,128]{2,1,0:T(8,128)(2,1)}), bf16[16,112,128]{2,1,0:T(8,128)(2,1)S(1)}, u32[]{:S(2)}, u32[]{:S(2)}) async-start(bf16[16,112,128]{2,1,0:T(8,128)(2,1)} %attend.1), calls=%async_computation.1 | async-start | bytes 917504 | tf_op jit(solution)/shard_map/all_to_all | solution.py:259
  151.4 0.8 copy-start
Sparse Core Ops, SparseCore 0:
  46.5 54.1 all-gather.3
  102.8 48.5 all-gather.5

commit v2 on v1

v2 whole, which is shorter than its diff:
```python
import functools
import math

import jax
import jax.numpy as jnp
from jax import lax
from jax.experimental import pallas as pl
from jax.experimental.pallas import tpu as pltpu
from jax.sharding import PartitionSpec as P

HD = 72
TOK = 192
CAP = 12
LANES = 128
BLK = 128
BF = jnp.bfloat16
F32 = jnp.float32
NT = (((1,), (1,)), ((), ()))

NEAR = 5
FAR = 4


def tile_shifts(chunks):
    found = {}
    for f in range(chunks):
        for t in range(CAP * f // 16, (CAP * f + CAP - 1) // 16 + 1):
            found.setdefault(16 * t - CAP * f, []).append((t, f))
    return found


def iota(shape, dim):
    return lax.broadcasted_iota(jnp.int32, shape, dim)


def onehot(condition):
    return jnp.where(condition, 1.0, 0.0).astype(BF)


def slots_of(dest, n_pack, tok):
    owner = ((dest >> 6) * 171) >> 9
    owned = iota((n_pack, tok), 0) == owner
    before = onehot(iota((tok, tok), 0) < iota((tok, tok), 1))
    counted = jnp.dot(onehot(owned), before, preferred_element_type=F32)
    slot = jnp.sum(jnp.where(owned, counted, 0.0), axis=0, keepdims=True).astype(jnp.int32)
    return owner, slot


def total_of(parts):
    return functools.reduce(lambda a, b: a + b, parts)


def pack_kernel(n_pack, chunks, first, labelled, dest_ref, rows_ref, out_ref):
    tok = rows_ref.shape[0]
    dest = dest_ref[...]
    owner, slot = slots_of(dest, n_pack, tok)
    row = iota((n_pack * 16, tok), 0)
    parts = {}
    for shift, pairs in tile_shifts(chunks).items():
        at = slot - shift
        key = jnp.where((at >= 0) & (at < 16), owner * 16 + at, -1)
        picked = jnp.concatenate(
            [rows_ref[:, (first + f) * LANES : (first + f + 1) * LANES] for _, f in pairs], axis=1
        )
        moved = jnp.dot(onehot(row == key), picked, preferred_element_type=F32)
        for n, (tile, _) in enumerate(pairs):
            parts.setdefault(tile, []).append(moved[:, n * LANES : (n + 1) * LANES])
    if labelled:
        place = dest - owner * tok
        tags = jnp.where(iota((LANES, tok), 0) == slot, (place + 1).astype(F32), 0.0).astype(BF)
        here = onehot(row == owner * 16 + CAP * chunks % 16)
        parts[max(parts)].append(lax.dot_general(here, tags, NT, preferred_element_type=F32))
    for tile in parts:
        block = total_of(parts[tile]).astype(BF)
        out_ref[:, tile * 16 : (tile + 1) * 16, :] = block.reshape(n_pack, 16, LANES)


def place_rows(n_pack, chunks, labels, in_ref, out_ref):
    tok = TOK
    group = n_pack * 16
    col = iota((n_pack, group), 1)
    lead = iota((n_pack, group), 0) * 16
    mine = (col >= lead) & (col < lead + 16)
    offset = iota((LANES, group), 0) - (iota((LANES, group), 1) & 15)
    place = iota((tok, group), 0) + 1
    parts = {}
    for shift, pairs in tile_shifts(chunks).items():
        spread = jnp.dot(labels, onehot(offset == shift), preferred_element_type=F32)
        label = jnp.sum(jnp.where(mine, spread, 0.0), axis=0, keepdims=True).astype(jnp.int32)
        picked = jnp.concatenate(
            [in_ref[:, t * 16 : (t + 1) * 16, :].reshape(group, LANES) for t, _ in pairs], axis=1
        )
        moved = jnp.dot(onehot(place == label), picked, preferred_element_type=F32)
        for n, (_, f) in enumerate(pairs):
            parts.setdefault(f, []).append(moved[:, n * LANES : (n + 1) * LANES])
    for f in parts:
        out_ref[0:tok, f * LANES : (f + 1) * LANES] = total_of(parts[f]).astype(BF)


def unpack_near_kernel(n_pack, in_ref, w_ref, out_ref, label_ref):
    group = n_pack * 16
    tile = in_ref[:, NEAR * CAP // 16 * 16 :, :].reshape(group, LANES)
    at = iota((n_pack, group), 0) * 16 + NEAR * CAP % 16
    labels = jnp.dot(
        onehot(iota((n_pack, group), 1) == at), tile, preferred_element_type=F32
    ).astype(BF)
    label_ref[...] = labels
    place_rows(n_pack, NEAR, labels, in_ref, out_ref)
    cut = NEAR * LANES
    rest = FAR * LANES
    out_ref[TOK : TOK + 64, :] = w_ref[0:64, 0:cut]
    out_ref[TOK + 64 : TOK + 128, 0:rest] = w_ref[0:64, cut:]
    out_ref[TOK + 64 : TOK + 128, rest:] = jnp.zeros((64, cut - rest), BF)
    last = w_ref[64:HD, :].astype(F32)
    low = last[:, 0:cut]
    high = jnp.concatenate([last[:, cut:], jnp.zeros((HD - 64, cut - rest), F32)], axis=1)
    out_ref[TOK + 128 : TOK + 160, :] = jnp.concatenate([low, low, high, high], axis=0).astype(BF)


def unpack_far_kernel(n_pack, in_ref, label_ref, out_ref):
    place_rows(n_pack, FAR, label_ref[...], in_ref, out_ref)


QT = 256
KT = 512
AROWS = 112
NEG = -3e38
LIMIT = pltpu.CompilerParams(vmem_limit_bytes=56 * 2**20)


def attend_kernel(
    steps, n_seq, order_ref, doc_ref, near_ref, mine_ref, pair_ref, w_ref, out_ref, q_s, k_s, v_s, o_s, bound_s
):
    step = pl.program_id(0)
    rows = pl.ds(pl.multiple_of(order_ref[step] * TOK, 64), TOK)
    far = jnp.where(step < steps // 2, mine_ref[0], pair_ref[0])
    x = jnp.concatenate([near_ref[0], far], axis=1)
    qkv = [
        lax.dot_general(x, w_ref[j], NT, preferred_element_type=F32).astype(BF) for j in range(3)
    ]
    q_s[rows, :] = qkv[0]
    k_s[rows, :] = qkv[1]
    v_s[rows, 0:HD] = qkv[2]
    v_s[rows, HD:LANES] = jnp.where(iota((TOK, LANES - HD), 1) == 0, 1.0, 0.0).astype(BF)

    @pl.when(step == steps - 1)
    def _():
        length = k_s.shape[0] - KT
        blocks = length // BLK
        scale = math.log2(math.e) / math.sqrt(HD)
        k_s[length:, :] = jnp.zeros((KT, HD), BF)
        v_s[length:, :] = jnp.zeros((KT, LANES), BF)
        first = jnp.int32(0)
        for b in range(blocks):
            if b:
                first = jnp.where(doc_ref[0, b * BLK] == doc_ref[0, (b - 1) * BLK], first, b)
            bound_s[0, b] = first
        last = jnp.int32(blocks)
        for b in reversed(range(blocks)):
            if b < blocks - 1:
                last = jnp.where(doc_ref[0, b * BLK] == doc_ref[0, (b + 1) * BLK], last, b + 1)
            bound_s[1, b] = last
        per = QT // BLK

        def one_tile(t, _):
            q = q_s[pl.ds(pl.multiple_of(t * QT, QT), QT), :]
            lo = bound_s[0, t * per]
            hi = bound_s[1, t * per + per - 1]
            chunks = (hi - lo + KT // BLK - 1) // (KT // BLK)

            def one_chunk(c, carry):
                high, total = carry
                begin = lo + c * (KT // BLK)
                keys = pl.ds(pl.multiple_of(begin * BLK, BLK), KT)
                scores = lax.dot_general(q, k_s[keys, :], NT, preferred_element_type=F32)
                block = begin + iota((1, KT), 1) // BLK
                halves = []
                for i in range(per):
                    keep = (block >= bound_s[0, t * per + i]) & (block < bound_s[1, t * per + i])
                    halves.append(
                        jnp.where(keep, scores[i * BLK : (i + 1) * BLK, :], -jnp.inf)
                    )
                scores = jnp.concatenate(halves, axis=0)
                newer = jnp.maximum(high, jnp.max(scores, axis=1, keepdims=True))
                expo = jnp.exp2((scores - newer) * scale).astype(BF)
                total = total * jnp.exp2((high - newer) * scale) + jnp.dot(
                    expo, v_s[keys, :], preferred_element_type=F32
                )
                return newer, total

            high = jnp.full((QT, 1), NEG, F32)
            total = jnp.zeros((QT, LANES), F32)
            _, total = lax.fori_loop(0, chunks, one_chunk, (high, total))
            done = total[:, 0:HD] / total[:, HD : HD + 1]
            o_s[pl.ds(pl.multiple_of(t * QT, QT), QT), 0:HD] = done
            return 0

        lax.fori_loop(0, length // QT, one_tile, 0)
        tok = length // n_seq
        for s in range(n_seq):
            turned = o_s[s * tok : (s + 1) * tok, :].T
            out_ref[s, 0:64, :] = turned[0:64, 0:LANES].astype(BF)
            out_ref[s, 64:96, :] = jnp.concatenate(
                [turned[0:32, LANES:tok], turned[32:64, LANES:tok]], axis=1
            ).astype(BF)
            out_ref[s, 96:112, :] = jnp.concatenate(
                [
                    turned[64:72, 0:LANES],
                    jnp.concatenate(
                        [turned[64:72, LANES:tok], jnp.zeros((8, 2 * LANES - tok), F32)], axis=1
                    ),
                ],
                axis=0,
            ).astype(BF)


def project_kernel(n_seq, in_ref, wa_ref, wb_ref, wc_ref, wd_ref, we_ref, out_ref):
    width = out_ref.shape[1]
    tok = out_ref.shape[0]
    rest = tok - LANES
    lo = in_ref[:, 0:32, :].reshape(n_seq * 32, LANES)
    hi = in_ref[:, 32:64, :].reshape(n_seq * 32, LANES)
    far = in_ref[:, 64:96, :].reshape(n_seq * 32, LANES)
    tail = in_ref[:, 96:112, :].reshape(n_seq * 16, LANES).astype(F32)
    upper = (iota(tail.shape, 0) & 15) < 8
    tail_near = jnp.where(upper, tail, 0.0).astype(BF)
    tail_far = jnp.where(upper, 0.0, tail).astype(BF)
    near = jnp.concatenate([lo, hi, tail_near], axis=0).T
    far_t = far.T
    distant = jnp.concatenate([far_t[0:rest], far_t[rest:LANES], tail_far.T[0:rest]], axis=1)
    left = jnp.concatenate([near, distant], axis=0)
    cut = NEAR * LANES
    for lo_ref, hi_ref, t, begin, end in (
        (wa_ref, wb_ref, 0, 0, cut),
        (wc_ref, wd_ref, 16, cut, width),
    ):
        weights = jnp.concatenate(
            [
                lo_ref[:, :, 0 : end - begin].reshape(n_seq * 32, end - begin),
                hi_ref[:, :, 0 : end - begin].reshape(n_seq * 32, end - begin),
                we_ref[:, t : t + 16, 0 : end - begin].reshape(n_seq * 16, end - begin),
            ],
            axis=0,
        )
        out_ref[:, begin:end] = jnp.dot(left, weights, preferred_element_type=F32).astype(BF)


def whole(*shape):
    return pl.BlockSpec(shape, lambda *_: (0,) * len(shape))


def attend_call(order, doc_ids, near, mine, pair, w_t):
    n_seq = near.shape[0]
    length = n_seq * TOK
    half = n_seq // 2
    far = (1, TOK, FAR * LANES)
    return pl.pallas_call(
        functools.partial(attend_kernel, n_seq, n_seq),
        grid_spec=pltpu.PrefetchScalarGridSpec(
            num_scalar_prefetch=1,
            grid=(n_seq,),
            in_specs=[
                pl.BlockSpec(memory_space=pltpu.SMEM),
                pl.BlockSpec((1, TOK, NEAR * LANES), lambda i, o: (o[i], 0, 0)),
                pl.BlockSpec(far, lambda i, o: (jnp.minimum(i, half - 1), 0, 0)),
                pl.BlockSpec(far, lambda i, o: (jnp.maximum(i - half, 0), 0, 0)),
                whole(*w_t.shape),
            ],
            out_specs=whole(n_seq, AROWS, LANES),
            scratch_shapes=[
                pltpu.VMEM((length, HD), BF),
                pltpu.VMEM((length + KT, HD), BF),
                pltpu.VMEM((length + KT, LANES), BF),
                pltpu.VMEM((length, LANES), F32),
                pltpu.SMEM((2, length // BLK), jnp.int32),
            ],
        ),
        out_shape=jax.ShapeDtypeStruct((n_seq, AROWS, LANES), BF),
        compiler_params=LIMIT,
        name="attend",
    )(order, doc_ids, near, mine, pair, w_t)


def ring_gather(block, n_seq):
    chips = n_seq // 2
    up = [(i, (i + 2) % n_seq) for i in range(n_seq)]
    down = [(i, (i - 2) % n_seq) for i in range(n_seq)]
    right = left = block
    held = [block]
    for _ in range((chips - 1) // 2):
        right = lax.ppermute(right, "seq", up)
        left = lax.ppermute(left, "seq", down)
        held += [right, left]
    middle = block.shape[0] // 2
    held += [
        lax.ppermute(right[:middle], "seq", up),
        lax.ppermute(left[middle:], "seq", down),
    ]
    return jnp.concatenate(held, axis=0).reshape(chips, *block.shape)


def local_call(kernel, out_shape, *operands, name):
    return pl.pallas_call(kernel, out_shape=out_shape, compiler_params=LIMIT, name=name)(*operands)


def body(source, destination, doc_ids, w_qkv, w_out):
    n_pack = lax.axis_size("pack")
    n_seq = lax.axis_size("seq")
    width = source.shape[2]
    shape = jax.ShapeDtypeStruct
    near_rows = NEAR * CAP // 16 * 16 + 16
    far_rows = FAR * CAP

    def exchange(outbox):
        return lax.all_to_all(outbox, "pack", split_axis=0, concat_axis=0, tiled=True)

    def packed_rows(chunks, first, labelled, rows, name):
        return local_call(
            functools.partial(pack_kernel, n_pack, chunks, first, labelled),
            shape((n_pack, rows, LANES), BF),
            destination,
            source[0],
            name=name,
        )

    near_box = exchange(packed_rows(NEAR, 0, True, near_rows, "pack_near"))
    far_out = packed_rows(FAR, NEAR, False, far_rows, "pack_far")
    near_box, far_out = lax.optimization_barrier((near_box, far_out))
    far_box = exchange(far_out)
    near, labels = local_call(
        functools.partial(unpack_near_kernel, n_pack),
        (shape((TOK + 160, NEAR * LANES), BF), shape((n_pack, LANES), BF)),
        near_box,
        w_out,
        name="unpack_near",
    )
    near_all = lax.all_gather(near, "seq", axis=0, tiled=False)
    far = local_call(
        functools.partial(unpack_far_kernel, n_pack),
        shape((TOK, FAR * LANES), BF),
        far_box,
        labels,
        name="unpack_far",
    )
    mine = ring_gather(far, n_seq)
    pair = lax.ppermute(mine, "seq", [(i, i ^ 1) for i in range(n_seq)])

    me = lax.axis_index("seq").astype(jnp.int32)
    back = jnp.array([0, 1, -1, 2, -2, 3, -3, 4], jnp.int32)
    chip = lax.rem(me // 2 - back + n_seq // 2, n_seq // 2)
    core = me % 2
    order = jnp.concatenate([2 * chip + core, 2 * chip + 1 - core])
    attended = attend_call(
        order, doc_ids, near_all, mine, pair, jnp.transpose(w_qkv, (0, 2, 1))
    )
    blocks = lax.all_to_all(attended, "seq", split_axis=0, concat_axis=0, tiled=True)

    def w_spec(n):
        return pl.BlockSpec((n_seq, 32, NEAR * LANES), lambda i: (0, TOK // 32 + n, 0))

    out = pl.pallas_call(
        functools.partial(project_kernel, n_seq),
        grid=(1,),
        out_shape=shape((TOK, width), BF),
        in_specs=[whole(*blocks.shape)] + [w_spec(n) for n in range(5)],
        out_specs=whole(TOK, width),
        compiler_params=LIMIT,
        name="project",
    )(blocks, near_all, near_all, near_all, near_all, near_all)
    return out[None]


def solution(mesh):
    placed = (
        P("seq", "pack", None),
        P("seq", "pack"),
        P("pack", None),
        P(None, None, "seq"),
        P("seq", None),
    )
    return jax.shard_map(
        body, mesh=mesh, in_specs=placed, out_specs=P("pack", "seq", None), check_vma=False
    )
```

time: 165 us -> 189 us (1.15)
  the two profiles are of different devices: /device:TPU:7 before, /device:TPU:3 now
where the time goes in v2:
time: 189 us; the launch traced here: 188 us
  Pallas kernels  50 us (26%)
  starting transfers between devices  48.7 us (26%)
  blocking collectives  40.6 us (21%)
  waiting for transfers between devices  31.2 us (17%)
  between operations  13.6 us (7%)
  local copies, waits for them, and re-layouts  3.03 us (2%)
    pallas_call x1, Pallas kernels, attend_call(): pl.pallas_call(functools.partial(attend_kernel, n_seq, n_seq), grid_spec=...  35.6 us
    all_to_all x1, blocking collectives, body(): lax.all_to_all(attended, 'seq', split_axis=0, concat_axis=0, tiled=True)  21.8 us
    all_to_all x1, blocking collectives, exchange(): lax.all_to_all(outbox, 'pack', split_axis=0, concat_axis=0, tiled=True)  18.8 us
    ppermute x3, waiting for transfers between devices, ring_gather(): right = lax.ppermute(right, 'seq', up)  16.9 us
    ppermute x3, starting transfers between devices, ring_gather(): left = lax.ppermute(left, 'seq', down)  12.9 us
    all_to_all x1, starting transfers between devices, exchange(): lax.all_to_all(outbox, 'pack', split_axis=0, concat_axis=0, tiled=True)  12.9 us
    pallas_call x4, Pallas kernels, local_call(): pl.pallas_call(kernel, out_shape=out_shape, compiler_params=LIMIT, name=n...  10.8 us
    all_to_all x1, waiting for transfers between devices, exchange(): lax.all_to_all(outbox, 'pack', split_axis=0, concat_axis=0, tiled=True)  10.4 us
  transfers between devices with their start and end apart: 11, of which 7 were waited for; matrix products, arithmetic and copies ran while one was open for 1% of the time, Pallas kernels for 3%

profile of v2, /device:TPU:3, one launch (start us, length us, event | category | flops | bytes accessed | tf_op | source)
XLA Modules:
  0.0 187.8 jit_solution(10640021091853083661)
XLA Ops:
  6.5 2.6 %pack_near.1 = bf16[32,64,128]{2,1,0:T(8,128)(2,1)} custom-call(s32[1,192]{1,0:T(1,128)} %dest_ref.3, bf16[192,1152]{1,0:T(8,128)(2,1)} %bitcast.13), custom_call_target="tpu_custom_call" | custom-call | tf_op jit(solution)/shard_map/pack_near/pallas_call | solution.py:303
  9.2 12.9 %all-to-all-start = ((bf16[32,64,128]{2,1,0:T(8,128)(2,1)}), bf16[32,64,128]{2,1,0:T(8,128)(2,1)S(1)}, u32[]{:S(2)}, u32[]{:S(2)}) async-start(bf16[32,64,128]{2,1,0:T(8,128)(2,1)} %pack_near.1), calls=%async_computation | async-start | bytes 1048576 | tf_op jit(solution)/shard_map/all_to_all | solution.py:315
  22.1 0.0 all-gather.3.cloned.1.call-start
  22.1 2.5 %pack_far.1 = bf16[32,48,128]{2,1,0:T(8,128)(2,1)} custom-call(s32[1,192]{1,0:T(1,128)} %dest_ref.3, bf16[192,1152]{1,0:T(8,128)(2,1)} %bitcast.14), custom_call_target="tpu_custom_call" | custom-call | tf_op jit(solution)/shard_map/pack_far/pallas_call | solution.py:303
  24.6 10.4 %all-to-all-done.in_ref = bf16[32,64,128]{2,1,0:T(8,128)(2,1)S(1)} async-done(((bf16[32,64,128]{2,1,0:T(8,128)(2,1)}), bf16[32,64,128]{2,1,0:T(8,128)(2,1)S(1)}, u32[]{:S(2)}, u32[]{:S(2)}) %all-to-all-start) | async-done | bytes 524320 | tf_op jit(solution)/shard_map/all_to_all | solution.py:315
  35.0 0.0 copy-start
  35.0 0.8 copy-done
  35.8 2.9 %unpack_near.1 = (bf16[352,640]{1,0:T(8,128)(2,1)}, bf16[32,128]{1,0:T(8,128)(2,1)}) custom-call(bf16[32,64,128]{2,1,0:T(8,128)(2,1)} %copy-done, bf16[72,1152]{1,0:T(8,128)(2,1)} %w_ref.1), custom_call_target="tpu_custom_call" | custom-call | tf_op jit(solution)/shard_map/unpack_near/pallas_call | solution.py:303
  38.7 0.0 all-gather.3.cloned.1.call-update
  38.7 18.8 %all_to_all.15.in_ref = bf16[32,48,128]{2,1,0:T(8,128)(2,1)} all-to-all(bf16[32,48,128]{2,1,0:T(8,128)(2,1)} %pack_far.1), channel_id=1, replica_groups=mesh['pack'=32,'seq'=16] {'pack'}, dimensions={0} | all-to-all | bytes 786432 | tf_op jit(solution)/shard_map/all_to_all | solution.py:315
  57.5 2.7 %unpack_far.1 = bf16[192,512]{1,0:T(8,128)(2,1)} custom-call(bf16[32,48,128]{2,1,0:T(8,128)(2,1)} %all_to_all.15.in_ref, bf16[32,128]{1,0:T(8,128)(2,1)} %get-tuple-element.12.label_ref), custom_call_target="tpu_custom_call" | custom-call | tf_op jit(solution)/shard_map/unpack_far/pallas_call | solution.py:303
  60.2 3.2 %collective-permute-start = (bf16[192,512]{1,0:T(8,128)(2,1)}, bf16[192,512]{1,0:T(8,128)(2,1)S(1)}, u32[]{:S(2)}, u32[]{:S(2)}) collective-permute-start(bf16[192,512]{1,0:T(8,128)(2,1)} %unpack_far.1), channel_id=1, source_target_pairs={{0,2},{1,3},{2,4},{3,5},{4,6},{5,7},{6,8},{7,9},{8,10},{9,11},{10,... | collective-permute-start | bytes 589832 | tf_op jit(solution)/shard_map/ppermute | solution.py:291
  63.5 3.8 %collective-permute-start.1 = (bf16[192,512]{1,0:T(8,128)(2,1)}, bf16[192,512]{1,0:T(8,128)(2,1)S(1)}, u32[]{:S(2)}, u32[]{:S(2)}) collective-permute-start(bf16[192,512]{1,0:T(8,128)(2,1)} %unpack_far.1), channel_id=1, source_target_pairs={{0,14},{1,15},{2,0},{3,1},{4,2},{5,3},{6,4},{7,5},{8,6},{9,7},{10,... | collective-permute-start | bytes 589832 | tf_op jit(solution)/shard_map/ppermute | solution.py:292
  67.2 1.0 constant_dynamic-update-slice_fusion.8
  68.2 0.0 copy-start.3
  68.2 5.4 %collective-permute-done = bf16[192,512]{1,0:T(8,128)(2,1)S(1)} collective-permute-done((bf16[192,512]{1,0:T(8,128)(2,1)}, bf16[192,512]{1,0:T(8,128)(2,1)S(1)}, u32[]{:S(2)}, u32[]{:S(2)}) %collective-permute-start) | collective-permute-done | bytes 196640 | tf_op jit(solution)/shard_map/ppermute | solution.py:291
  73.6 1.9 %collective-permute-start.2 = (bf16[192,512]{1,0:T(8,128)(2,1)S(1)}, bf16[192,512]{1,0:T(8,128)(2,1)S(1)}, u32[]{:S(2)}, u32[]{:S(2)}) collective-permute-start(bf16[192,512]{1,0:T(8,128)(2,1)S(1)} %collective-permute-done), channel_id=1, source_target_pairs={{0,2},{1,3},{2,4},{3,5},{4,6},{5,7},{6,8},{7,9},{8,10},{9,11},{10,... | collective-permute-start | bytes 589832 | tf_op jit(solution)/shard_map/ppermute | solution.py:291
  75.5 0.0 collective-permute-done.1
  75.5 4.6 %collective-permute-start.3 = (bf16[192,512]{1,0:T(8,128)(2,1)S(1)}, bf16[192,512]{1,0:T(8,128)(2,1)S(1)}, u32[]{:S(2)}, u32[]{:S(2)}) collective-permute-start(bf16[192,512]{1,0:T(8,128)(2,1)S(1)} %collective-permute-done.1), channel_id=1, source_target_pairs={{0,14},{1,15},{2,0},{3,1},{4,2},{5,3},{6,4},{7,5},{8,6},{9,7},{10,... | collective-permute-start | bytes 589832 | tf_op jit(solution)/shard_map/ppermute | solution.py:292
  80.2 5.8 %collective-permute-done.2 = bf16[192,512]{1,0:T(8,128)(2,1)S(1)} collective-permute-done((bf16[192,512]{1,0:T(8,128)(2,1)S(1)}, bf16[192,512]{1,0:T(8,128)(2,1)S(1)}, u32[]{:S(2)}, u32[]{:S(2)}) %collective-permute-start.2) | collective-permute-done | bytes 196640 | tf_op jit(solution)/shard_map/ppermute | solution.py:291
  86.0 1.9 %collective-permute-start.4 = (bf16[192,512]{1,0:T(8,128)(2,1)S(1)}, bf16[192,512]{1,0:T(8,128)(2,1)S(1)}, u32[]{:S(2)}, u32[]{:S(2)}) collective-permute-start(bf16[192,512]{1,0:T(8,128)(2,1)S(1)} %collective-permute-done.2), channel_id=1, source_target_pairs={{0,2},{1,3},{2,4},{3,5},{4,6},{5,7},{6,8},{7,9},{8,10},{9,11},{10,... | collective-permute-start | bytes 589832 | tf_op jit(solution)/shard_map/ppermute | solution.py:291
  87.9 0.0 collective-permute-done.3
  87.9 4.6 %collective-permute-start.5 = (bf16[192,512]{1,0:T(8,128)(2,1)S(1)}, bf16[192,512]{1,0:T(8,128)(2,1)S(1)}, u32[]{:S(2)}, u32[]{:S(2)}) collective-permute-start(bf16[192,512]{1,0:T(8,128)(2,1)S(1)} %collective-permute-done.3), channel_id=1, source_target_pairs={{0,14},{1,15},{2,0},{3,1},{4,2},{5,3},{6,4},{7,5},{8,6},{9,7},{10,... | collective-permute-start | bytes 589832 | tf_op jit(solution)/shard_map/ppermute | solution.py:292
  92.5 5.6 %collective-permute-done.4 = bf16[192,512]{1,0:T(8,128)(2,1)S(1)} collective-permute-done((bf16[192,512]{1,0:T(8,128)(2,1)S(1)}, bf16[192,512]{1,0:T(8,128)(2,1)S(1)}, u32[]{:S(2)}, u32[]{:S(2)}) %collective-permute-start.4) | collective-permute-done | bytes 196640 | tf_op jit(solution)/shard_map/ppermute | solution.py:291
  98.2 1.9 %collective-permute-start.6 = (bf16[96,512]{1,0:T(8,128)(2,1)S(1)}, bf16[96,512]{1,0:T(8,128)(2,1)S(1)}, u32[]{:S(2)}, u32[]{:S(2)}) collective-permute-start(bf16[96,512]{1,0:T(8,128)(2,1)S(1)} %slice.8), channel_id=1, source_target_pairs={{0,2},{1,3},{2,4},{3,5},{4,6},{5,7},{6,8},{7,9},{8,10},{9,11},{10,... | collective-permute-start | bytes 294920 | tf_op jit(solution)/shard_map/ppermute | solution.py:296
  100.1 0.0 collective-permute-done.5
  100.2 4.6 %collective-permute-start.7 = (bf16[96,512]{1,0:T(8,128)(2,1)S(1)}, bf16[96,512]{1,0:T(8,128)(2,1)S(1)}, u32[]{:S(2)}, u32[]{:S(2)}) collective-permute-start(bf16[96,512]{1,0:T(8,128)(2,1)S(1)} %slice.9), channel_id=1, source_target_pairs={{0,14},{1,15},{2,0},{3,1},{4,2},{5,3},{6,4},{7,5},{8,6},{9,7},{10,... | collective-permute-start | bytes 294920 | tf_op jit(solution)/shard_map/ppermute | solution.py:297
  104.8 0.1 collective-permute-done.6
  104.9 1.5 collective-permute-done.7
  106.4 0.0 copy-start.1
  106.4 9.3 %collective-permute-start.8 = (bf16[8,192,512]{2,1,0:T(8,128)(2,1)S(1)}, bf16[8,192,512]{2,1,0:T(8,128)(2,1)S(1)}, u32[]{:S(2)}, u32[]{:S(2)}) collective-permute-start(bf16[8,192,512]{2,1,0:T(8,128)(2,1)S(1)} %bitcast.11), channel_id=1, source_target_pairs={{0,1},{1,0},{2,3},{3,2},{4,5},{5,4},{6,7},{7,6},{8,9},{9,8},{10,11... | collective-permute-start | bytes 4718600 | tf_op jit(solution)/shard_map/ppermute | solution.py:346
  115.7 0.0 copy-done.3
  115.8 0.6 pad_add_fusion.order_ref
  116.3 2.4 %collective-permute-done.8.pair_ref = bf16[8,192,512]{2,1,0:T(8,128)(2,1)S(1)} collective-permute-done((bf16[8,192,512]{2,1,0:T(8,128)(2,1)S(1)}, bf16[8,192,512]{2,1,0:T(8,128)(2,1)S(1)}, u32[]{:S(2)}, u32[]{:S(2)}) %collective-permute-start.8) | collective-permute-done | bytes 1572896 | tf_op jit(solution)/shard_map/ppermute | solution.py:346
  118.7 0.0 copy-start.2
  118.7 0.0 all-gather.3.cloned.1.call-done
  118.7 0.0 copy-done.1
  118.7 1.1 copy-done.2
  119.9 35.6 %attend.1 = bf16[16,112,128]{2,1,0:T(8,128)(2,1)} custom-call(s32[16]{0:T(128)} %pad_add_fusion.order_ref, s32[1,3072]{1,0:T(1,128)} %doc_ref.1, bf16[16,352,640]{2,1,0:T(8,128)(2,1)} %bitcast.5, bf16[8,192,512]{2,1,0:T(8,128)(2,1)} %bitcast.12, bf16[8,192,512]{2,1,0:T(8,128)(2,1)} %copy-done.2, bf16[3,72,1152]{2,1,0:T(8,128)(2,1)} %bitcast.15), custom_call_target="tpu_custom_call" | custom-call | tf_op jit(solution)/shard_map/attend/pallas_call | solution.py:257
  155.5 21.8 %all_to_all.16.in_ref = bf16[16,112,128]{2,1,0:T(8,128)(2,1)} all-to-all(bf16[16,112,128]{2,1,0:T(8,128)(2,1)} %attend.1), channel_id=1, replica_groups=mesh['pack'=32,'seq'=16] {'seq'}, dimensions={0} | all-to-all | bytes 917504 | tf_op jit(solution)/shard_map/all_to_all | solution.py:356
  177.3 3.6 %project.1 = bf16[192,1152]{1,0:T(8,128)(2,1)} custom-call(bf16[16,112,128]{2,1,0:T(8,128)(2,1)} %all_to_all.16.in_ref, bf16[16,352,640]{2,1,0:T(8,128)(2,1)} %bitcast.6, bf16[16,352,640]{2,1,0:T(8,128)(2,1)} %bitcast.7, bf16[16,352,640]{2,1,0:T(8,128)(2,1)} %bitcast.8, bf16[16,352,640]{2,1,0:T(8,128)(2,1)} %bitcast.9, bf16[16,352,640]{2,1,0:T(8,128)(2,1)} %bitcast.10), custom_call_target="tpu_custom_call" | custom-call | tf_op jit(solution)/shard_map/project/pallas_call | solution.py:361
  (12 shorter events, 0.1 us)
Async XLA Ops:
  9.2 25.8 %all-to-all-start = ((bf16[32,64,128]{2,1,0:T(8,128)(2,1)}), bf16[32,64,128]{2,1,0:T(8,128)(2,1)S(1)}, u32[]{:S(2)}, u32[]{:S(2)}) async-start(bf16[32,64,128]{2,1,0:T(8,128)(2,1)} %pack_near.1), calls=%async_computation | async-start | bytes 1048576 | tf_op jit(solution)/shard_map/all_to_all | solution.py:315
  22.1 96.6 %all-gather.3.cloned.1.call-start = ((), (), s32[]{:S(2)}) async-start(), calls=%async_computation.3 | async-start | bytes 7659520 | tf_op jit(solution)/shard_map/all_gather | solution.py:337
  35.0 0.8 copy-start
  60.2 13.4 %collective-permute-start = (bf16[192,512]{1,0:T(8,128)(2,1)}, bf16[192,512]{1,0:T(8,128)(2,1)S(1)}, u32[]{:S(2)}, u32[]{:S(2)}) collective-permute-start(bf16[192,512]{1,0:T(8,128)(2,1)} %unpack_far.1), channel_id=1, source_target_pairs={{0,2},{1,3},{2,4},{3,5},{4,6},{5,7},{6,8},{7,9},{8,10},{9,11},{10,... | collective-permute-start | bytes 589832 | tf_op jit(solution)/shard_map/ppermute | solution.py:291
  63.5 12.1 %collective-permute-start.1 = (bf16[192,512]{1,0:T(8,128)(2,1)}, bf16[192,512]{1,0:T(8,128)(2,1)S(1)}, u32[]{:S(2)}, u32[]{:S(2)}) collective-permute-start(bf16[192,512]{1,0:T(8,128)(2,1)} %unpack_far.1), channel_id=1, source_target_pairs={{0,14},{1,15},{2,0},{3,1},{4,2},{5,3},{6,4},{7,5},{8,6},{9,7},{10,... | collective-permute-start | bytes 589832 | tf_op jit(solution)/shard_map/ppermute | solution.py:292
  68.2 47.5 %copy-start.3 = (s32[8]{0:T(128)S(1)}, s32[8]{0:T(128)}, u32[]{:S(2)}) copy-start(s32[8]{0:T(128)} %constant.43) | copy-start | bytes 100
  73.6 12.4 %collective-permute-start.2 = (bf16[192,512]{1,0:T(8,128)(2,1)S(1)}, bf16[192,512]{1,0:T(8,128)(2,1)S(1)}, u32[]{:S(2)}, u32[]{:S(2)}) collective-permute-start(bf16[192,512]{1,0:T(8,128)(2,1)S(1)} %collective-permute-done), channel_id=1, source_target_pairs={{0,2},{1,3},{2,4},{3,5},{4,6},{5,7},{6,8},{7,9},{8,10},{9,11},{10,... | collective-permute-start | bytes 589832 | tf_op jit(solution)/shard_map/ppermute | solution.py:291
  75.5 12.4 %collective-permute-start.3 = (bf16[192,512]{1,0:T(8,128)(2,1)S(1)}, bf16[192,512]{1,0:T(8,128)(2,1)S(1)}, u32[]{:S(2)}, u32[]{:S(2)}) collective-permute-start(bf16[192,512]{1,0:T(8,128)(2,1)S(1)} %collective-permute-done.1), channel_id=1, source_target_pairs={{0,14},{1,15},{2,0},{3,1},{4,2},{5,3},{6,4},{7,5},{8,6},{9,7},{10,... | collective-permute-start | bytes 589832 | tf_op jit(solution)/shard_map/ppermute | solution.py:292
  86.0 12.2 %collective-permute-start.4 = (bf16[192,512]{1,0:T(8,128)(2,1)S(1)}, bf16[192,512]{1,0:T(8,128)(2,1)S(1)}, u32[]{:S(2)}, u32[]{:S(2)}) collective-permute-start(bf16[192,512]{1,0:T(8,128)(2,1)S(1)} %collective-permute-done.2), channel_id=1, source_target_pairs={{0,2},{1,3},{2,4},{3,5},{4,6},{5,7},{6,8},{7,9},{8,10},{9,11},{10,... | collective-permute-start | bytes 589832 | tf_op jit(solution)/shard_map/ppermute | solution.py:291
  87.9 12.2 %collective-permute-start.5 = (bf16[192,512]{1,0:T(8,128)(2,1)S(1)}, bf16[192,512]{1,0:T(8,128)(2,1)S(1)}, u32[]{:S(2)}, u32[]{:S(2)}) collective-permute-start(bf16[192,512]{1,0:T(8,128)(2,1)S(1)} %collective-permute-done.3), channel_id=1, source_target_pairs={{0,14},{1,15},{2,0},{3,1},{4,2},{5,3},{6,4},{7,5},{8,6},{9,7},{10,... | collective-permute-start | bytes 589832 | tf_op jit(solution)/shard_map/ppermute | solution.py:292
  98.2 6.6 %collective-permute-start.6 = (bf16[96,512]{1,0:T(8,128)(2,1)S(1)}, bf16[96,512]{1,0:T(8,128)(2,1)S(1)}, u32[]{:S(2)}, u32[]{:S(2)}) collective-permute-start(bf16[96,512]{1,0:T(8,128)(2,1)S(1)} %slice.8), channel_id=1, source_target_pairs={{0,2},{1,3},{2,4},{3,5},{4,6},{5,7},{6,8},{7,9},{8,10},{9,11},{10,... | collective-permute-start | bytes 294920 | tf_op jit(solution)/shard_map/ppermute | solution.py:296
  100.2 6.2 %collective-permute-start.7 = (bf16[96,512]{1,0:T(8,128)(2,1)S(1)}, bf16[96,512]{1,0:T(8,128)(2,1)S(1)}, u32[]{:S(2)}, u32[]{:S(2)}) collective-permute-start(bf16[96,512]{1,0:T(8,128)(2,1)S(1)} %slice.9), channel_id=1, source_target_pairs={{0,14},{1,15},{2,0},{3,1},{4,2},{5,3},{6,4},{7,5},{8,6},{9,7},{10,... | collective-permute-start | bytes 294920 | tf_op jit(solution)/shard_map/ppermute | solution.py:297
  106.4 12.4 %copy-start.1 = (bf16[1536,512]{1,0:T(8,128)(2,1)}, bf16[1536,512]{1,0:T(8,128)(2,1)S(1)}, u32[]{:S(2)}) copy-start(bf16[1536,512]{1,0:T(8,128)(2,1)S(1)} %constant_dynamic-update-slice_fusion) | copy-start | bytes 4718596
  106.4 12.4 %collective-permute-start.8 = (bf16[8,192,512]{2,1,0:T(8,128)(2,1)S(1)}, bf16[8,192,512]{2,1,0:T(8,128)(2,1)S(1)}, u32[]{:S(2)}, u32[]{:S(2)}) collective-permute-start(bf16[8,192,512]{2,1,0:T(8,128)(2,1)S(1)} %bitcast.11), channel_id=1, source_target_pairs={{0,1},{1,0},{2,3},{3,2},{4,5},{5,4},{6,7},{7,6},{8,9},{9,8},{10,11... | collective-permute-start | bytes 4718600 | tf_op jit(solution)/shard_map/ppermute | solution.py:346
  118.7 1.2 copy-start.2
Sparse Core Ops, SparseCore 0:
  38.9 66.8 all-gather.2

commit v3 on v1

--- a/solution.py
+++ b/solution.py
@@ -87,9 +87,11 @@
         out_ref[:, f * LANES : (f + 1) * LANES] = whole.astype(BF)
 
 
-TOKT = 256
+TOKT = 1024
 QT = 256
-KT = 512
+KT = 1024
+SIDE = 1
+VROWS = 80
 AROWS = 112
 NEG = -3e38
 LIMIT = pltpu.CompilerParams(vmem_limit_bytes=56 * 2**20)
@@ -97,23 +99,22 @@
 
 def attend_kernel(steps, n_seq, doc_ref, x_ref, w_ref, out_ref, q_s, k_s, v_s, o_s, bound_s):
     step = pl.program_id(0)
-    rows = pl.ds(pl.multiple_of(step * TOKT, TOKT), TOKT)
-    x = x_ref[...]
-    qkv = [
-        lax.dot_general(x, w_ref[j], NT, preferred_element_type=F32).astype(BF) for j in range(3)
-    ]
-    q_s[rows, :] = qkv[0]
-    k_s[rows, :] = qkv[1]
-    v_s[rows, 0:HD] = qkv[2]
-    v_s[rows, HD:LANES] = jnp.where(iota((TOKT, LANES - HD), 1) == 0, 1.0, 0.0).astype(BF)
+    start = pl.multiple_of(step * TOKT, TOKT)
+    qkv = lax.dot_general(x_ref[...], w_ref[...], NT, preferred_element_type=F32)
+    q_s[pl.ds(start, TOKT), :] = (qkv[:, 0:HD] * (1.0 / math.sqrt(HD))).astype(BF)
+    k_s[pl.ds(start, TOKT), :] = qkv[:, HD : 2 * HD].astype(BF)
+    turned = qkv[:, LANES : 3 * HD].T[2 * HD - LANES :, :]
+    ones = jnp.ones((VROWS - HD, TOKT), F32)
+    v_s[:, pl.ds(start, TOKT)] = jnp.concatenate([turned, ones], axis=0).astype(BF)
 
     @pl.when(step == steps - 1)
     def _():
-        length = k_s.shape[0] - KT
+        length = q_s.shape[0]
         blocks = length // BLK
-        scale = math.log2(math.e) / math.sqrt(HD)
+        per_q = QT // BLK
+        per_k = KT // BLK
         k_s[length:, :] = jnp.zeros((KT, HD), BF)
-        v_s[length:, :] = jnp.zeros((KT, LANES), BF)
+        v_s[:, length:] = jnp.zeros((VROWS, KT), BF)
         first = jnp.int32(0)
         for b in range(blocks):
             if b:
@@ -124,57 +125,64 @@
             if b < blocks - 1:
                 last = jnp.where(doc_ref[0, b * BLK] == doc_ref[0, (b + 1) * BLK], last, b + 1)
             bound_s[1, b] = last
-        per = QT // BLK
-
-        def one_tile(t, _):
-            q = q_s[pl.ds(pl.multiple_of(t * QT, QT), QT), :]
-            lo = bound_s[0, t * per]
-            hi = bound_s[1, t * per + per - 1]
-            chunks = (hi - lo + KT // BLK - 1) // (KT // BLK)
+
+        def some_tiles(group, _):
+            tiles = []
+            for u in range(SIDE):
+                t = group * SIDE + u
+                bounds = [
+                    (bound_s[0, t * per_q + i], bound_s[1, t * per_q + i]) for i in range(per_q)
+                ]
+                q = q_s[pl.ds(pl.multiple_of(t * QT, QT), QT), :]
+                tiles.append((t, q, bounds))
+            chunks = functools.reduce(
+                jnp.maximum, [b[-1][1] - b[0][0] for _, _, b in tiles]
+            )
+            chunks = (chunks + per_k - 1) // per_k
 
             def one_chunk(c, carry):
-                high, total = carry
-                begin = lo + c * (KT // BLK)
-                keys = pl.ds(pl.multiple_of(begin * BLK, BLK), KT)
-                scores = lax.dot_general(q, k_s[keys, :], NT, preferred_element_type=F32)
-                block = begin + iota((1, KT), 1) // BLK
-                halves = []
-                for i in range(per):
-                    keep = (block >= bound_s[0, t * per + i]) & (block < bound_s[1, t * per + i])
-                    halves.append(
-                        jnp.where(keep, scores[i * BLK : (i + 1) * BLK, :], -jnp.inf)
+                result = []
+                for (_, q, bounds), (high, total) in zip(tiles, carry):
+                    begin = bounds[0][0] + c * per_k
+                    keys = pl.ds(pl.multiple_of(jnp.minimum(begin, blocks) * BLK, BLK), KT)
+                    scores = lax.dot_general(k_s[keys, :], q, NT, preferred_element_type=F32)
+                    columns = []
+                    for i, (lo, hi) in enumerate(bounds):
+                        kept = [
+                            jnp.where(
+                                (begin + j >= lo) & (begin + j < hi),
+                                scores[j * BLK : (j + 1) * BLK, i * BLK : (i + 1) * BLK],
+                                -jnp.inf,
+                            )
+                            for j in range(per_k)
+                        ]
+                        columns.append(jnp.concatenate(kept, axis=0))
+                    scores = jnp.concatenate(columns, axis=1)
+                    newer = jnp.maximum(high, jnp.max(scores, axis=0, keepdims=True))
+                    expo = jnp.exp(scores - newer).astype(BF)
+                    total = total * jnp.exp(high - newer) + jnp.dot(
+                        v_s[:, keys], expo, preferred_element_type=F32
                     )
-                scores = jnp.concatenate(halves, axis=0)
-                newer = jnp.maximum(high, jnp.max(scores, axis=1, keepdims=True))
-                expo = jnp.exp2((scores - newer) * scale).astype(BF)
-                total = total * jnp.exp2((high - newer) * scale) + jnp.dot(
-                    expo, v_s[keys, :], preferred_element_type=F32
-                )
-                return newer, total
-
-            high = jnp.full((QT, 1), NEG, F32)
-            total = jnp.zeros((QT, LANES), F32)
-            _, total = lax.fori_loop(0, chunks, one_chunk, (high, total))
-            done = total[:, 0:HD] / total[:, HD : HD + 1]
-            o_s[pl.ds(pl.multiple_of(t * QT, QT), QT), 0:HD] = done
+                    result.append((newer, total))
+                return tuple(result)
+
+            carry = tuple(
+                (jnp.full((1, QT), NEG, F32), jnp.zeros((VROWS, QT), F32)) for _ in range(SIDE)
+            )
+            for (t, _, _), (_, total) in zip(tiles, lax.fori_loop(0, chunks, one_chunk, carry)):
+                o_s[:, pl.ds(pl.multiple_of(t * QT, QT), QT)] = total / total[HD : HD + 1, :]
             return 0
 
-        lax.fori_loop(0, length // QT, one_tile, 0)
+        lax.fori_loop(0, length // (QT * SIDE), some_tiles, 0)
         tok = length // n_seq
         for s in range(n_seq):
-            turned = o_s[s * tok : (s + 1) * tok, :].T
-            out_ref[s, 0:64, :] = turned[0:64, 0:LANES].astype(BF)
-            out_ref[s, 64:96, :] = jnp.concatenate(
-                [turned[0:32, LANES:tok], turned[32:64, LANES:tok]], axis=1
-            ).astype(BF)
+            mine = o_s[0:HD, s * tok : (s + 1) * tok]
+            rest = mine[:, LANES:tok]
+            out_ref[s, 0:64, :] = mine[0:64, 0:LANES].astype(BF)
+            out_ref[s, 64:96, :] = jnp.concatenate([rest[0:32], rest[32:64]], axis=1).astype(BF)
+            empty = jnp.zeros((HD - 64, 2 * LANES - tok), F32)
             out_ref[s, 96:112, :] = jnp.concatenate(
-                [
-                    turned[64:72, 0:LANES],
-                    jnp.concatenate(
-                        [turned[64:72, LANES:tok], jnp.zeros((8, 2 * LANES - tok), F32)], axis=1
-                    ),
-                ],
-                axis=0,
+                [mine[64:HD, 0:LANES], jnp.concatenate([rest[64:HD], empty], axis=1)], axis=0
             ).astype(BF)
 
 
@@ -193,11 +201,12 @@
     far_t = far.T
     distant = jnp.concatenate([far_t[0:rest], far_t[rest:LANES], tail_far.T[0:rest]], axis=1)
     left = jnp.concatenate([near, distant], axis=0)
+    last = w_ref[:, 64:HD, :].astype(F32)
     weights = jnp.concatenate(
         [
             w_ref[:, 0:32, :].reshape(n_seq * 32, width),
             w_ref[:, 32:64, :].reshape(n_seq * 32, width),
-            w_ref[:, 64:80, :].reshape(n_seq * 16, width),
+            jnp.concatenate([last, last], axis=1).reshape(n_seq * 16, width).astype(BF),
         ],
         axis=0,
     )
@@ -218,14 +227,14 @@
         in_specs=[
             pl.BlockSpec(memory_space=pltpu.SMEM),
             pl.BlockSpec((TOKT, width), lambda i: (i, 0)),
-            whole(3, HD, width),
+            whole(*w_t.shape),
         ],
         out_specs=whole(n_seq, AROWS, LANES),
         scratch_shapes=[
             pltpu.VMEM((length, HD), BF),
             pltpu.VMEM((length + KT, HD), BF),
-            pltpu.VMEM((length + KT, LANES), BF),
-            pltpu.VMEM((length, LANES), F32),
+            pltpu.VMEM((VROWS, length + KT), BF),
+            pltpu.VMEM((VROWS, length), F32),
             pltpu.SMEM((2, length // BLK), jnp.int32),
         ],
         compiler_params=LIMIT,
@@ -237,8 +246,7 @@
     n_pack = lax.axis_size("pack")
     n_seq = lax.axis_size("seq")
     tok, width = source.shape[1:]
-    spare = jnp.concatenate([w_out, w_out[64:HD]], axis=0)
-    w_all = lax.all_gather(spare, "seq", axis=0, tiled=False)
+    w_all = lax.all_gather(w_out, "seq", axis=0, tiled=False)
 
     outbox = pl.pallas_call(
         functools.partial(pack_kernel, n_pack),
@@ -253,9 +261,12 @@
         compiler_params=LIMIT,
         name="unpack_rows",
     )(inbox)
+    packed, w_all = lax.optimization_barrier((packed, w_all))
     tokens = lax.all_gather(packed, "seq", axis=0, tiled=True)
 
-    attended = attend_call(doc_ids, tokens, jnp.transpose(w_qkv, (0, 2, 1)), n_seq)
+    attended = attend_call(
+        doc_ids, tokens, jnp.transpose(w_qkv, (0, 2, 1)).reshape(3 * HD, width), n_seq
+    )
     blocks = lax.all_to_all(attended, "seq", split_axis=0, concat_axis=0, tiled=True)
 
     out = pl.pallas_call(

time: 165 us -> 163 us (0.988)
  blocking collectives: 33.9 us -> 54.7 us
  waiting for transfers between devices: 75.5 us -> 63.9 us
  starting transfers between devices: 4.78 us -> 0.04 us
  Pallas kernels: 31.8 us -> 28.2 us
    all_to_all x0 -> x1, blocking collectives: none -> 20.8 us  [body(): lax.all_to_all(attended, 'seq', split_axis=0, concat_axis=0, tiled=True)]
    all_gather x1, waiting for transfers between devices: 23.6 us -> 10.1 us  [body(): w_all = lax.all_gather(w_out, 'seq', axis=0, tiled=False)]
    all_to_all x1 -> x0, starting transfers between devices: 4.73 us -> none  [body(): lax.all_to_all(attended, 'seq', split_axis=0, concat_axis=0, tiled=True)]
    pallas_call x1, Pallas kernels: 22.4 us -> 18.8 us  [attend_call(): pl.pallas_call(functools.partial(attend_kernel, steps, n_seq), grid=(step...]
  transfers between devices with their start and end apart: 3 -> 2, of which waited for: 2 -> 2; matrix products, arithmetic and copies ran while one was open for 1% -> 0% of each run, Pallas kernels for 14% -> 4%
where the time goes in v3:
time: 163 us; the launch traced here: 160 us
  waiting for transfers between devices  63.9 us (39%)
  blocking collectives  54.7 us (34%)
  Pallas kernels  28.2 us (17%)
  between operations  13.4 us (8%)
    all_gather x1, waiting for transfers between devices, body(): tokens = lax.all_gather(packed, 'seq', axis=0, tiled=True)  53.1 us
    all_to_all x1, blocking collectives, body(): lax.all_to_all(outbox, 'pack', split_axis=0, concat_axis=0, tiled=True)  33.9 us
    all_to_all x1, blocking collectives, body(): lax.all_to_all(attended, 'seq', split_axis=0, concat_axis=0, tiled=True)  20.8 us
    pallas_call x1, Pallas kernels, attend_call(): pl.pallas_call(functools.partial(attend_kernel, steps, n_seq), grid=(step...  18.8 us
    all_gather x1, waiting for transfers between devices, body(): w_all = lax.all_gather(w_out, 'seq', axis=0, tiled=False)  10.1 us
    pallas_call x1, Pallas kernels, body(): pl.pallas_call(functools.partial(project_kernel, n_seq), out_shape=jax.Sh...  3.51 us
  transfers between devices with their start and end apart: 2, of which 2 were waited for; matrix products, arithmetic and copies ran while one was open for 0% of the time, Pallas kernels for 4%

profile of v3, /device:TPU:7, one launch (start us, length us, event | category | flops | bytes accessed | tf_op | source)
XLA Modules:
  0.0 160.3 jit_solution(10144927890709530595)
XLA Ops:
  6.5 0.0 all-gather.6.cloned.1.call-start
  6.5 0.7 all-gather.6.cloned.1.call-update
  7.3 0.0 all-gather.4.cloned.1.call-start
  7.3 2.8 %pack_rows.1 = bf16[32,112,128]{2,1,0:T(8,128)(2,1)} custom-call(s32[1,192]{1,0:T(1,128)} %dest_ref.1, bf16[192,1152]{1,0:T(8,128)(2,1)} %bitcast.8), custom_call_target="tpu_custom_call" | custom-call | tf_op jit(solution)/shard_map/pack_rows/pallas_call | solution.py:251
  10.1 33.9 %all_to_all.10.in_ref = bf16[32,112,128]{2,1,0:T(8,128)(2,1)} all-to-all(bf16[32,112,128]{2,1,0:T(8,128)(2,1)} %pack_rows.1), channel_id=1, replica_groups=mesh['pack'=32,'seq'=16] {'pack'}, dimensions={0} | all-to-all | bytes 1835008 | tf_op jit(solution)/shard_map/all_to_all | solution.py:257
  44.1 3.1 %unpack_rows.1 = bf16[192,1152]{1,0:T(8,128)(2,1)} custom-call(bf16[32,112,128]{2,1,0:T(8,128)(2,1)} %all_to_all.10.in_ref), custom_call_target="tpu_custom_call" | custom-call | tf_op jit(solution)/shard_map/unpack_rows/pallas_call | solution.py:258
  47.1 10.1 %all-gather.6.cloned.1.call-done = bf16[1152,1152]{1,0:T(8,128)(2,1)} async-done(((bf16[72,1152]{1,0:T(8,128)(2,1)}), bf16[1152,1152]{1,0:T(8,128)(2,1)}) %all-gather.6.cloned.1.call-update) | async-done | bytes 2654224 | tf_op jit(solution)/shard_map/all_gather | solution.py:249
  57.2 0.0 all-gather.4.cloned.1.call-update
  57.2 53.1 %all-gather.4.cloned.1.call-done.x_ref = bf16[3072,1152]{1,0:T(8,128)(2,1)} async-done(((bf16[192,1152]{1,0:T(8,128)(2,1)}), bf16[3072,1152]{1,0:T(8,128)(2,1)}) %all-gather.4.cloned.1.call-update) | async-done | bytes 7077904 | tf_op jit(solution)/shard_map/all_gather | solution.py:265
  110.3 18.8 %attend.1 = bf16[16,112,128]{2,1,0:T(8,128)(2,1)} custom-call(s32[1,3072]{1,0:T(1,128)} %doc_ref.1, bf16[3072,1152]{1,0:T(8,128)(2,1)} %all-gather.4.cloned.1.call-done.x_ref, bf16[216,1152]{1,0:T(8,128)(2,1)} %bitcast.7), custom_call_target="tpu_custom_call" | custom-call | tf_op jit(solution)/shard_map/attend/pallas_call | solution.py:223
  129.2 20.8 %all_to_all.11.in_ref = bf16[16,112,128]{2,1,0:T(8,128)(2,1)} all-to-all(bf16[16,112,128]{2,1,0:T(8,128)(2,1)} %attend.1), channel_id=1, replica_groups=mesh['pack'=32,'seq'=16] {'seq'}, dimensions={0} | all-to-all | bytes 917504 | tf_op jit(solution)/shard_map/all_to_all | solution.py:270
  150.0 3.5 %project.1 = bf16[192,1152]{1,0:T(8,128)(2,1)} custom-call(bf16[16,112,128]{2,1,0:T(8,128)(2,1)} %all_to_all.11.in_ref, bf16[16,72,1152]{2,1,0:T(8,128)(2,1)} %bitcast.6), custom_call_target="tpu_custom_call" | custom-call | tf_op jit(solution)/shard_map/project/pallas_call | solution.py:272
Async XLA Ops:
  6.5 50.7 %all-gather.6.cloned.1.call-start = ((), (), s32[]{:S(2)}) async-start(), calls=%async_computation.3 | async-start | bytes 2820096 | tf_op jit(solution)/shard_map/all_gather | solution.py:249
  7.3 103.1 %all-gather.4.cloned.1.call-start = ((), (), s32[]{:S(2)}) async-start(), calls=%async_computation.2 | async-start | bytes 7520256 | tf_op jit(solution)/shard_map/all_gather | solution.py:265
Sparse Core Ops, SparseCore 0:
  9.5 47.6 all-gather.5
  59.3 50.9 all-gather.3

commit v4 on v3

v4 whole, which is shorter than its diff:
```python
import functools
import math

import jax
import jax.numpy as jnp
from jax import lax
from jax.experimental import pallas as pl
from jax.experimental.pallas import tpu as pltpu
from jax.sharding import PartitionSpec as P

HD = 72
CAP = 12
LANES = 128
BLK = 128
BF = jnp.bfloat16
F32 = jnp.float32
NT = (((1,), (1,)), ((), ()))

SHIFTS = (
    (0, ((0, 0), (3, 4), (6, 8))),
    (-12, ((0, 1), (3, 5))),
    (4, ((1, 1), (4, 5))),
    (-8, ((1, 2), (4, 6))),
    (8, ((2, 2), (5, 6))),
    (-4, ((2, 3), (5, 7))),
)
TILES = 7


def iota(shape, dim):
    return lax.broadcasted_iota(jnp.int32, shape, dim)


def onehot(condition):
    return jnp.where(condition, 1.0, 0.0).astype(BF)


def pack_kernel(n_pack, dest_ref, rows_ref, out_ref):
    tok = rows_ref.shape[0]
    group = n_pack * 16
    dest = dest_ref[...]
    owner = ((dest >> 6) * 171) >> 9
    place = dest - owner * tok
    owned = iota((n_pack, tok), 0) == owner
    before = onehot(iota((tok, tok), 0) < iota((tok, tok), 1))
    counted = jnp.dot(onehot(owned), before, preferred_element_type=F32)
    slot = jnp.sum(jnp.where(owned, counted, 0.0), axis=0, keepdims=True).astype(jnp.int32)
    row = iota((group, tok), 0)
    parts = {}
    for shift, pairs in SHIFTS:
        at = slot - shift
        key = jnp.where((at >= 0) & (at < 16), owner * 16 + at, -1)
        picked = jnp.concatenate(
            [rows_ref[:, f * LANES : (f + 1) * LANES] for _, f in pairs], axis=1
        )
        moved = jnp.dot(onehot(row == key), picked, preferred_element_type=F32)
        for n, (tile, _) in enumerate(pairs):
            parts.setdefault(tile, []).append(moved[:, n * LANES : (n + 1) * LANES])
    tags = jnp.where(iota((LANES, tok), 0) == slot, (place + 1).astype(F32), 0.0).astype(BF)
    here = onehot(row == owner * 16 + CAP)
    parts[TILES - 1].append(lax.dot_general(here, tags, NT, preferred_element_type=F32))
    for tile in range(TILES):
        whole = functools.reduce(lambda a, b: a + b, parts[tile])
        out_ref[:, tile * 16 : (tile + 1) * 16, :] = whole.astype(BF).reshape(n_pack, 16, LANES)


def unpack_kernel(n_pack, in_ref, *refs):
    out_ref = refs[-1]
    tok = out_ref.shape[0]
    group = n_pack * 16
    tiles = [in_ref[:, t * 16 : (t + 1) * 16, :].reshape(group, LANES) for t in range(TILES)]
    col = iota((n_pack, group), 1)
    lead = iota((n_pack, group), 0) * 16
    labels = jnp.dot(onehot(col == lead + CAP), tiles[-1], preferred_element_type=F32).astype(BF)
    mine = (col >= lead) & (col < lead + 16)
    offset = iota((LANES, group), 0) - (iota((LANES, group), 1) & 15)
    place = iota((tok, group), 0) + 1
    parts = {}
    for shift, pairs in SHIFTS:
        spread = jnp.dot(labels, onehot(offset == shift), preferred_element_type=F32)
        label = jnp.sum(jnp.where(mine, spread, 0.0), axis=0, keepdims=True).astype(jnp.int32)
        picked = jnp.concatenate([tiles[t] for t, _ in pairs], axis=1)
        moved = jnp.dot(onehot(place == label), picked, preferred_element_type=F32)
        for n, (_, f) in enumerate(pairs):
            parts.setdefault(f, []).append(moved[:, n * LANES : (n + 1) * LANES])
    for f in sorted(parts):
        whole = functools.reduce(lambda a, b: a + b, parts[f])
        out_ref[:, f * LANES : (f + 1) * LANES] = whole.astype(BF)


TOK = 192
QT = 256
KT = 1024
SIDE = 1
VROWS = 80
QKV = 256
AROWS = 112
NEG = -3e38
BACK = (0, 1, -1, 2, -2, 3, -3, 4)
LIMIT = pltpu.CompilerParams(vmem_limit_bytes=56 * 2**20)


def origin(me, n):
    chips = len(BACK)
    core = me & 1
    chip = ((me >> 1) - BACK[n % chips]) & (chips - 1)
    return 2 * chip + (core if n < chips else 1 - core)


def qkv_kernel(*refs):
    *x_refs, mine_w_ref, pair_w_ref, mine_ref, pair_ref = refs
    x = jnp.concatenate([ref[...] for ref in x_refs], axis=0)
    rows = x.shape[0]
    scale = jnp.where(iota((1, 3 * HD), 1) < HD, 1.0 / math.sqrt(HD), 1.0)
    fill = jnp.where(iota((rows, QKV - 3 * HD), 1) < VROWS - HD, 1.0, 0.0)
    for w_ref, out_ref in ((mine_w_ref, mine_ref), (pair_w_ref, pair_ref)):
        qkv = lax.dot_general(x, w_ref[...], NT, preferred_element_type=F32) * scale
        whole = jnp.concatenate([qkv, fill], axis=1).astype(BF)
        out_ref[...] = whole.reshape(rows // TOK, TOK, QKV)


def attend_kernel(n_seq, me_ref, doc_ref, *refs):
    *in_refs, out_ref, q_s, k_s, row_s, v_s, o_s, bound_s = refs
    n = 0
    for ref in in_refs:
        for i in range(ref.shape[0]):
            rows = pl.ds(pl.multiple_of(origin(me_ref[0], n) * TOK, 64), TOK)
            q_s[rows, :] = ref[i, :, 0:HD]
            k_s[rows, :] = ref[i, :, HD : 2 * HD]
            row_s[rows, :] = ref[i, :, LANES:QKV]
            n += 1
    length = q_s.shape[0]
    blocks = length // BLK
    per_q = QT // BLK
    per_k = KT // BLK
    for b in range(blocks):
        turned = row_s[b * BLK : (b + 1) * BLK, :].T
        begin = 2 * HD - LANES
        v_s[:, b * BLK : (b + 1) * BLK] = turned[begin : begin + VROWS, :]
    k_s[length:, :] = jnp.zeros((KT, HD), BF)
    v_s[:, length:] = jnp.zeros((VROWS, KT), BF)
    first = jnp.int32(0)
    for b in range(blocks):
        if b:
            first = jnp.where(doc_ref[0, b * BLK] == doc_ref[0, (b - 1) * BLK], first, b)
        bound_s[0, b] = first
    last = jnp.int32(blocks)
    for b in reversed(range(blocks)):
        if b < blocks - 1:
            last = jnp.where(doc_ref[0, b * BLK] == doc_ref[0, (b + 1) * BLK], last, b + 1)
        bound_s[1, b] = last

    def some_tiles(group, _):
        tiles = []
        for u in range(SIDE):
            t = group * SIDE + u
            bounds = [
                (bound_s[0, t * per_q + i], bound_s[1, t * per_q + i]) for i in range(per_q)
            ]
            q = q_s[pl.ds(pl.multiple_of(t * QT, QT), QT), :]
            tiles.append((t, q, bounds))
        chunks = functools.reduce(
            jnp.maximum, [b[-1][1] - b[0][0] for _, _, b in tiles]
        )
        chunks = (chunks + per_k - 1) // per_k

        def one_chunk(c, carry):
            result = []
            for (_, q, bounds), (high, total) in zip(tiles, carry):
                begin = bounds[0][0] + c * per_k
                keys = pl.ds(pl.multiple_of(jnp.minimum(begin, blocks) * BLK, BLK), KT)
                scores = lax.dot_general(k_s[keys, :], q, NT, preferred_element_type=F32)
                columns = []
                for i, (lo, hi) in enumerate(bounds):
                    kept = [
                        jnp.where(
                            (begin + j >= lo) & (begin + j < hi),
                            scores[j * BLK : (j + 1) * BLK, i * BLK : (i + 1) * BLK],
                            -jnp.inf,
                        )
                        for j in range(per_k)
                    ]
                    columns.append(jnp.concatenate(kept, axis=0))
                scores = jnp.concatenate(columns, axis=1)
                newer = jnp.maximum(high, jnp.max(scores, axis=0, keepdims=True))
                expo = jnp.exp(scores - newer).astype(BF)
                total = total * jnp.exp(high - newer) + jnp.dot(
                    v_s[:, keys], expo, preferred_element_type=F32
                )
                result.append((newer, total))
            return tuple(result)

        carry = tuple(
            (jnp.full((1, QT), NEG, F32), jnp.zeros((VROWS, QT), F32)) for _ in range(SIDE)
        )
        for (t, _, _), (_, total) in zip(tiles, lax.fori_loop(0, chunks, one_chunk, carry)):
            o_s[:, pl.ds(pl.multiple_of(t * QT, QT), QT)] = total / total[HD : HD + 1, :]
        return 0

    lax.fori_loop(0, length // (QT * SIDE), some_tiles, 0)
    tok = length // n_seq
    for s in range(n_seq):
        mine = o_s[0:HD, s * tok : (s + 1) * tok]
        rest = mine[:, LANES:tok]
        out_ref[s, 0:64, :] = mine[0:64, 0:LANES].astype(BF)
        out_ref[s, 64:96, :] = jnp.concatenate([rest[0:32], rest[32:64]], axis=1).astype(BF)
        empty = jnp.zeros((HD - 64, 2 * LANES - tok), F32)
        out_ref[s, 96:112, :] = jnp.concatenate(
            [mine[64:HD, 0:LANES], jnp.concatenate([rest[64:HD], empty], axis=1)], axis=0
        ).astype(BF)


def project_kernel(n_seq, me_ref, in_ref, mine_w_ref, pair_w_ref, out_ref):
    width = out_ref.shape[1]
    tok = out_ref.shape[0]
    rest = tok - LANES
    half = n_seq // 2
    came = [origin(me_ref[0], n) for n in range(n_seq)]

    def features(begin, end):
        return jnp.concatenate([in_ref[s, begin:end, :] for s in came], axis=0)

    lo = features(0, 32)
    hi = features(32, 64)
    far = features(64, 96)
    tail = features(96, 112).astype(F32)
    upper = (iota(tail.shape, 0) & 15) < 8
    tail_near = jnp.where(upper, tail, 0.0).astype(BF)
    tail_far = jnp.where(upper, 0.0, tail).astype(BF)
    near = jnp.concatenate([lo, hi, tail_near], axis=0).T
    far_t = far.T
    distant = jnp.concatenate([far_t[0:rest], far_t[rest:LANES], tail_far.T[0:rest]], axis=1)
    left = jnp.concatenate([near, distant], axis=0)
    weights = []
    for begin in (0, 32):
        for ref in (mine_w_ref, pair_w_ref):
            weights.append(ref[:, begin : begin + 32, :].reshape(half * 32, width))
    for ref in (mine_w_ref, pair_w_ref):
        last = ref[:, 64:HD, :].astype(F32)
        weights.append(jnp.concatenate([last, last], axis=1).reshape(half * 16, width).astype(BF))
    weights = jnp.concatenate(weights, axis=0)
    out_ref[...] = jnp.dot(left, weights, preferred_element_type=F32).astype(BF)


def cost(flops, operands, out_shape):
    total = sum(math.prod(x.shape) * x.dtype.itemsize for x in operands)
    total += sum(math.prod(x.shape) * x.dtype.itemsize for x in jax.tree.leaves(out_shape))
    return pl.CostEstimate(flops=flops, bytes_accessed=total, transcendentals=0)


def local_call(kernel, out_shape, *operands, name, flops, small=0, scratch=(), behind=()):
    smem = pl.BlockSpec(memory_space=pltpu.SMEM)
    vmem = pl.BlockSpec(memory_space=pltpu.VMEM)
    after = [pl.BlockSpec(memory_space=pl.ANY)] * len(behind)
    return pl.pallas_call(
        kernel,
        out_shape=out_shape,
        in_specs=[smem] * small + [vmem] * (len(operands) - small) + after,
        out_specs=jax.tree.map(lambda _: vmem, out_shape),
        scratch_shapes=scratch,
        compiler_params=LIMIT,
        cost_estimate=cost(flops, operands, out_shape),
        name=name,
    )(*operands, *behind)


def project_qkv(blocks, mine_w, pair_w, name):
    rows = sum(x.shape[0] for x in blocks)
    out = jax.ShapeDtypeStruct((rows // TOK, TOK, QKV), BF)
    flops = 2 * rows * mine_w.shape[1] * 6 * HD
    return local_call(
        qkv_kernel, (out, out), *blocks, mine_w, pair_w, name=name, flops=flops
    )


def attend_call(me, doc_ids, n_seq, *blocks):
    length = n_seq * TOK
    return local_call(
        functools.partial(attend_kernel, n_seq),
        jax.ShapeDtypeStruct((n_seq, AROWS, LANES), BF),
        me,
        doc_ids,
        *blocks,
        small=2,
        flops=2 * length * length * HD,
        scratch=[
            pltpu.VMEM((length, HD), BF),
            pltpu.VMEM((length + KT, HD), BF),
            pltpu.VMEM((length, LANES), BF),
            pltpu.VMEM((VROWS, length + KT), BF),
            pltpu.VMEM((VROWS, length), F32),
            pltpu.SMEM((2, length // BLK), jnp.int32),
        ],
        name="attend",
    )


def ring_step(right, left, n_seq):
    up = [(i, (i + 2) % n_seq) for i in range(n_seq)]
    down = [(i, (i - 2) % n_seq) for i in range(n_seq)]
    return lax.ppermute(right, "seq", up), lax.ppermute(left, "seq", down)


def body(source, destination, doc_ids, w_qkv, w_out):
    n_pack = lax.axis_size("pack")
    n_seq = lax.axis_size("seq")
    width = source.shape[2]
    shape = jax.ShapeDtypeStruct
    me = lax.axis_index("seq").astype(jnp.int32).reshape(1)
    w_t = jnp.transpose(w_qkv, (0, 2, 1)).reshape(3 * HD, width)

    def other_core(x):
        return lax.ppermute(x, "seq", [(i, i ^ 1) for i in range(n_seq)])

    outbox = local_call(
        functools.partial(pack_kernel, n_pack),
        shape((n_pack, TILES * 16, LANES), BF),
        destination,
        source[0],
        name="pack_rows",
        flops=10**9,
    )
    inbox = lax.all_to_all(outbox, "pack", split_axis=0, concat_axis=0, tiled=True)

    pair_w = other_core(w_t)
    right = left = w_out
    held = [w_out]
    for _ in range(3):
        right, left = ring_step(right, left, n_seq)
        held += [right, left]
    held.append(ring_step(right, left, n_seq)[0])
    w_mine = jnp.stack(held)
    w_pair = other_core(w_mine)

    packed = local_call(
        functools.partial(unpack_kernel, n_pack),
        shape((TOK, width), BF),
        inbox,
        name="unpack_rows",
        flops=10**9,
        behind=(w_pair, pair_w),
    )
    right = left = packed
    held = [packed]
    for _ in range(3):
        right, left = ring_step(right, left, n_seq)
        held += [right, left]
    held += ring_step(right[: TOK // 2], left[TOK // 2 :], n_seq)

    mine_a, theirs_a = project_qkv(held[:5], w_t, pair_w, "qkv_first")
    mine_b, theirs_b = project_qkv(held[5:], w_t, pair_w, "qkv_last")
    attended = attend_call(
        me, doc_ids, n_seq, mine_a, mine_b, other_core(theirs_a), other_core(theirs_b)
    )
    blocks = lax.all_to_all(attended, "seq", split_axis=0, concat_axis=0, tiled=True)

    out = local_call(
        functools.partial(project_kernel, n_seq),
        shape((TOK, width), BF),
        me,
        blocks,
        w_mine,
        w_pair,
        name="project",
        flops=2 * TOK * width * width,
        small=1,
    )
    return out[None]


def solution(mesh):
    placed = (
        P("seq", "pack", None),
        P("seq", "pack"),
        P("pack", None),
        P(None, None, "seq"),
        P("seq", None),
    )
    return jax.shard_map(
        body, mesh=mesh, in_specs=placed, out_specs=P("pack", "seq", None), check_vma=False
    )
```

time: 163 us -> 171 us (1.049)
  starting transfers between devices: 0.04 us -> 75.8 us
  blocking collectives: 54.7 us -> 23.1 us
  waiting for transfers between devices: 63.9 us -> 33.8 us
  between operations: 13.4 us -> 0.42 us
  Pallas kernels: 28.2 us -> 32.6 us
  local copies, waits for them, and re-layouts: 0 us -> 3.37 us
    all_gather x2 -> x0, waiting for transfers between devices: 63.2 us -> none  [the longest x1 53.1 us: body(): tokens = lax.all_gather(packed, 'seq', axis=0, tiled=True)]
    ppermute x0 -> x19, starting transfers between devices: none -> 62.7 us  [the longest x15 48 us: ring_step(): return (lax.ppermute(right, 'seq', up), lax.ppermute(left, 'seq', down))]
    all_to_all x1 -> x0, blocking collectives: 33.9 us -> none  [body(): lax.all_to_all(outbox, 'pack', split_axis=0, concat_axis=0, tiled=True)]
    ppermute x0 -> x19, waiting for transfers between devices: none -> 33.8 us  [the longest x15 30.1 us: ring_step(): return (lax.ppermute(right, 'seq', up), lax.ppermute(left, 'seq', down))]
    all_to_all x0 -> x1, starting transfers between devices: none -> 13.1 us  [body(): lax.all_to_all(outbox, 'pack', split_axis=0, concat_axis=0, tiled=True)]
    pallas_call x4 -> x6, Pallas kernels: 28.2 us -> 32.6 us  [local_call(): pl.pallas_call(kernel, out_shape=out_shape, in_specs=[smem] * small + [vm...]
    unnamed x0 -> x35, local copies, waits for them, and re-layouts: none -> 3.31 us
    all_to_all x1, blocking collectives: 20.8 us -> 23.1 us  [body(): lax.all_to_all(attended, 'seq', split_axis=0, concat_axis=0, tiled=True)]
  transfers between devices with their start and end apart: 2 -> 20, of which waited for: 2 -> 8; matrix products, arithmetic and copies ran while one was open for 0% -> 0% of each run, Pallas kernels for 4% -> 6%
where the time goes in v4:
time: 171 us; the launch traced here: 169 us
  starting transfers between devices  75.8 us (44%)
  waiting for transfers between devices  33.8 us (20%)
  Pallas kernels  32.6 us (19%)
  blocking collectives  23.1 us (14%)
  local copies, waits for them, and re-layouts  3.37 us (2%)
    ppermute x15, starting transfers between devices, ring_step(): return (lax.ppermute(right, 'seq', up), lax.ppermute(left, 'seq', down))  48 us
    pallas_call x6, Pallas kernels, local_call(): pl.pallas_call(kernel, out_shape=out_shape, in_specs=[smem] * small + [vm...  32.6 us
    ppermute x15, waiting for transfers between devices, ring_step(): return (lax.ppermute(right, 'seq', up), lax.ppermute(left, 'seq', down))  30.1 us
    all_to_all x1, blocking collectives, body(): lax.all_to_all(attended, 'seq', split_axis=0, concat_axis=0, tiled=True)  23.1 us
    ppermute x4, starting transfers between devices, other_core(): return lax.ppermute(x, 'seq', [(i, i ^ 1) for i in range(n_seq)])  14.8 us
    all_to_all x1, starting transfers between devices, body(): lax.all_to_all(outbox, 'pack', split_axis=0, concat_axis=0, tiled=True)  13.1 us
    ppermute x4, waiting for transfers between devices, other_core(): return lax.ppermute(x, 'seq', [(i, i ^ 1) for i in range(n_seq)])  3.7 us
  transfers between devices with their start and end apart: 20, of which 8 were waited for; matrix products, arithmetic and copies ran while one was open for 0% of the time, Pallas kernels for 6%

profile of v4, /device:TPU:7, one launch (start us, length us, event | category | flops | bytes accessed | tf_op | source)
XLA Modules:
  0.0 169.0 jit_solution(13345644440155403787)
XLA Ops:
  0.0 3.2 %collective-permute-start = (bf16[72,1152]{1,0:T(8,128)(2,1)}, bf16[72,1152]{1,0:T(8,128)(2,1)S(1)}, u32[]{:S(2)}, u32[]{:S(2)}) collective-permute-start(bf16[72,1152]{1,0:T(8,128)(2,1)} %param.9), channel_id=1, source_target_pairs={{0,2},{1,3},{2,4},{3,5},{4,6},{5,7},{6,8},{7,9},{8,10},{9,11},{10,... | collective-permute-start | bytes 497672 | tf_op jit(solution)/shard_map/ppermute | solution.py:301
  3.2 3.8 %collective-permute-start.1 = (bf16[72,1152]{1,0:T(8,128)(2,1)}, bf16[72,1152]{1,0:T(8,128)(2,1)S(1)}, u32[]{:S(2)}, u32[]{:S(2)}) collective-permute-start(bf16[72,1152]{1,0:T(8,128)(2,1)} %param.9), channel_id=1, source_target_pairs={{0,14},{1,15},{2,0},{3,1},{4,2},{5,3},{6,4},{7,5},{8,6},{9,7},{10,... | collective-permute-start | bytes 497672 | tf_op jit(solution)/shard_map/ppermute | solution.py:301
  7.0 2.8 %pack_rows.1 = bf16[32,112,128]{2,1,0:T(8,128)(2,1)} custom-call(s32[1,192]{1,0:T(1,128)} %dest_ref.1, bf16[192,1152]{1,0:T(8,128)(2,1)} %bitcast.25), custom_call_target="tpu_custom_call" | custom-call | flops 1000000000 | bytes 1360640 | tf_op jit(solution)/shard_map/pack_rows/pallas_call | solution.py:255
  9.9 13.1 %all-to-all-start = ((bf16[32,112,128]{2,1,0:T(8,128)(2,1)}), bf16[32,112,128]{2,1,0:T(8,128)(2,1)}, u32[]{:S(2)}, u32[]{:S(2)}) async-start(bf16[32,112,128]{2,1,0:T(8,128)(2,1)} %pack_rows.1), calls=%async_computation | async-start | bytes 1835008 | tf_op jit(solution)/shard_map/all_to_all | solution.py:323
  22.9 0.0 copy-start.4
  23.0 0.0 collective-permute-done
  23.0 2.1 %collective-permute-start.2 = (bf16[72,1152]{1,0:T(8,128)(2,1)S(1)}, bf16[72,1152]{1,0:T(8,128)(2,1)S(1)}, u32[]{:S(2)}, u32[]{:S(2)}) collective-permute-start(bf16[72,1152]{1,0:T(8,128)(2,1)S(1)} %collective-permute-done), channel_id=1, source_target_pairs={{0,2},{1,3},{2,4},{3,5},{4,6},{5,7},{6,8},{7,9},{8,10},{9,11},{10,... | collective-permute-start | bytes 497672 | tf_op jit(solution)/shard_map/ppermute | solution.py:301
  25.1 0.0 collective-permute-done.1
  25.1 4.6 %collective-permute-start.3 = (bf16[72,1152]{1,0:T(8,128)(2,1)S(1)}, bf16[72,1152]{1,0:T(8,128)(2,1)S(1)}, u32[]{:S(2)}, u32[]{:S(2)}) collective-permute-start(bf16[72,1152]{1,0:T(8,128)(2,1)S(1)} %collective-permute-done.1), channel_id=1, source_target_pairs={{0,14},{1,15},{2,0},{3,1},{4,2},{5,3},{6,4},{7,5},{8,6},{9,7},{10,... | collective-permute-start | bytes 497672 | tf_op jit(solution)/shard_map/ppermute | solution.py:301
  29.7 1.1 collective-permute-done.2
  30.8 1.9 %collective-permute-start.4 = (bf16[72,1152]{1,0:T(8,128)(2,1)S(1)}, bf16[72,1152]{1,0:T(8,128)(2,1)S(1)}, u32[]{:S(2)}, u32[]{:S(2)}) collective-permute-start(bf16[72,1152]{1,0:T(8,128)(2,1)S(1)} %collective-permute-done.2), channel_id=1, source_target_pairs={{0,2},{1,3},{2,4},{3,5},{4,6},{5,7},{6,8},{7,9},{8,10},{9,11},{10,... | collective-permute-start | bytes 497672 | tf_op jit(solution)/shard_map/ppermute | solution.py:301
  32.8 0.0 collective-permute-done.3
  32.8 4.6 %collective-permute-start.5 = (bf16[72,1152]{1,0:T(8,128)(2,1)S(1)}, bf16[72,1152]{1,0:T(8,128)(2,1)S(1)}, u32[]{:S(2)}, u32[]{:S(2)}) collective-permute-start(bf16[72,1152]{1,0:T(8,128)(2,1)S(1)} %collective-permute-done.3), channel_id=1, source_target_pairs={{0,14},{1,15},{2,0},{3,1},{4,2},{5,3},{6,4},{7,5},{8,6},{9,7},{10,... | collective-permute-start | bytes 497672 | tf_op jit(solution)/shard_map/ppermute | solution.py:301
  37.4 1.1 collective-permute-done.4
  38.5 1.9 %collective-permute-start.6 = (bf16[72,1152]{1,0:T(8,128)(2,1)S(1)}, bf16[72,1152]{1,0:T(8,128)(2,1)S(1)}, u32[]{:S(2)}, u32[]{:S(2)}) collective-permute-start(bf16[72,1152]{1,0:T(8,128)(2,1)S(1)} %collective-permute-done.4), channel_id=1, source_target_pairs={{0,2},{1,3},{2,4},{3,5},{4,6},{5,7},{6,8},{7,9},{8,10},{9,11},{10,... | collective-permute-start | bytes 497672 | tf_op jit(solution)/shard_map/ppermute | solution.py:301
  40.4 0.0 collective-permute-done.5
  40.5 5.7 %collective-permute-done.6 = bf16[72,1152]{1,0:T(8,128)(2,1)S(1)} collective-permute-done((bf16[72,1152]{1,0:T(8,128)(2,1)S(1)}, bf16[72,1152]{1,0:T(8,128)(2,1)S(1)}, u32[]{:S(2)}, u32[]{:S(2)}) %collective-permute-start.6) | collective-permute-done | bytes 165920 | tf_op jit(solution)/shard_map/ppermute | solution.py:301
  46.2 5.7 %collective-permute-start.7 = (bf16[8,72,1152]{2,1,0:T(8,128)(2,1)S(1)}, bf16[8,72,1152]{2,1,0:T(8,128)(2,1)S(1)}, u32[]{:S(2)}, u32[]{:S(2)}) collective-permute-start(bf16[8,72,1152]{2,1,0:T(8,128)(2,1)S(1)} %bitcast_dynamic-update-slice_fusion.mine_w_ref), channel_id=1, source_target_pairs={{0,1},{1,0},{2,3},{3,2},{4,5},{5,4},{6,7},{7,6},{8,9},{9,8},{10,11... | collective-permute-start | bytes 3981320 | tf_op jit(solution)/shard_map/ppermute | solution.py:313
  51.9 1.9 %collective-permute-start.8 = (bf16[216,1152]{1,0:T(8,128)(2,1)S(1)}, bf16[216,1152]{1,0:T(8,128)(2,1)}, u32[]{:S(2)}, u32[]{:S(2)}) collective-permute-start(bf16[216,1152]{1,0:T(8,128)(2,1)S(1)} %bitcast.24), channel_id=1, source_target_pairs={{0,1},{1,0},{2,3},{3,2},{4,5},{5,4},{6,7},{7,6},{8,9},{9,8},{10,11... | collective-permute-start | bytes 1493000 | tf_op jit(solution)/shard_map/ppermute | solution.py:313
  53.8 2.0 %collective-permute-done.8.refs_1_.refs_6_.refs_5_ = bf16[216,1152]{1,0:T(8,128)(2,1)} collective-permute-done((bf16[216,1152]{1,0:T(8,128)(2,1)S(1)}, bf16[216,1152]{1,0:T(8,128)(2,1)}, u32[]{:S(2)}, u32[]{:S(2)}) %collective-permute-start.8) | collective-permute-done | bytes 497696 | tf_op jit(solution)/shard_map/ppermute | solution.py:313
  55.8 0.0 all-to-all-done.in_ref
  55.8 1.1 copy-done.1
  56.9 3.1 %unpack_rows.1.refs_0_ = bf16[192,1152]{1,0:T(8,128)(2,1)} custom-call(bf16[32,112,128]{2,1,0:T(8,128)(2,1)} %all-to-all-done.in_ref, bf16[8,72,1152]{2,1,0:T(8,128)(2,1)} %copy-done.1, bf16[216,1152]{1,0:T(8,128)(2,1)} %collective-permute-done.8.refs_1_.refs_6_.refs_5_), custom_call_target="tpu_custom_call" | custom-call | flops 1000000000 | bytes 1359872 | tf_op jit(solution)/shard_map/unpack_rows/pallas_call | solution.py:255
  60.0 1.9 %collective-permute-start.9 = (bf16[192,1152]{1,0:T(8,128)(2,1)}, bf16[192,1152]{1,0:T(8,128)(2,1)S(1)}, u32[]{:S(2)}, u32[]{:S(2)}) collective-permute-start(bf16[192,1152]{1,0:T(8,128)(2,1)} %unpack_rows.1.refs_0_), channel_id=1, source_target_pairs={{0,2},{1,3},{2,4},{3,5},{4,6},{5,7},{6,8},{7,9},{8,10},{9,11},{10,... | collective-permute-start | bytes 1327112 | tf_op jit(solution)/shard_map/ppermute | solution.py:301
  61.9 4.6 %collective-permute-start.10 = (bf16[192,1152]{1,0:T(8,128)(2,1)}, bf16[192,1152]{1,0:T(8,128)(2,1)S(1)}, u32[]{:S(2)}, u32[]{:S(2)}) collective-permute-start(bf16[192,1152]{1,0:T(8,128)(2,1)} %unpack_rows.1.refs_0_), channel_id=1, source_target_pairs={{0,14},{1,15},{2,0},{3,1},{4,2},{5,3},{6,4},{7,5},{8,6},{9,7},{10,... | collective-permute-start | bytes 1327112 | tf_op jit(solution)/shard_map/ppermute | solution.py:301
  66.5 8.4 %collective-permute-done.9.refs_1_ = bf16[192,1152]{1,0:T(8,128)(2,1)S(1)} collective-permute-done((bf16[192,1152]{1,0:T(8,128)(2,1)}, bf16[192,1152]{1,0:T(8,128)(2,1)S(1)}, u32[]{:S(2)}, u32[]{:S(2)}) %collective-permute-start.9) | collective-permute-done | bytes 442400 | tf_op jit(solution)/shard_map/ppermute | solution.py:301
  74.9 1.9 %collective-permute-start.11 = (bf16[192,1152]{1,0:T(8,128)(2,1)S(1)}, bf16[192,1152]{1,0:T(8,128)(2,1)S(1)}, u32[]{:S(2)}, u32[]{:S(2)}) collective-permute-start(bf16[192,1152]{1,0:T(8,128)(2,1)S(1)} %collective-permute-done.9.refs_1_), channel_id=1, source_target_pairs={{0,2},{1,3},{2,4},{3,5},{4,6},{5,7},{6,8},{7,9},{8,10},{9,11},{10,... | collective-permute-start | bytes 1327112 | tf_op jit(solution)/shard_map/ppermute | solution.py:301
  76.8 4.6 %collective-permute-start.12 = (bf16[192,1152]{1,0:T(8,128)(2,1)S(1)}, bf16[192,1152]{1,0:T(8,128)(2,1)S(1)}, u32[]{:S(2)}, u32[]{:S(2)}) collective-permute-start(bf16[192,1152]{1,0:T(8,128)(2,1)S(1)} %collective-permute-done.10.refs_2_), channel_id=1, source_target_pairs={{0,14},{1,15},{2,0},{3,1},{4,2},{5,3},{6,4},{7,5},{8,6},{9,7},{10,... | collective-permute-start | bytes 1327112 | tf_op jit(solution)/shard_map/ppermute | solution.py:301
  81.4 7.3 %collective-permute-done.11.refs_3_ = bf16[192,1152]{1,0:T(8,128)(2,1)S(1)} collective-permute-done((bf16[192,1152]{1,0:T(8,128)(2,1)S(1)}, bf16[192,1152]{1,0:T(8,128)(2,1)S(1)}, u32[]{:S(2)}, u32[]{:S(2)}) %collective-permute-start.11) | collective-permute-done | bytes 442400 | tf_op jit(solution)/shard_map/ppermute | solution.py:301
  88.7 1.9 %collective-permute-start.13 = (bf16[192,1152]{1,0:T(8,128)(2,1)S(1)}, bf16[192,1152]{1,0:T(8,128)(2,1)S(1)}, u32[]{:S(2)}, u32[]{:S(2)}) collective-permute-start(bf16[192,1152]{1,0:T(8,128)(2,1)S(1)} %collective-permute-done.11.refs_3_), channel_id=1, source_target_pairs={{0,2},{1,3},{2,4},{3,5},{4,6},{5,7},{6,8},{7,9},{8,10},{9,11},{10,... | collective-permute-start | bytes 1327112 | tf_op jit(solution)/shard_map/ppermute | solution.py:301
  90.6 0.0 collective-permute-done.12.refs_4_
  90.7 4.6 %collective-permute-start.14 = (bf16[192,1152]{1,0:T(8,128)(2,1)S(1)}, bf16[192,1152]{1,0:T(8,128)(2,1)S(1)}, u32[]{:S(2)}, u32[]{:S(2)}) collective-permute-start(bf16[192,1152]{1,0:T(8,128)(2,1)S(1)} %collective-permute-done.12.refs_4_), channel_id=1, source_target_pairs={{0,14},{1,15},{2,0},{3,1},{4,2},{5,3},{6,4},{7,5},{8,6},{9,7},{10,... | collective-permute-start | bytes 1327112 | tf_op jit(solution)/shard_map/ppermute | solution.py:301
  95.2 6.4 %collective-permute-done.13.refs_0_ = bf16[192,1152]{1,0:T(8,128)(2,1)S(1)} collective-permute-done((bf16[192,1152]{1,0:T(8,128)(2,1)S(1)}, bf16[192,1152]{1,0:T(8,128)(2,1)S(1)}, u32[]{:S(2)}, u32[]{:S(2)}) %collective-permute-start.13) | collective-permute-done | bytes 442400 | tf_op jit(solution)/shard_map/ppermute | solution.py:301
  101.6 1.9 %collective-permute-start.15 = (bf16[96,1152]{1,0:T(8,128)(2,1)S(1)}, bf16[96,1152]{1,0:T(8,128)(2,1)S(1)}, u32[]{:S(2)}, u32[]{:S(2)}) collective-permute-start(bf16[96,1152]{1,0:T(8,128)(2,1)S(1)} %slice.8), channel_id=1, source_target_pairs={{0,2},{1,3},{2,4},{3,5},{4,6},{5,7},{6,8},{7,9},{8,10},{9,11},{10,... | collective-permute-start | bytes 663560 | tf_op jit(solution)/shard_map/ppermute | solution.py:301
  103.6 0.0 collective-permute-done.14.refs_1_
  103.6 4.6 %collective-permute-start.16 = (bf16[96,1152]{1,0:T(8,128)(2,1)S(1)}, bf16[96,1152]{1,0:T(8,128)(2,1)S(1)}, u32[]{:S(2)}, u32[]{:S(2)}) collective-permute-start(bf16[96,1152]{1,0:T(8,128)(2,1)S(1)} %slice.9), channel_id=1, source_target_pairs={{0,14},{1,15},{2,0},{3,1},{4,2},{5,3},{6,4},{7,5},{8,6},{9,7},{10,... | collective-permute-start | bytes 663560 | tf_op jit(solution)/shard_map/ppermute | solution.py:301
  108.2 4.3 %qkv_first.1 = (bf16[5,192,256]{2,1,0:T(8,128)(2,1)}, bf16[5,192,256]{2,1,0:T(8,128)(2,1)}) custom-call(bf16[192,1152]{1,0:T(8,128)(2,1)} %unpack_rows.1.refs_0_, bf16[192,1152]{1,0:T(8,128)(2,1)} %copy-done.9, bf16[192,1152]{1,0:T(8,128)(2,1)} %copy-done.10, bf16[192,1152]{1,0:T(8,128)(2,1)} %copy-done.11, bf16[192,1152]{1,0:T(8,128)(2,1)} %copy-done.12, ...), custom_call_target="tpu_custom_call" | custom-call | flops 955514880 | bytes 4190208 | tf_op jit(solution)/shard_map/qkv_first/pallas_call | solution.py:255
  112.5 5.2 %collective-permute-start.17 = (bf16[5,192,256]{2,1,0:T(8,128)(2,1)}, bf16[5,192,256]{2,1,0:T(8,128)(2,1)S(1)}, u32[]{:S(2)}, u32[]{:S(2)}) collective-permute-start(bf16[5,192,256]{2,1,0:T(8,128)(2,1)} %get-tuple-element.11), channel_id=1, source_target_pairs={{0,1},{1,0},{2,3},{3,2},{4,5},{5,4},{6,7},{7,6},{8,9},{9,8},{10,11... | collective-permute-start | bytes 1474568 | tf_op jit(solution)/shard_map/ppermute | solution.py:313
  117.7 0.0 collective-permute-done.15.refs_2_
  117.8 0.7 copy-done.5
  118.4 0.7 copy-done.6
  119.1 3.4 %qkv_last.1 = (bf16[3,192,256]{2,1,0:T(8,128)(2,1)}, bf16[3,192,256]{2,1,0:T(8,128)(2,1)}) custom-call(bf16[192,1152]{1,0:T(8,128)(2,1)} %copy-done.2, bf16[192,1152]{1,0:T(8,128)(2,1)} %copy-done.3, bf16[96,1152]{1,0:T(8,128)(2,1)} %copy-done.5, bf16[96,1152]{1,0:T(8,128)(2,1)} %copy-done.6, bf16[216,1152]{1,0:T(8,128)(2,1)} %bitcast.23, ...), custom_call_target="tpu_custom_call" | custom-call | flops 573308928 | bytes 2912256 | tf_op jit(solution)/shard_map/qkv_last/pallas_call | solution.py:255
  122.5 1.9 %collective-permute-start.18 = (bf16[3,192,256]{2,1,0:T(8,128)(2,1)}, bf16[3,192,256]{2,1,0:T(8,128)(2,1)S(1)}, u32[]{:S(2)}, u32[]{:S(2)}) collective-permute-start(bf16[3,192,256]{2,1,0:T(8,128)(2,1)} %get-tuple-element.12), channel_id=1, source_target_pairs={{0,1},{1,0},{2,3},{3,2},{4,5},{5,4},{6,7},{7,6},{8,9},{9,8},{10,11... | collective-permute-start | bytes 884744 | tf_op jit(solution)/shard_map/ppermute | solution.py:313
  124.4 1.7 %collective-permute-done.18.refs_3_ = bf16[3,192,256]{2,1,0:T(8,128)(2,1)S(1)} collective-permute-done((bf16[3,192,256]{2,1,0:T(8,128)(2,1)}, bf16[3,192,256]{2,1,0:T(8,128)(2,1)S(1)}, u32[]{:S(2)}, u32[]{:S(2)}) %collective-permute-start.18) | collective-permute-done | bytes 294944 | tf_op jit(solution)/shard_map/ppermute | solution.py:313
  126.2 0.7 copy-done.13
  126.9 15.6 %attend.1 = bf16[16,112,128]{2,1,0:T(8,128)(2,1)} custom-call(s32[1]{0:T(128)} %bitcast.me_ref, s32[1,3072]{1,0:T(1,128)} %doc_ref.1, bf16[5,192,256]{2,1,0:T(8,128)(2,1)} %get-tuple-element.9.refs_0_, bf16[3,192,256]{2,1,0:T(8,128)(2,1)} %get-tuple-element.10.refs_1_, bf16[5,192,256]{2,1,0:T(8,128)(2,1)} %copy-done.8, bf16[3,192,256]{2,1,0:T(8,128)(2,1)} %copy-done.13), custom_call_target="tpu_custom_call" | custom-call | flops 1358954496 | bytes 2043908 | tf_op jit(solution)/shard_map/attend/pallas_call | solution.py:255
  142.4 23.1 %all_to_all.10.in_ref = bf16[16,112,128]{2,1,0:T(8,128)(2,1)} all-to-all(bf16[16,112,128]{2,1,0:T(8,128)(2,1)} %attend.1), channel_id=1, replica_groups=mesh['pack'=32,'seq'=16] {'seq'}, dimensions={0} | all-to-all | bytes 917504 | tf_op jit(solution)/shard_map/all_to_all | solution.py:355
  165.6 3.5 %project.1 = bf16[192,1152]{1,0:T(8,128)(2,1)} custom-call(s32[1]{0:T(128)} %bitcast.me_ref, bf16[16,112,128]{2,1,0:T(8,128)(2,1)} %all_to_all.10.in_ref, bf16[8,72,1152]{2,1,0:T(8,128)(2,1)} %copy-done, bf16[8,72,1152]{2,1,0:T(8,128)(2,1)} %copy-done.1), custom_call_target="tpu_custom_call" | custom-call | flops 509607936 | bytes 3555332 | tf_op jit(solution)/shard_map/project/pallas_call | solution.py:255
  (37 shorter events, 0.3 us)
Async XLA Ops:
  0.0 23.0 %collective-permute-start = (bf16[72,1152]{1,0:T(8,128)(2,1)}, bf16[72,1152]{1,0:T(8,128)(2,1)S(1)}, u32[]{:S(2)}, u32[]{:S(2)}) collective-permute-start(bf16[72,1152]{1,0:T(8,128)(2,1)} %param.9), channel_id=1, source_target_pairs={{0,2},{1,3},{2,4},{3,5},{4,6},{5,7},{6,8},{7,9},{8,10},{9,11},{10,... | collective-permute-start | bytes 497672 | tf_op jit(solution)/shard_map/ppermute | solution.py:301
  3.2 21.9 %collective-permute-start.1 = (bf16[72,1152]{1,0:T(8,128)(2,1)}, bf16[72,1152]{1,0:T(8,128)(2,1)S(1)}, u32[]{:S(2)}, u32[]{:S(2)}) collective-permute-start(bf16[72,1152]{1,0:T(8,128)(2,1)} %param.9), channel_id=1, source_target_pairs={{0,14},{1,15},{2,0},{3,1},{4,2},{5,3},{6,4},{7,5},{8,6},{9,7},{10,... | collective-permute-start | bytes 497672 | tf_op jit(solution)/shard_map/ppermute | solution.py:301
  9.9 13.1 %copy-start.7 = (bf16[72,1152]{1,0:T(8,128)(2,1)S(1)}, bf16[72,1152]{1,0:T(8,128)(2,1)}, u32[]{:S(2)}) copy-start(bf16[72,1152]{1,0:T(8,128)(2,1)} %param.9) | copy-start | bytes 497668
  9.9 46.0 %all-to-all-start = ((bf16[32,112,128]{2,1,0:T(8,128)(2,1)}), bf16[32,112,128]{2,1,0:T(8,128)(2,1)}, u32[]{:S(2)}, u32[]{:S(2)}) async-start(bf16[32,112,128]{2,1,0:T(8,128)(2,1)} %pack_rows.1), calls=%async_computation | async-start | bytes 1835008 | tf_op jit(solution)/shard_map/all_to_all | solution.py:323
  22.9 29.0 %copy-start.4 = (bf16[3,1152,72]{1,2,0:T(8,128)(2,1)S(1)}, bf16[3,1152,72]{1,2,0:T(8,128)(2,1)}, u32[]{:S(2)}) copy-start(bf16[3,1152,72]{1,2,0:T(8,128)(2,1)} %param.8) | copy-start | bytes 1492996
  23.0 7.8 %collective-permute-start.2 = (bf16[72,1152]{1,0:T(8,128)(2,1)S(1)}, bf16[72,1152]{1,0:T(8,128)(2,1)S(1)}, u32[]{:S(2)}, u32[]{:S(2)}) collective-permute-start(bf16[72,1152]{1,0:T(8,128)(2,1)S(1)} %collective-permute-done), channel_id=1, source_target_pairs={{0,2},{1,3},{2,4},{3,5},{4,6},{5,7},{6,8},{7,9},{8,10},{9,11},{10,... | collective-permute-start | bytes 497672 | tf_op jit(solution)/shard_map/ppermute | solution.py:301
  25.1 7.7 %collective-permute-start.3 = (bf16[72,1152]{1,0:T(8,128)(2,1)S(1)}, bf16[72,1152]{1,0:T(8,128)(2,1)S(1)}, u32[]{:S(2)}, u32[]{:S(2)}) collective-permute-start(bf16[72,1152]{1,0:T(8,128)(2,1)S(1)} %collective-permute-done.1), channel_id=1, source_target_pairs={{0,14},{1,15},{2,0},{3,1},{4,2},{5,3},{6,4},{7,5},{8,6},{9,7},{10,... | collective-permute-start | bytes 497672 | tf_op jit(solution)/shard_map/ppermute | solution.py:301
  30.8 7.7 %collective-permute-start.4 = (bf16[72,1152]{1,0:T(8,128)(2,1)S(1)}, bf16[72,1152]{1,0:T(8,128)(2,1)S(1)}, u32[]{:S(2)}, u32[]{:S(2)}) collective-permute-start(bf16[72,1152]{1,0:T(8,128)(2,1)S(1)} %collective-permute-done.2), channel_id=1, source_target_pairs={{0,2},{1,3},{2,4},{3,5},{4,6},{5,7},{6,8},{7,9},{8,10},{9,11},{10,... | collective-permute-start | bytes 497672 | tf_op jit(solution)/shard_map/ppermute | solution.py:301
  32.8 7.7 %collective-permute-start.5 = (bf16[72,1152]{1,0:T(8,128)(2,1)S(1)}, bf16[72,1152]{1,0:T(8,128)(2,1)S(1)}, u32[]{:S(2)}, u32[]{:S(2)}) collective-permute-start(bf16[72,1152]{1,0:T(8,128)(2,1)S(1)} %collective-permute-done.3), channel_id=1, source_target_pairs={{0,14},{1,15},{2,0},{3,1},{4,2},{5,3},{6,4},{7,5},{8,6},{9,7},{10,... | collective-permute-start | bytes 497672 | tf_op jit(solution)/shard_map/ppermute | solution.py:301
  38.5 7.7 %collective-permute-start.6 = (bf16[72,1152]{1,0:T(8,128)(2,1)S(1)}, bf16[72,1152]{1,0:T(8,128)(2,1)S(1)}, u32[]{:S(2)}, u32[]{:S(2)}) collective-permute-start(bf16[72,1152]{1,0:T(8,128)(2,1)S(1)} %collective-permute-done.4), channel_id=1, source_target_pairs={{0,2},{1,3},{2,4},{3,5},{4,6},{5,7},{6,8},{7,9},{8,10},{9,11},{10,... | collective-permute-start | bytes 497672 | tf_op jit(solution)/shard_map/ppermute | solution.py:301
  46.2 13.8 %copy-start = (bf16[8,72,1152]{2,1,0:T(8,128)(2,1)}, bf16[8,72,1152]{2,1,0:T(8,128)(2,1)S(1)}, u32[]{:S(2)}) copy-start(bf16[8,72,1152]{2,1,0:T(8,128)(2,1)S(1)} %bitcast_dynamic-update-slice_fusion.mine_w_ref) | copy-start | bytes 3981316
  46.2 9.6 %collective-permute-start.7 = (bf16[8,72,1152]{2,1,0:T(8,128)(2,1)S(1)}, bf16[8,72,1152]{2,1,0:T(8,128)(2,1)S(1)}, u32[]{:S(2)}, u32[]{:S(2)}) collective-permute-start(bf16[8,72,1152]{2,1,0:T(8,128)(2,1)S(1)} %bitcast_dynamic-update-slice_fusion.mine_w_ref), channel_id=1, source_target_pairs={{0,1},{1,0},{2,3},{3,2},{4,5},{5,4},{6,7},{7,6},{8,9},{9,8},{10,11... | collective-permute-start | bytes 3981320 | tf_op jit(solution)/shard_map/ppermute | solution.py:313
  51.9 3.9 %collective-permute-start.8 = (bf16[216,1152]{1,0:T(8,128)(2,1)S(1)}, bf16[216,1152]{1,0:T(8,128)(2,1)}, u32[]{:S(2)}, u32[]{:S(2)}) collective-permute-start(bf16[216,1152]{1,0:T(8,128)(2,1)S(1)} %bitcast.24), channel_id=1, source_target_pairs={{0,1},{1,0},{2,3},{3,2},{4,5},{5,4},{6,7},{7,6},{8,9},{9,8},{10,11... | collective-permute-start | bytes 1493000 | tf_op jit(solution)/shard_map/ppermute | solution.py:313
  55.8 1.1 copy-start.1
  60.0 14.9 %collective-permute-start.9 = (bf16[192,1152]{1,0:T(8,128)(2,1)}, bf16[192,1152]{1,0:T(8,128)(2,1)S(1)}, u32[]{:S(2)}, u32[]{:S(2)}) collective-permute-start(bf16[192,1152]{1,0:T(8,128)(2,1)} %unpack_rows.1.refs_0_), channel_id=1, source_target_pairs={{0,2},{1,3},{2,4},{3,5},{4,6},{5,7},{6,8},{7,9},{8,10},{9,11},{10,... | collective-permute-start | bytes 1327112 | tf_op jit(solution)/shard_map/ppermute | solution.py:301
  61.9 14.9 %collective-permute-start.10 = (bf16[192,1152]{1,0:T(8,128)(2,1)}, bf16[192,1152]{1,0:T(8,128)(2,1)S(1)}, u32[]{:S(2)}, u32[]{:S(2)}) collective-permute-start(bf16[192,1152]{1,0:T(8,128)(2,1)} %unpack_rows.1.refs_0_), channel_id=1, source_target_pairs={{0,14},{1,15},{2,0},{3,1},{4,2},{5,3},{6,4},{7,5},{8,6},{9,7},{10,... | collective-permute-start | bytes 1327112 | tf_op jit(solution)/shard_map/ppermute | solution.py:301
  74.9 33.3 %copy-start.9 = (bf16[192,1152]{1,0:T(8,128)(2,1)}, bf16[192,1152]{1,0:T(8,128)(2,1)S(1)}, u32[]{:S(2)}) copy-start(bf16[192,1152]{1,0:T(8,128)(2,1)S(1)} %collective-permute-done.9.refs_1_) | copy-start | bytes 1327108
  74.9 13.8 %collective-permute-start.11 = (bf16[192,1152]{1,0:T(8,128)(2,1)S(1)}, bf16[192,1152]{1,0:T(8,128)(2,1)S(1)}, u32[]{:S(2)}, u32[]{:S(2)}) collective-permute-start(bf16[192,1152]{1,0:T(8,128)(2,1)S(1)} %collective-permute-done.9.refs_1_), channel_id=1, source_target_pairs={{0,2},{1,3},{2,4},{3,5},{4,6},{5,7},{6,8},{7,9},{8,10},{9,11},{10,... | collective-permute-start | bytes 1327112 | tf_op jit(solution)/shard_map/ppermute | solution.py:301
  76.8 31.4 %copy-start.10 = (bf16[192,1152]{1,0:T(8,128)(2,1)}, bf16[192,1152]{1,0:T(8,128)(2,1)S(1)}, u32[]{:S(2)}) copy-start(bf16[192,1152]{1,0:T(8,128)(2,1)S(1)} %collective-permute-done.10.refs_2_) | copy-start | bytes 1327108
  76.8 13.8 %collective-permute-start.12 = (bf16[192,1152]{1,0:T(8,128)(2,1)S(1)}, bf16[192,1152]{1,0:T(8,128)(2,1)S(1)}, u32[]{:S(2)}, u32[]{:S(2)}) collective-permute-start(bf16[192,1152]{1,0:T(8,128)(2,1)S(1)} %collective-permute-done.10.refs_2_), channel_id=1, source_target_pairs={{0,14},{1,15},{2,0},{3,1},{4,2},{5,3},{6,4},{7,5},{8,6},{9,7},{10,... | collective-permute-start | bytes 1327112 | tf_op jit(solution)/shard_map/ppermute | solution.py:301
  88.7 19.5 %copy-start.11 = (bf16[192,1152]{1,0:T(8,128)(2,1)}, bf16[192,1152]{1,0:T(8,128)(2,1)S(1)}, u32[]{:S(2)}) copy-start(bf16[192,1152]{1,0:T(8,128)(2,1)S(1)} %collective-permute-done.11.refs_3_) | copy-start | bytes 1327108
  88.7 12.9 %collective-permute-start.13 = (bf16[192,1152]{1,0:T(8,128)(2,1)S(1)}, bf16[192,1152]{1,0:T(8,128)(2,1)S(1)}, u32[]{:S(2)}, u32[]{:S(2)}) collective-permute-start(bf16[192,1152]{1,0:T(8,128)(2,1)S(1)} %collective-permute-done.11.refs_3_), channel_id=1, source_target_pairs={{0,2},{1,3},{2,4},{3,5},{4,6},{5,7},{6,8},{7,9},{8,10},{9,11},{10,... | collective-permute-start | bytes 1327112 | tf_op jit(solution)/shard_map/ppermute | solution.py:301
  90.6 17.6 %copy-start.12 = (bf16[192,1152]{1,0:T(8,128)(2,1)}, bf16[192,1152]{1,0:T(8,128)(2,1)S(1)}, u32[]{:S(2)}) copy-start(bf16[192,1152]{1,0:T(8,128)(2,1)S(1)} %collective-permute-done.12.refs_4_) | copy-start | bytes 1327108
  90.7 12.9 %collective-permute-start.14 = (bf16[192,1152]{1,0:T(8,128)(2,1)S(1)}, bf16[192,1152]{1,0:T(8,128)(2,1)S(1)}, u32[]{:S(2)}, u32[]{:S(2)}) collective-permute-start(bf16[192,1152]{1,0:T(8,128)(2,1)S(1)} %collective-permute-done.12.refs_4_), channel_id=1, source_target_pairs={{0,14},{1,15},{2,0},{3,1},{4,2},{5,3},{6,4},{7,5},{8,6},{9,7},{10,... | collective-permute-start | bytes 1327112 | tf_op jit(solution)/shard_map/ppermute | solution.py:301
  101.6 10.9 %copy-start.2 = (bf16[192,1152]{1,0:T(8,128)(2,1)}, bf16[192,1152]{1,0:T(8,128)(2,1)S(1)}, u32[]{:S(2)}) copy-start(bf16[192,1152]{1,0:T(8,128)(2,1)S(1)} %collective-permute-done.13.refs_0_) | copy-start | bytes 1327108
  101.6 16.1 %collective-permute-start.15 = (bf16[96,1152]{1,0:T(8,128)(2,1)S(1)}, bf16[96,1152]{1,0:T(8,128)(2,1)S(1)}, u32[]{:S(2)}, u32[]{:S(2)}) collective-permute-start(bf16[96,1152]{1,0:T(8,128)(2,1)S(1)} %slice.8), channel_id=1, source_target_pairs={{0,2},{1,3},{2,4},{3,5},{4,6},{5,7},{6,8},{7,9},{8,10},{9,11},{10,... | collective-permute-start | bytes 663560 | tf_op jit(solution)/shard_map/ppermute | solution.py:301
  103.6 8.9 %copy-start.3 = (bf16[192,1152]{1,0:T(8,128)(2,1)}, bf16[192,1152]{1,0:T(8,128)(2,1)S(1)}, u32[]{:S(2)}) copy-start(bf16[192,1152]{1,0:T(8,128)(2,1)S(1)} %collective-permute-done.14.refs_1_) | copy-start | bytes 1327108
  103.6 14.2 %collective-permute-start.16 = (bf16[96,1152]{1,0:T(8,128)(2,1)S(1)}, bf16[96,1152]{1,0:T(8,128)(2,1)S(1)}, u32[]{:S(2)}, u32[]{:S(2)}) collective-permute-start(bf16[96,1152]{1,0:T(8,128)(2,1)S(1)} %slice.9), channel_id=1, source_target_pairs={{0,14},{1,15},{2,0},{3,1},{4,2},{5,3},{6,4},{7,5},{8,6},{9,7},{10,... | collective-permute-start | bytes 663560 | tf_op jit(solution)/shard_map/ppermute | solution.py:301
  112.5 11.9 %collective-permute-start.17 = (bf16[5,192,256]{2,1,0:T(8,128)(2,1)}, bf16[5,192,256]{2,1,0:T(8,128)(2,1)S(1)}, u32[]{:S(2)}, u32[]{:S(2)}) collective-permute-start(bf16[5,192,256]{2,1,0:T(8,128)(2,1)} %get-tuple-element.11), channel_id=1, source_target_pairs={{0,1},{1,0},{2,3},{3,2},{4,5},{5,4},{6,7},{7,6},{8,9},{9,8},{10,11... | collective-permute-start | bytes 1474568 | tf_op jit(solution)/shard_map/ppermute | solution.py:313
  117.8 0.7 copy-start.5
  118.4 0.7 copy-start.6
  122.5 3.7 %collective-permute-start.18 = (bf16[3,192,256]{2,1,0:T(8,128)(2,1)}, bf16[3,192,256]{2,1,0:T(8,128)(2,1)S(1)}, u32[]{:S(2)}, u32[]{:S(2)}) collective-permute-start(bf16[3,192,256]{2,1,0:T(8,128)(2,1)} %get-tuple-element.12), channel_id=1, source_target_pairs={{0,1},{1,0},{2,3},{3,2},{4,5},{5,4},{6,7},{7,6},{8,9},{9,8},{10,11... | collective-permute-start | bytes 884744 | tf_op jit(solution)/shard_map/ppermute | solution.py:313
  124.4 1.7 %copy-start.8 = (bf16[5,192,256]{2,1,0:T(8,128)(2,1)}, bf16[5,192,256]{2,1,0:T(8,128)(2,1)S(1)}, u32[]{:S(2)}) copy-start(bf16[5,192,256]{2,1,0:T(8,128)(2,1)S(1)} %collective-permute-done.17.refs_2_) | copy-start | bytes 1474564
  126.2 0.7 copy-start.13

commit v5 on v3

--- a/solution.py
+++ b/solution.py
@@ -64,8 +64,8 @@
         out_ref[:, tile * 16 : (tile + 1) * 16, :] = whole.astype(BF).reshape(n_pack, 16, LANES)
 
 
-def unpack_kernel(n_pack, in_ref, out_ref):
-    tok = out_ref.shape[0]
+def unpack_kernel(n_pack, in_ref, w_ref, out_ref):
+    tok = TOK
     group = n_pack * 16
     tiles = [in_ref[:, t * 16 : (t + 1) * 16, :].reshape(group, LANES) for t in range(TILES)]
     col = iota((n_pack, group), 1)
@@ -84,10 +84,15 @@
             parts.setdefault(f, []).append(moved[:, n * LANES : (n + 1) * LANES])
     for f in sorted(parts):
         whole = functools.reduce(lambda a, b: a + b, parts[f])
-        out_ref[:, f * LANES : (f + 1) * LANES] = whole.astype(BF)
-
-
-TOKT = 1024
+        out_ref[0:tok, f * LANES : (f + 1) * LANES] = whole.astype(BF)
+    out_ref[tok : tok + 64, :] = w_ref[0:64, :]
+    last = w_ref[64:HD, :].astype(F32)
+    out_ref[tok + 64 : tok + WROWS, :] = jnp.concatenate([last, last], axis=0).astype(BF)
+
+
+TOK = 192
+WROWS = 80
+STEP = 4
 QT = 256
 KT = 1024
 SIDE = 1
@@ -99,13 +104,15 @@
 
 def attend_kernel(steps, n_seq, doc_ref, x_ref, w_ref, out_ref, q_s, k_s, v_s, o_s, bound_s):
     step = pl.program_id(0)
-    start = pl.multiple_of(step * TOKT, TOKT)
-    qkv = lax.dot_general(x_ref[...], w_ref[...], NT, preferred_element_type=F32)
-    q_s[pl.ds(start, TOKT), :] = (qkv[:, 0:HD] * (1.0 / math.sqrt(HD))).astype(BF)
-    k_s[pl.ds(start, TOKT), :] = qkv[:, HD : 2 * HD].astype(BF)
+    count = STEP * TOK
+    start = pl.multiple_of(step * count, count)
+    x = x_ref[...].reshape(count, x_ref.shape[2])
+    qkv = lax.dot_general(x, w_ref[...], NT, preferred_element_type=F32)
+    q_s[pl.ds(start, count), :] = (qkv[:, 0:HD] * (1.0 / math.sqrt(HD))).astype(BF)
+    k_s[pl.ds(start, count), :] = qkv[:, HD : 2 * HD].astype(BF)
     turned = qkv[:, LANES : 3 * HD].T[2 * HD - LANES :, :]
-    ones = jnp.ones((VROWS - HD, TOKT), F32)
-    v_s[:, pl.ds(start, TOKT)] = jnp.concatenate([turned, ones], axis=0).astype(BF)
+    ones = jnp.ones((VROWS - HD, count), F32)
+    v_s[:, pl.ds(start, count)] = jnp.concatenate([turned, ones], axis=0).astype(BF)
 
     @pl.when(step == steps - 1)
     def _():
@@ -186,30 +193,26 @@
             ).astype(BF)
 
 
-def project_kernel(n_seq, in_ref, w_ref, out_ref):
+def project_kernel(n_seq, in_ref, *refs):
+    *w_refs, out_ref = refs
     width = out_ref.shape[1]
     tok = out_ref.shape[0]
     rest = tok - LANES
-    lo = in_ref[:, 0:32, :].reshape(n_seq * 32, LANES)
-    hi = in_ref[:, 32:64, :].reshape(n_seq * 32, LANES)
-    far = in_ref[:, 64:96, :].reshape(n_seq * 32, LANES)
-    tail = in_ref[:, 96:112, :].reshape(n_seq * 16, LANES).astype(F32)
+
+    def features(begin):
+        return in_ref[:, begin : begin + 16, :].reshape(n_seq * 16, LANES)
+
+    tail = features(96).astype(F32)
     upper = (iota(tail.shape, 0) & 15) < 8
     tail_near = jnp.where(upper, tail, 0.0).astype(BF)
     tail_far = jnp.where(upper, 0.0, tail).astype(BF)
-    near = jnp.concatenate([lo, hi, tail_near], axis=0).T
-    far_t = far.T
-    distant = jnp.concatenate([far_t[0:rest], far_t[rest:LANES], tail_far.T[0:rest]], axis=1)
+    near = jnp.concatenate([features(16 * g) for g in range(4)] + [tail_near], axis=0).T
+    first, second = features(64).T, features(80).T
+    distant = jnp.concatenate(
+        [first[0:rest], second[0:rest], first[rest:], second[rest:], tail_far.T[0:rest]], axis=1
+    )
     left = jnp.concatenate([near, distant], axis=0)
-    last = w_ref[:, 64:HD, :].astype(F32)
-    weights = jnp.concatenate(
-        [
-            w_ref[:, 0:32, :].reshape(n_seq * 32, width),
-            w_ref[:, 32:64, :].reshape(n_seq * 32, width),
-            jnp.concatenate([last, last], axis=1).reshape(n_seq * 16, width).astype(BF),
-        ],
-        axis=0,
-    )
+    weights = jnp.concatenate([ref[...].reshape(n_seq * 16, width) for ref in w_refs], axis=0)
     out_ref[...] = jnp.dot(left, weights, preferred_element_type=F32).astype(BF)
 
 
@@ -218,15 +221,16 @@
 
 
 def attend_call(doc_ids, tokens, w_t, n_seq):
-    length, width = tokens.shape
-    steps = length // TOKT
+    length = n_seq * TOK
+    width = tokens.shape[2]
+    steps = n_seq // STEP
     return pl.pallas_call(
         functools.partial(attend_kernel, steps, n_seq),
         grid=(steps,),
         out_shape=jax.ShapeDtypeStruct((n_seq, AROWS, LANES), BF),
         in_specs=[
             pl.BlockSpec(memory_space=pltpu.SMEM),
-            pl.BlockSpec((TOKT, width), lambda i: (i, 0)),
+            pl.BlockSpec((STEP, TOK, width), lambda i: (i, 0, 0)),
             whole(*w_t.shape),
         ],
         out_specs=whole(n_seq, AROWS, LANES),
@@ -246,8 +250,6 @@
     n_pack = lax.axis_size("pack")
     n_seq = lax.axis_size("seq")
     tok, width = source.shape[1:]
-    w_all = lax.all_gather(w_out, "seq", axis=0, tiled=False)
-
     outbox = pl.pallas_call(
         functools.partial(pack_kernel, n_pack),
         out_shape=jax.ShapeDtypeStruct((n_pack, TILES * 16, LANES), BF),
@@ -257,24 +259,30 @@
     inbox = lax.all_to_all(outbox, "pack", split_axis=0, concat_axis=0, tiled=True)
     packed = pl.pallas_call(
         functools.partial(unpack_kernel, n_pack),
-        out_shape=jax.ShapeDtypeStruct((tok, width), BF),
+        out_shape=jax.ShapeDtypeStruct((tok + WROWS, width), BF),
         compiler_params=LIMIT,
         name="unpack_rows",
-    )(inbox)
-    packed, w_all = lax.optimization_barrier((packed, w_all))
-    tokens = lax.all_gather(packed, "seq", axis=0, tiled=True)
+    )(inbox, w_out)
+    tokens = lax.all_gather(packed, "seq", axis=0, tiled=False)
 
     attended = attend_call(
         doc_ids, tokens, jnp.transpose(w_qkv, (0, 2, 1)).reshape(3 * HD, width), n_seq
     )
     blocks = lax.all_to_all(attended, "seq", split_axis=0, concat_axis=0, tiled=True)
 
+    def w_spec(group):
+        return pl.BlockSpec((n_seq, 16, width), lambda i: (0, tok // 16 + group, 0))
+
+    groups = WROWS // 16
     out = pl.pallas_call(
         functools.partial(project_kernel, n_seq),
+        grid=(1,),
         out_shape=jax.ShapeDtypeStruct((tok, width), BF),
+        in_specs=[whole(*blocks.shape)] + [w_spec(g) for g in range(groups)],
+        out_specs=whole(tok, width),
         compiler_params=LIMIT,
         name="project",
-    )(blocks, w_all)
+    )(blocks, *[tokens] * groups)
     return out[None]
 
 

time: 163 us -> 174 us (1.067)
  the two profiles are of different devices: /device:TPU:7 before, /device:TPU:65 now
where the time goes in v5:
time: 174 us; the launch traced here: 173 us
  waiting for transfers between devices  65.2 us (37%)
  blocking collectives  57 us (33%)
  Pallas kernels  37.8 us (22%)
  between operations  13.4 us (8%)
    all_gather x1, waiting for transfers between devices, body(): tokens = lax.all_gather(packed, 'seq', axis=0, tiled=False)  65.2 us
    all_to_all x1, blocking collectives, body(): lax.all_to_all(outbox, 'pack', split_axis=0, concat_axis=0, tiled=True)  36.3 us
    pallas_call x1, Pallas kernels, attend_call(): pl.pallas_call(functools.partial(attend_kernel, steps, n_seq), grid=(step...  28.3 us
    all_to_all x1, blocking collectives, body(): lax.all_to_all(attended, 'seq', split_axis=0, concat_axis=0, tiled=True)  20.8 us
    pallas_call x1, Pallas kernels, body(): pl.pallas_call(functools.partial(project_kernel, n_seq), grid=(1,), out_s...  3.52 us
  transfers between devices with their start and end apart: 1, of which 1 were waited for; matrix products, arithmetic and copies ran while one was open for 0% of the time, Pallas kernels for 0%

profile of v5, /device:TPU:65, one launch (start us, length us, event | category | flops | bytes accessed | tf_op | source)
XLA Modules:
  0.0 173.5 jit_solution(4167814791392080633)
XLA Ops:
  6.5 0.0 all-gather.3.cloned.1.call-start
  6.5 2.8 %pack_rows.1 = bf16[32,112,128]{2,1,0:T(8,128)(2,1)} custom-call(s32[1,192]{1,0:T(1,128)} %dest_ref.1, bf16[192,1152]{1,0:T(8,128)(2,1)} %bitcast.13), custom_call_target="tpu_custom_call" | custom-call | tf_op jit(solution)/shard_map/pack_rows/pallas_call | solution.py:253
  9.4 36.3 %all_to_all.10.in_ref = bf16[32,112,128]{2,1,0:T(8,128)(2,1)} all-to-all(bf16[32,112,128]{2,1,0:T(8,128)(2,1)} %pack_rows.1), channel_id=1, replica_groups=mesh['pack'=32,'seq'=16] {'pack'}, dimensions={0} | all-to-all | bytes 1835008 | tf_op jit(solution)/shard_map/all_to_all | solution.py:259
  45.6 3.1 %unpack_rows.1 = bf16[272,1152]{1,0:T(8,128)(2,1)} custom-call(bf16[32,112,128]{2,1,0:T(8,128)(2,1)} %all_to_all.10.in_ref, bf16[72,1152]{1,0:T(8,128)(2,1)} %w_ref.1), custom_call_target="tpu_custom_call" | custom-call | tf_op jit(solution)/shard_map/unpack_rows/pallas_call | solution.py:260
  48.8 0.0 all-gather.3.cloned.1.call-update
  48.8 65.2 %all-gather.3.cloned.1.call-done = bf16[4352,1152]{1,0:T(8,128)(2,1)} async-done(((bf16[272,1152]{1,0:T(8,128)(2,1)}), bf16[4352,1152]{1,0:T(8,128)(2,1)}) %all-gather.3.cloned.1.call-update) | async-done | bytes 10027024 | tf_op jit(solution)/shard_map/all_gather | solution.py:266
  114.0 28.3 %attend.1 = bf16[16,112,128]{2,1,0:T(8,128)(2,1)} custom-call(s32[1,3072]{1,0:T(1,128)} %doc_ref.1, bf16[16,272,1152]{2,1,0:T(8,128)(2,1)} %bitcast.6, bf16[216,1152]{1,0:T(8,128)(2,1)} %bitcast.12), custom_call_target="tpu_custom_call" | custom-call | tf_op jit(solution)/shard_map/attend/pallas_call | solution.py:227
  142.3 20.8 %all_to_all.11.in_ref = bf16[16,112,128]{2,1,0:T(8,128)(2,1)} all-to-all(bf16[16,112,128]{2,1,0:T(8,128)(2,1)} %attend.1), channel_id=1, replica_groups=mesh['pack'=32,'seq'=16] {'seq'}, dimensions={0} | all-to-all | bytes 917504 | tf_op jit(solution)/shard_map/all_to_all | solution.py:271
  163.1 3.5 %project.1 = bf16[192,1152]{1,0:T(8,128)(2,1)} custom-call(bf16[16,112,128]{2,1,0:T(8,128)(2,1)} %all_to_all.11.in_ref, bf16[16,272,1152]{2,1,0:T(8,128)(2,1)} %bitcast.7, bf16[16,272,1152]{2,1,0:T(8,128)(2,1)} %bitcast.8, bf16[16,272,1152]{2,1,0:T(8,128)(2,1)} %bitcast.9, bf16[16,272,1152]{2,1,0:T(8,128)(2,1)} %bitcast.10, bf16[16,272,1152]{2,1,0:T(8,128)(2,1)} %bitcast.11), custom_call_target="tpu_custom_call" | custom-call | tf_op jit(solution)/shard_map/project/pallas_call | solution.py:277
Async XLA Ops:
  6.5 107.5 %all-gather.3.cloned.1.call-start = ((), (), s32[]{:S(2)}) async-start(), calls=%async_computation.2 | async-start | bytes 10653696 | tf_op jit(solution)/shard_map/all_gather | solution.py:266
Sparse Core Ops, SparseCore 0:
  48.9 65.0 all-gather.2

commit v6 on v4

--- a/solution.py
+++ b/solution.py
@@ -89,7 +89,7 @@
 
 
 TOK = 192
-QT = 256
+QT = 768
 KT = 1024
 SIDE = 1
 VROWS = 80
@@ -210,20 +210,14 @@
         ).astype(BF)
 
 
-def project_kernel(n_seq, me_ref, in_ref, mine_w_ref, pair_w_ref, out_ref):
+def project_kernel(n_seq, in_ref, w_ref, out_ref):
     width = out_ref.shape[1]
     tok = out_ref.shape[0]
     rest = tok - LANES
-    half = n_seq // 2
-    came = [origin(me_ref[0], n) for n in range(n_seq)]
-
-    def features(begin, end):
-        return jnp.concatenate([in_ref[s, begin:end, :] for s in came], axis=0)
-
-    lo = features(0, 32)
-    hi = features(32, 64)
-    far = features(64, 96)
-    tail = features(96, 112).astype(F32)
+    lo = in_ref[:, 0:32, :].reshape(n_seq * 32, LANES)
+    hi = in_ref[:, 32:64, :].reshape(n_seq * 32, LANES)
+    far = in_ref[:, 64:96, :].reshape(n_seq * 32, LANES)
+    tail = in_ref[:, 96:112, :].reshape(n_seq * 16, LANES).astype(F32)
     upper = (iota(tail.shape, 0) & 15) < 8
     tail_near = jnp.where(upper, tail, 0.0).astype(BF)
     tail_far = jnp.where(upper, 0.0, tail).astype(BF)
@@ -231,14 +225,15 @@
     far_t = far.T
     distant = jnp.concatenate([far_t[0:rest], far_t[rest:LANES], tail_far.T[0:rest]], axis=1)
     left = jnp.concatenate([near, distant], axis=0)
-    weights = []
-    for begin in (0, 32):
-        for ref in (mine_w_ref, pair_w_ref):
-            weights.append(ref[:, begin : begin + 32, :].reshape(half * 32, width))
-    for ref in (mine_w_ref, pair_w_ref):
-        last = ref[:, 64:HD, :].astype(F32)
-        weights.append(jnp.concatenate([last, last], axis=1).reshape(half * 16, width).astype(BF))
-    weights = jnp.concatenate(weights, axis=0)
+    last = w_ref[:, 64:HD, :].astype(F32)
+    weights = jnp.concatenate(
+        [
+            w_ref[:, 0:32, :].reshape(n_seq * 32, width),
+            w_ref[:, 32:64, :].reshape(n_seq * 32, width),
+            jnp.concatenate([last, last], axis=1).reshape(n_seq * 16, width).astype(BF),
+        ],
+        axis=0,
+    )
     out_ref[...] = jnp.dot(left, weights, preferred_element_type=F32).astype(BF)
 
 
@@ -323,14 +318,7 @@
     inbox = lax.all_to_all(outbox, "pack", split_axis=0, concat_axis=0, tiled=True)
 
     pair_w = other_core(w_t)
-    right = left = w_out
-    held = [w_out]
-    for _ in range(3):
-        right, left = ring_step(right, left, n_seq)
-        held += [right, left]
-    held.append(ring_step(right, left, n_seq)[0])
-    w_mine = jnp.stack(held)
-    w_pair = other_core(w_mine)
+    w_all = lax.all_gather(w_out, "seq", axis=0, tiled=False)
 
     packed = local_call(
         functools.partial(unpack_kernel, n_pack),
@@ -338,7 +326,7 @@
         inbox,
         name="unpack_rows",
         flops=10**9,
-        behind=(w_pair, pair_w),
+        behind=(pair_w,),
     )
     right = left = packed
     held = [packed]
@@ -347,23 +335,21 @@
         held += [right, left]
     held += ring_step(right[: TOK // 2], left[TOK // 2 :], n_seq)
 
-    mine_a, theirs_a = project_qkv(held[:5], w_t, pair_w, "qkv_first")
-    mine_b, theirs_b = project_qkv(held[5:], w_t, pair_w, "qkv_last")
-    attended = attend_call(
-        me, doc_ids, n_seq, mine_a, mine_b, other_core(theirs_a), other_core(theirs_b)
-    )
+    mine, theirs = [], []
+    for n, (begin, end) in enumerate(((0, 5), (5, 9))):
+        own, other = project_qkv(held[begin:end], w_t, pair_w, f"qkv_{n}")
+        mine.append(own)
+        theirs.append(other_core(other))
+    attended = attend_call(me, doc_ids, n_seq, *mine, *theirs)
     blocks = lax.all_to_all(attended, "seq", split_axis=0, concat_axis=0, tiled=True)
 
     out = local_call(
         functools.partial(project_kernel, n_seq),
         shape((TOK, width), BF),
-        me,
         blocks,
-        w_mine,
-        w_pair,
+        w_all,
         name="project",
         flops=2 * TOK * width * width,
-        small=1,
     )
     return out[None]
 

time: 171 us -> 169 us (0.988)
  the two profiles are of different devices: /device:TPU:7 before, /device:TPU:135 now
where the time goes in v6:
time: 169 us; the launch traced here: 168 us
  starting transfers between devices  48 us (28%)
  waiting for transfers between devices  45 us (27%)
  Pallas kernels  35.9 us (21%)
  blocking collectives  22.2 us (13%)
  between operations  13.7 us (8%)
  local copies, waits for them, and re-layouts  3.08 us (2%)
    pallas_call x6, Pallas kernels, local_call(): pl.pallas_call(kernel, out_shape=out_shape, in_specs=[smem] * small + [vm...  35.9 us
    ppermute x8, starting transfers between devices, ring_step(): return (lax.ppermute(right, 'seq', up), lax.ppermute(left, 'seq', down))  26.4 us
    all_to_all x1, blocking collectives, body(): lax.all_to_all(attended, 'seq', split_axis=0, concat_axis=0, tiled=True)  22.2 us
    ppermute x8, waiting for transfers between devices, ring_step(): return (lax.ppermute(right, 'seq', up), lax.ppermute(left, 'seq', down))  21.7 us
    all_to_all x1, waiting for transfers between devices, body(): lax.all_to_all(outbox, 'pack', split_axis=0, concat_axis=0, tiled=True)  19.4 us
    all_to_all x1, starting transfers between devices, body(): lax.all_to_all(outbox, 'pack', split_axis=0, concat_axis=0, tiled=True)  11.1 us
    ppermute x3, starting transfers between devices, other_core(): return lax.ppermute(x, 'seq', [(i, i ^ 1) for i in range(n_seq)])  10.5 us
  transfers between devices with their start and end apart: 13, of which 6 were waited for; matrix products, arithmetic and copies ran while one was open for 0% of the time, Pallas kernels for 19%

profile of v6, /device:TPU:135, one launch (start us, length us, event | category | flops | bytes accessed | tf_op | source)
XLA Modules:
  0.0 167.8 jit_solution(12053497126719824708)
XLA Ops:
  6.5 0.0 all-gather.3.cloned.1.call-start
  6.5 0.7 all-gather.3.cloned.1.call-update
  7.3 0.0 copy-start.3
  7.3 2.9 %pack_rows.1 = bf16[32,112,128]{2,1,0:T(8,128)(2,1)} custom-call(s32[1,192]{1,0:T(1,128)} %dest_ref.1, bf16[192,1152]{1,0:T(8,128)(2,1)} %bitcast.11), custom_call_target="tpu_custom_call" | custom-call | flops 1000000000 | bytes 1360640 | tf_op jit(solution)/shard_map/pack_rows/pallas_call | solution.py:250
  10.1 11.1 %all-to-all-start = ((bf16[32,112,128]{2,1,0:T(8,128)(2,1)}), bf16[32,112,128]{2,1,0:T(8,128)(2,1)S(1)}, u32[]{:S(2)}, u32[]{:S(2)}) async-start(bf16[32,112,128]{2,1,0:T(8,128)(2,1)} %pack_rows.1), calls=%async_computation | async-start | bytes 1835008 | tf_op jit(solution)/shard_map/all_to_all | solution.py:318
  21.2 0.0 copy-done.3
  21.2 3.1 %collective-permute-start = (bf16[216,1152]{1,0:T(8,128)(2,1)S(1)}, bf16[216,1152]{1,0:T(8,128)(2,1)S(1)}, u32[]{:S(2)}, u32[]{:S(2)}) collective-permute-start(bf16[216,1152]{1,0:T(8,128)(2,1)S(1)} %bitcast.10), channel_id=1, source_target_pairs={{0,1},{1,0},{2,3},{3,2},{4,5},{5,4},{6,7},{7,6},{8,9},{9,8},{10,11... | collective-permute-start | bytes 1493000 | tf_op jit(solution)/shard_map/ppermute | solution.py:308
  24.4 1.5 collective-permute-done.refs_0_.refs_6_.refs_5_
  25.9 19.4 %all-to-all-done.in_ref = bf16[32,112,128]{2,1,0:T(8,128)(2,1)S(1)} async-done(((bf16[32,112,128]{2,1,0:T(8,128)(2,1)}), bf16[32,112,128]{2,1,0:T(8,128)(2,1)S(1)}, u32[]{:S(2)}, u32[]{:S(2)}) %all-to-all-start) | async-done | bytes 917536 | tf_op jit(solution)/shard_map/all_to_all | solution.py:318
  45.3 0.0 copy-done.4
  45.3 0.9 copy-done.2
  46.2 3.1 %unpack_rows.1.refs_0_ = bf16[192,1152]{1,0:T(8,128)(2,1)} custom-call(bf16[32,112,128]{2,1,0:T(8,128)(2,1)} %copy-done.2, bf16[216,1152]{1,0:T(8,128)(2,1)} %copy-done.4), custom_call_target="tpu_custom_call" | custom-call | flops 1000000000 | bytes 1359872 | tf_op jit(solution)/shard_map/unpack_rows/pallas_call | solution.py:250
  49.3 3.2 %collective-permute-start.1 = (bf16[192,1152]{1,0:T(8,128)(2,1)}, bf16[192,1152]{1,0:T(8,128)(2,1)S(1)}, u32[]{:S(2)}, u32[]{:S(2)}) collective-permute-start(bf16[192,1152]{1,0:T(8,128)(2,1)} %unpack_rows.1.refs_0_), channel_id=1, source_target_pairs={{0,2},{1,3},{2,4},{3,5},{4,6},{5,7},{6,8},{7,9},{8,10},{9,11},{10,... | collective-permute-start | bytes 1327112 | tf_op jit(solution)/shard_map/ppermute | solution.py:296
  52.5 3.8 %collective-permute-start.2 = (bf16[192,1152]{1,0:T(8,128)(2,1)}, bf16[192,1152]{1,0:T(8,128)(2,1)S(1)}, u32[]{:S(2)}, u32[]{:S(2)}) collective-permute-start(bf16[192,1152]{1,0:T(8,128)(2,1)} %unpack_rows.1.refs_0_), channel_id=1, source_target_pairs={{0,14},{1,15},{2,0},{3,1},{4,2},{5,3},{6,4},{7,5},{8,6},{9,7},{10,... | collective-permute-start | bytes 1327112 | tf_op jit(solution)/shard_map/ppermute | solution.py:296
  56.3 8.3 %collective-permute-done.1.refs_1_ = bf16[192,1152]{1,0:T(8,128)(2,1)S(1)} collective-permute-done((bf16[192,1152]{1,0:T(8,128)(2,1)}, bf16[192,1152]{1,0:T(8,128)(2,1)S(1)}, u32[]{:S(2)}, u32[]{:S(2)}) %collective-permute-start.1) | collective-permute-done | bytes 442400 | tf_op jit(solution)/shard_map/ppermute | solution.py:296
  64.6 1.9 %collective-permute-start.3 = (bf16[192,1152]{1,0:T(8,128)(2,1)S(1)}, bf16[192,1152]{1,0:T(8,128)(2,1)S(1)}, u32[]{:S(2)}, u32[]{:S(2)}) collective-permute-start(bf16[192,1152]{1,0:T(8,128)(2,1)S(1)} %collective-permute-done.1.refs_1_), channel_id=1, source_target_pairs={{0,2},{1,3},{2,4},{3,5},{4,6},{5,7},{6,8},{7,9},{8,10},{9,11},{10,... | collective-permute-start | bytes 1327112 | tf_op jit(solution)/shard_map/ppermute | solution.py:296
  66.5 0.0 collective-permute-done.2.refs_2_
  66.5 0.0 copy-start.9
  66.6 4.6 %collective-permute-start.4 = (bf16[192,1152]{1,0:T(8,128)(2,1)S(1)}, bf16[192,1152]{1,0:T(8,128)(2,1)S(1)}, u32[]{:S(2)}, u32[]{:S(2)}) collective-permute-start(bf16[192,1152]{1,0:T(8,128)(2,1)S(1)} %collective-permute-done.2.refs_2_), channel_id=1, source_target_pairs={{0,14},{1,15},{2,0},{3,1},{4,2},{5,3},{6,4},{7,5},{8,6},{9,7},{10,... | collective-permute-start | bytes 1327112 | tf_op jit(solution)/shard_map/ppermute | solution.py:296
  71.1 7.2 %collective-permute-done.3.refs_3_ = bf16[192,1152]{1,0:T(8,128)(2,1)S(1)} collective-permute-done((bf16[192,1152]{1,0:T(8,128)(2,1)S(1)}, bf16[192,1152]{1,0:T(8,128)(2,1)S(1)}, u32[]{:S(2)}, u32[]{:S(2)}) %collective-permute-start.3) | collective-permute-done | bytes 442400 | tf_op jit(solution)/shard_map/ppermute | solution.py:296
  78.3 1.9 %collective-permute-start.5 = (bf16[192,1152]{1,0:T(8,128)(2,1)S(1)}, bf16[192,1152]{1,0:T(8,128)(2,1)S(1)}, u32[]{:S(2)}, u32[]{:S(2)}) collective-permute-start(bf16[192,1152]{1,0:T(8,128)(2,1)S(1)} %collective-permute-done.3.refs_3_), channel_id=1, source_target_pairs={{0,2},{1,3},{2,4},{3,5},{4,6},{5,7},{6,8},{7,9},{8,10},{9,11},{10,... | collective-permute-start | bytes 1327112 | tf_op jit(solution)/shard_map/ppermute | solution.py:296
  80.2 0.0 collective-permute-done.4.refs_4_
  80.2 0.0 copy-start.11
  80.2 4.6 %collective-permute-start.6 = (bf16[192,1152]{1,0:T(8,128)(2,1)S(1)}, bf16[192,1152]{1,0:T(8,128)(2,1)S(1)}, u32[]{:S(2)}, u32[]{:S(2)}) collective-permute-start(bf16[192,1152]{1,0:T(8,128)(2,1)S(1)} %collective-permute-done.4.refs_4_), channel_id=1, source_target_pairs={{0,14},{1,15},{2,0},{3,1},{4,2},{5,3},{6,4},{7,5},{8,6},{9,7},{10,... | collective-permute-start | bytes 1327112 | tf_op jit(solution)/shard_map/ppermute | solution.py:296
  84.8 6.2 %collective-permute-done.5.refs_0_ = bf16[192,1152]{1,0:T(8,128)(2,1)S(1)} collective-permute-done((bf16[192,1152]{1,0:T(8,128)(2,1)S(1)}, bf16[192,1152]{1,0:T(8,128)(2,1)S(1)}, u32[]{:S(2)}, u32[]{:S(2)}) %collective-permute-start.5) | collective-permute-done | bytes 442400 | tf_op jit(solution)/shard_map/ppermute | solution.py:296
  91.1 1.9 %collective-permute-start.7 = (bf16[96,1152]{1,0:T(8,128)(2,1)S(1)}, bf16[96,1152]{1,0:T(8,128)(2,1)S(1)}, u32[]{:S(2)}, u32[]{:S(2)}) collective-permute-start(bf16[96,1152]{1,0:T(8,128)(2,1)S(1)} %slice.8), channel_id=1, source_target_pairs={{0,2},{1,3},{2,4},{3,5},{4,6},{5,7},{6,8},{7,9},{8,10},{9,11},{10,... | collective-permute-start | bytes 663560 | tf_op jit(solution)/shard_map/ppermute | solution.py:296
  93.0 0.0 collective-permute-done.6.refs_1_
  93.0 0.0 copy-start.1
  93.0 4.6 %collective-permute-start.8 = (bf16[96,1152]{1,0:T(8,128)(2,1)S(1)}, bf16[96,1152]{1,0:T(8,128)(2,1)S(1)}, u32[]{:S(2)}, u32[]{:S(2)}) collective-permute-start(bf16[96,1152]{1,0:T(8,128)(2,1)S(1)} %slice.9), channel_id=1, source_target_pairs={{0,14},{1,15},{2,0},{3,1},{4,2},{5,3},{6,4},{7,5},{8,6},{9,7},{10,... | collective-permute-start | bytes 663560 | tf_op jit(solution)/shard_map/ppermute | solution.py:296
  97.6 0.0 copy-done.8
  97.6 0.0 copy-done.9
  97.6 0.0 copy-done.10
  97.6 0.0 copy-done.11
  97.7 4.2 %qkv_0.1 = (bf16[5,192,256]{2,1,0:T(8,128)(2,1)}, bf16[5,192,256]{2,1,0:T(8,128)(2,1)}) custom-call(bf16[192,1152]{1,0:T(8,128)(2,1)} %unpack_rows.1.refs_0_, bf16[192,1152]{1,0:T(8,128)(2,1)} %copy-done.8, bf16[192,1152]{1,0:T(8,128)(2,1)} %copy-done.9, bf16[192,1152]{1,0:T(8,128)(2,1)} %copy-done.10, bf16[192,1152]{1,0:T(8,128)(2,1)} %copy-done.11, ...), custom_call_target="tpu_custom_call" | custom-call | flops 955514880 | bytes 4190208 | tf_op jit(solution)/shard_map/qkv_0/pallas_call | solution.py:250
  101.9 5.4 %collective-permute-start.9 = (bf16[5,192,256]{2,1,0:T(8,128)(2,1)}, bf16[5,192,256]{2,1,0:T(8,128)(2,1)S(1)}, u32[]{:S(2)}, u32[]{:S(2)}) collective-permute-start(bf16[5,192,256]{2,1,0:T(8,128)(2,1)} %get-tuple-element.11), channel_id=1, source_target_pairs={{0,1},{1,0},{2,3},{3,2},{4,5},{5,4},{6,7},{7,6},{8,9},{9,8},{10,11... | collective-permute-start | bytes 1474568 | tf_op jit(solution)/shard_map/ppermute | solution.py:308
  107.3 0.0 collective-permute-done.7.refs_2_
  107.3 0.0 collective-permute-done.8.refs_3_
  107.3 0.7 copy-done.5
  108.0 0.7 copy-done.6
  108.7 3.4 %qkv_1.1 = (bf16[3,192,256]{2,1,0:T(8,128)(2,1)}, bf16[3,192,256]{2,1,0:T(8,128)(2,1)}) custom-call(bf16[192,1152]{1,0:T(8,128)(2,1)} %copy-done, bf16[192,1152]{1,0:T(8,128)(2,1)} %copy-done.1, bf16[96,1152]{1,0:T(8,128)(2,1)} %copy-done.5, bf16[96,1152]{1,0:T(8,128)(2,1)} %copy-done.6, bf16[216,1152]{1,0:T(8,128)(2,1)} %bitcast.9, bf16[216,1152]{1,0:T(8,128)(2,1)} %copy-done.4), custom_call_target="tpu_custom_call" | custom-call | flops 573308928 | bytes 2912256 | tf_op jit(solution)/shard_map/qkv_1/pallas_call | solution.py:250
  112.1 1.9 %collective-permute-start.10 = (bf16[3,192,256]{2,1,0:T(8,128)(2,1)}, bf16[3,192,256]{2,1,0:T(8,128)(2,1)S(1)}, u32[]{:S(2)}, u32[]{:S(2)}) collective-permute-start(bf16[3,192,256]{2,1,0:T(8,128)(2,1)} %get-tuple-element.12), channel_id=1, source_target_pairs={{0,1},{1,0},{2,3},{3,2},{4,5},{5,4},{6,7},{7,6},{8,9},{9,8},{10,11... | collective-permute-start | bytes 884744 | tf_op jit(solution)/shard_map/ppermute | solution.py:308
  114.0 0.0 collective-permute-done.9.refs_2_
  114.1 0.0 copy-start.7
  114.1 1.7 %collective-permute-done.10.refs_3_ = bf16[3,192,256]{2,1,0:T(8,128)(2,1)S(1)} collective-permute-done((bf16[3,192,256]{2,1,0:T(8,128)(2,1)}, bf16[3,192,256]{2,1,0:T(8,128)(2,1)S(1)}, u32[]{:S(2)}, u32[]{:S(2)}) %collective-permute-start.10) | collective-permute-done | bytes 294944 | tf_op jit(solution)/shard_map/ppermute | solution.py:308
  115.8 0.7 copy-done.12
  116.5 18.8 %attend.1 = bf16[16,112,128]{2,1,0:T(8,128)(2,1)} custom-call(s32[1]{0:T(128)} %bitcast.me_ref, s32[1,3072]{1,0:T(1,128)} %doc_ref.1, bf16[5,192,256]{2,1,0:T(8,128)(2,1)} %get-tuple-element.9.refs_0_, bf16[3,192,256]{2,1,0:T(8,128)(2,1)} %get-tuple-element.10.refs_1_, bf16[5,192,256]{2,1,0:T(8,128)(2,1)} %copy-done.7, bf16[3,192,256]{2,1,0:T(8,128)(2,1)} %copy-done.12), custom_call_target="tpu_custom_call" | custom-call | flops 1358954496 | bytes 2043908 | tf_op jit(solution)/shard_map/attend/pallas_call | solution.py:250
  135.3 22.2 %all_to_all.10.in_ref = bf16[16,112,128]{2,1,0:T(8,128)(2,1)} all-to-all(bf16[16,112,128]{2,1,0:T(8,128)(2,1)} %attend.1), channel_id=1, replica_groups=mesh['pack'=32,'seq'=16] {'seq'}, dimensions={0} | all-to-all | bytes 917504 | tf_op jit(solution)/shard_map/all_to_all | solution.py:344
  157.5 3.5 %project.1 = bf16[192,1152]{1,0:T(8,128)(2,1)} custom-call(bf16[16,112,128]{2,1,0:T(8,128)(2,1)} %all_to_all.10.in_ref, bf16[16,72,1152]{2,1,0:T(8,128)(2,1)} %bitcast.7), custom_call_target="tpu_custom_call" | custom-call | flops 509607936 | bytes 3555328 | tf_op jit(solution)/shard_map/project/pallas_call | solution.py:250
  (14 shorter events, 0.1 us)
Async XLA Ops:
  6.5 151.0 %all-gather.3.cloned.1.call-start = ((), (), s32[]{:S(2)}) async-start(), calls=%async_computation.2 | async-start | bytes 2820096 | tf_op jit(solution)/shard_map/all_gather | solution.py:321
  7.3 14.0 %copy-start.3 = (bf16[3,1152,72]{1,2,0:T(8,128)(2,1)S(1)}, bf16[3,1152,72]{1,2,0:T(8,128)(2,1)}, u32[]{:S(2)}) copy-start(bf16[3,1152,72]{1,2,0:T(8,128)(2,1)} %param.8) | copy-start | bytes 1492996
  10.1 35.2 %all-to-all-start = ((bf16[32,112,128]{2,1,0:T(8,128)(2,1)}), bf16[32,112,128]{2,1,0:T(8,128)(2,1)S(1)}, u32[]{:S(2)}, u32[]{:S(2)}) async-start(bf16[32,112,128]{2,1,0:T(8,128)(2,1)} %pack_rows.1), calls=%async_computation | async-start | bytes 1835008 | tf_op jit(solution)/shard_map/all_to_all | solution.py:318
  21.2 4.6 %collective-permute-start = (bf16[216,1152]{1,0:T(8,128)(2,1)S(1)}, bf16[216,1152]{1,0:T(8,128)(2,1)S(1)}, u32[]{:S(2)}, u32[]{:S(2)}) collective-permute-start(bf16[216,1152]{1,0:T(8,128)(2,1)S(1)} %bitcast.10), channel_id=1, source_target_pairs={{0,1},{1,0},{2,3},{3,2},{4,5},{5,4},{6,7},{7,6},{8,9},{9,8},{10,11... | collective-permute-start | bytes 1493000 | tf_op jit(solution)/shard_map/ppermute | solution.py:308
  25.9 19.4 %copy-start.4 = (bf16[216,1152]{1,0:T(8,128)(2,1)}, bf16[216,1152]{1,0:T(8,128)(2,1)S(1)}, u32[]{:S(2)}) copy-start(bf16[216,1152]{1,0:T(8,128)(2,1)S(1)} %collective-permute-done.refs_0_.refs_6_.refs_5_) | copy-start | bytes 1492996
  45.3 0.9 copy-start.2
  49.3 15.3 %collective-permute-start.1 = (bf16[192,1152]{1,0:T(8,128)(2,1)}, bf16[192,1152]{1,0:T(8,128)(2,1)S(1)}, u32[]{:S(2)}, u32[]{:S(2)}) collective-permute-start(bf16[192,1152]{1,0:T(8,128)(2,1)} %unpack_rows.1.refs_0_), channel_id=1, source_target_pairs={{0,2},{1,3},{2,4},{3,5},{4,6},{5,7},{6,8},{7,9},{8,10},{9,11},{10,... | collective-permute-start | bytes 1327112 | tf_op jit(solution)/shard_map/ppermute | solution.py:296
  52.5 14.0 %collective-permute-start.2 = (bf16[192,1152]{1,0:T(8,128)(2,1)}, bf16[192,1152]{1,0:T(8,128)(2,1)S(1)}, u32[]{:S(2)}, u32[]{:S(2)}) collective-permute-start(bf16[192,1152]{1,0:T(8,128)(2,1)} %unpack_rows.1.refs_0_), channel_id=1, source_target_pairs={{0,14},{1,15},{2,0},{3,1},{4,2},{5,3},{6,4},{7,5},{8,6},{9,7},{10,... | collective-permute-start | bytes 1327112 | tf_op jit(solution)/shard_map/ppermute | solution.py:296
  64.6 33.0 %copy-start.8 = (bf16[192,1152]{1,0:T(8,128)(2,1)}, bf16[192,1152]{1,0:T(8,128)(2,1)S(1)}, u32[]{:S(2)}) copy-start(bf16[192,1152]{1,0:T(8,128)(2,1)S(1)} %collective-permute-done.1.refs_1_) | copy-start | bytes 1327108
  64.6 13.7 %collective-permute-start.3 = (bf16[192,1152]{1,0:T(8,128)(2,1)S(1)}, bf16[192,1152]{1,0:T(8,128)(2,1)S(1)}, u32[]{:S(2)}, u32[]{:S(2)}) collective-permute-start(bf16[192,1152]{1,0:T(8,128)(2,1)S(1)} %collective-permute-done.1.refs_1_), channel_id=1, source_target_pairs={{0,2},{1,3},{2,4},{3,5},{4,6},{5,7},{6,8},{7,9},{8,10},{9,11},{10,... | collective-permute-start | bytes 1327112 | tf_op jit(solution)/shard_map/ppermute | solution.py:296
  66.5 31.1 %copy-start.9 = (bf16[192,1152]{1,0:T(8,128)(2,1)}, bf16[192,1152]{1,0:T(8,128)(2,1)S(1)}, u32[]{:S(2)}) copy-start(bf16[192,1152]{1,0:T(8,128)(2,1)S(1)} %collective-permute-done.2.refs_2_) | copy-start | bytes 1327108
  66.6 13.7 %collective-permute-start.4 = (bf16[192,1152]{1,0:T(8,128)(2,1)S(1)}, bf16[192,1152]{1,0:T(8,128)(2,1)S(1)}, u32[]{:S(2)}, u32[]{:S(2)}) collective-permute-start(bf16[192,1152]{1,0:T(8,128)(2,1)S(1)} %collective-permute-done.2.refs_2_), channel_id=1, source_target_pairs={{0,14},{1,15},{2,0},{3,1},{4,2},{5,3},{6,4},{7,5},{8,6},{9,7},{10,... | collective-permute-start | bytes 1327112 | tf_op jit(solution)/shard_map/ppermute | solution.py:296
  78.3 19.4 %copy-start.10 = (bf16[192,1152]{1,0:T(8,128)(2,1)}, bf16[192,1152]{1,0:T(8,128)(2,1)S(1)}, u32[]{:S(2)}) copy-start(bf16[192,1152]{1,0:T(8,128)(2,1)S(1)} %collective-permute-done.3.refs_3_) | copy-start | bytes 1327108
  78.3 12.7 %collective-permute-start.5 = (bf16[192,1152]{1,0:T(8,128)(2,1)S(1)}, bf16[192,1152]{1,0:T(8,128)(2,1)S(1)}, u32[]{:S(2)}, u32[]{:S(2)}) collective-permute-start(bf16[192,1152]{1,0:T(8,128)(2,1)S(1)} %collective-permute-done.3.refs_3_), channel_id=1, source_target_pairs={{0,2},{1,3},{2,4},{3,5},{4,6},{5,7},{6,8},{7,9},{8,10},{9,11},{10,... | collective-permute-start | bytes 1327112 | tf_op jit(solution)/shard_map/ppermute | solution.py:296
  80.2 17.4 %copy-start.11 = (bf16[192,1152]{1,0:T(8,128)(2,1)}, bf16[192,1152]{1,0:T(8,128)(2,1)S(1)}, u32[]{:S(2)}) copy-start(bf16[192,1152]{1,0:T(8,128)(2,1)S(1)} %collective-permute-done.4.refs_4_) | copy-start | bytes 1327108
  80.2 12.8 %collective-permute-start.6 = (bf16[192,1152]{1,0:T(8,128)(2,1)S(1)}, bf16[192,1152]{1,0:T(8,128)(2,1)S(1)}, u32[]{:S(2)}, u32[]{:S(2)}) collective-permute-start(bf16[192,1152]{1,0:T(8,128)(2,1)S(1)} %collective-permute-done.4.refs_4_), channel_id=1, source_target_pairs={{0,14},{1,15},{2,0},{3,1},{4,2},{5,3},{6,4},{7,5},{8,6},{9,7},{10,... | collective-permute-start | bytes 1327112 | tf_op jit(solution)/shard_map/ppermute | solution.py:296
  91.0 16.3 %copy-start = (bf16[192,1152]{1,0:T(8,128)(2,1)}, bf16[192,1152]{1,0:T(8,128)(2,1)S(1)}, u32[]{:S(2)}) copy-start(bf16[192,1152]{1,0:T(8,128)(2,1)S(1)} %collective-permute-done.5.refs_0_) | copy-start | bytes 1327108
  91.1 16.2 %collective-permute-start.7 = (bf16[96,1152]{1,0:T(8,128)(2,1)S(1)}, bf16[96,1152]{1,0:T(8,128)(2,1)S(1)}, u32[]{:S(2)}, u32[]{:S(2)}) collective-permute-start(bf16[96,1152]{1,0:T(8,128)(2,1)S(1)} %slice.8), channel_id=1, source_target_pairs={{0,2},{1,3},{2,4},{3,5},{4,6},{5,7},{6,8},{7,9},{8,10},{9,11},{10,... | collective-permute-start | bytes 663560 | tf_op jit(solution)/shard_map/ppermute | solution.py:296
  93.0 14.3 %copy-start.1 = (bf16[192,1152]{1,0:T(8,128)(2,1)}, bf16[192,1152]{1,0:T(8,128)(2,1)S(1)}, u32[]{:S(2)}) copy-start(bf16[192,1152]{1,0:T(8,128)(2,1)S(1)} %collective-permute-done.6.refs_1_) | copy-start | bytes 1327108
  93.0 14.3 %collective-permute-start.8 = (bf16[96,1152]{1,0:T(8,128)(2,1)S(1)}, bf16[96,1152]{1,0:T(8,128)(2,1)S(1)}, u32[]{:S(2)}, u32[]{:S(2)}) collective-permute-start(bf16[96,1152]{1,0:T(8,128)(2,1)S(1)} %slice.9), channel_id=1, source_target_pairs={{0,14},{1,15},{2,0},{3,1},{4,2},{5,3},{6,4},{7,5},{8,6},{9,7},{10,... | collective-permute-start | bytes 663560 | tf_op jit(solution)/shard_map/ppermute | solution.py:296
  101.9 12.1 %collective-permute-start.9 = (bf16[5,192,256]{2,1,0:T(8,128)(2,1)}, bf16[5,192,256]{2,1,0:T(8,128)(2,1)S(1)}, u32[]{:S(2)}, u32[]{:S(2)}) collective-permute-start(bf16[5,192,256]{2,1,0:T(8,128)(2,1)} %get-tuple-element.11), channel_id=1, source_target_pairs={{0,1},{1,0},{2,3},{3,2},{4,5},{5,4},{6,7},{7,6},{8,9},{9,8},{10,11... | collective-permute-start | bytes 1474568 | tf_op jit(solution)/shard_map/ppermute | solution.py:308
  107.3 0.7 copy-start.5
  108.0 0.7 copy-start.6
  112.1 3.7 %collective-permute-start.10 = (bf16[3,192,256]{2,1,0:T(8,128)(2,1)}, bf16[3,192,256]{2,1,0:T(8,128)(2,1)S(1)}, u32[]{:S(2)}, u32[]{:S(2)}) collective-permute-start(bf16[3,192,256]{2,1,0:T(8,128)(2,1)} %get-tuple-element.12), channel_id=1, source_target_pairs={{0,1},{1,0},{2,3},{3,2},{4,5},{5,4},{6,7},{7,6},{8,9},{9,8},{10,11... | collective-permute-start | bytes 884744 | tf_op jit(solution)/shard_map/ppermute | solution.py:308
  114.1 1.7 %copy-start.7 = (bf16[5,192,256]{2,1,0:T(8,128)(2,1)}, bf16[5,192,256]{2,1,0:T(8,128)(2,1)S(1)}, u32[]{:S(2)}) copy-start(bf16[5,192,256]{2,1,0:T(8,128)(2,1)S(1)} %collective-permute-done.9.refs_2_) | copy-start | bytes 1474564
  115.8 0.7 copy-start.12
Sparse Core Ops, SparseCore 0:
  9.5 46.3 all-gather.2

commit v7 on v6

--- a/solution.py
+++ b/solution.py
@@ -97,7 +97,7 @@
 AROWS = 112
 NEG = -3e38
 BACK = (0, 1, -1, 2, -2, 3, -3, 4)
-LIMIT = pltpu.CompilerParams(vmem_limit_bytes=56 * 2**20)
+LIMIT = pltpu.CompilerParams(vmem_limit_bytes=30 * 2**20)
 
 
 def origin(me, n):
@@ -290,6 +290,13 @@
     )
 
 
+def halves_kernel(right_ref, left_ref, *refs):
+    *_, top_ref, bottom_ref = refs
+    half = top_ref.shape[0]
+    top_ref[...] = right_ref[0:half, :]
+    bottom_ref[...] = left_ref[half:, :]
+
+
 def ring_step(right, left, n_seq):
     up = [(i, (i + 2) % n_seq) for i in range(n_seq)]
     down = [(i, (i - 2) % n_seq) for i in range(n_seq)]
@@ -333,14 +340,15 @@
     for _ in range(3):
         right, left = ring_step(right, left, n_seq)
         held += [right, left]
-    held += ring_step(right[: TOK // 2], left[TOK // 2 :], n_seq)
-
-    mine, theirs = [], []
-    for n, (begin, end) in enumerate(((0, 5), (5, 9))):
-        own, other = project_qkv(held[begin:end], w_t, pair_w, f"qkv_{n}")
-        mine.append(own)
-        theirs.append(other_core(other))
-    attended = attend_call(me, doc_ids, n_seq, *mine, *theirs)
+    mine, theirs = project_qkv(held[:5], w_t, pair_w, "qkv_first")
+    half = shape((TOK // 2, width), BF)
+    top, bottom = local_call(
+        halves_kernel, (half, half), right, left, behind=(theirs,), name="halves", flops=0
+    )
+    held += ring_step(top, bottom, n_seq)
+    last_mine, last_theirs = project_qkv(held[5:], w_t, pair_w, "qkv_last")
+    ours = [mine, last_mine, other_core(theirs), other_core(last_theirs)]
+    attended = attend_call(me, doc_ids, n_seq, *ours)
     blocks = lax.all_to_all(attended, "seq", split_axis=0, concat_axis=0, tiled=True)
 
     out = local_call(

time: 169 us -> 152 us (0.90)
  Pallas kernels: 35.9 us -> 16.8 us
  starting transfers between devices: 48 us -> 49.8 us
    pallas_call x6 -> x7, Pallas kernels: 35.9 us -> 16.8 us  [local_call(): pl.pallas_call(kernel, out_shape=out_shape, in_specs=[smem] * small + [vm...]
    unnamed x26 -> x10, local copies, waits for them, and re-layouts: 3.04 us -> 3.44 us
  transfers between devices with their start and end apart: 13 -> 13, of which waited for: 6 -> 7; matrix products, arithmetic and copies ran while one was open for 0% -> 0% of each run, Pallas kernels for 19% -> 10%
where the time goes in v7:
time: 152 us; the launch traced here: 151 us
  starting transfers between devices  49.8 us (33%)
  waiting for transfers between devices  45.5 us (30%)
  blocking collectives  21.8 us (14%)
  Pallas kernels  16.8 us (11%)
  between operations  13.6 us (9%)
  local copies, waits for them, and re-layouts  3.44 us (2%)
    ppermute x8, starting transfers between devices, ring_step(): return (lax.ppermute(right, 'seq', up), lax.ppermute(left, 'seq', down))  27.2 us
    ppermute x8, waiting for transfers between devices, ring_step(): return (lax.ppermute(right, 'seq', up), lax.ppermute(left, 'seq', down))  22.7 us
    all_to_all x1, blocking collectives, body(): lax.all_to_all(attended, 'seq', split_axis=0, concat_axis=0, tiled=True)  21.8 us
    all_to_all x1, waiting for transfers between devices, body(): lax.all_to_all(outbox, 'pack', split_axis=0, concat_axis=0, tiled=True)  19.4 us
    pallas_call x7, Pallas kernels, local_call(): pl.pallas_call(kernel, out_shape=out_shape, in_specs=[smem] * small + [vm...  16.8 us
    ppermute x3, starting transfers between devices, other_core(): return lax.ppermute(x, 'seq', [(i, i ^ 1) for i in range(n_seq)])  11.5 us
    all_to_all x1, starting transfers between devices, body(): lax.all_to_all(outbox, 'pack', split_axis=0, concat_axis=0, tiled=True)  11.1 us
    unnamed x10, local copies, waits for them, and re-layouts  3.44 us
  transfers between devices with their start and end apart: 13, of which 7 were waited for; matrix products, arithmetic and copies ran while one was open for 0% of the time, Pallas kernels for 10%

profile of v7, /device:TPU:135, one launch (start us, length us, event | category | flops | bytes accessed | tf_op | source)
XLA Modules:
  0.0 150.9 jit_solution(15837287704278522385)
XLA Ops:
  6.5 0.0 all-gather.3.cloned.1.call-start
  6.5 0.7 all-gather.3.cloned.1.call-update
  7.3 0.0 copy-start.2
  7.3 1.0 copy-done.2
  8.3 0.0 copy-start.4
  8.3 0.7 copy-done.4
  8.9 0.0 copy-start.1
  9.0 1.8 %pack_rows.1 = bf16[32,112,128]{2,1,0:T(8,128)(2,1)} custom-call(s32[1,192]{1,0:T(1,128)S(1)} %copy-done.4, bf16[192,1152]{1,0:T(8,128)(2,1)S(1)} %bitcast.11), custom_call_target="tpu_custom_call" | custom-call | flops 1000000000 | bytes 1360640 | tf_op jit(solution)/shard_map/pack_rows/pallas_call | solution.py:250
  10.7 11.1 %all-to-all-start = ((bf16[32,112,128]{2,1,0:T(8,128)(2,1)}), bf16[32,112,128]{2,1,0:T(8,128)(2,1)S(1)}, u32[]{:S(2)}, u32[]{:S(2)}) async-start(bf16[32,112,128]{2,1,0:T(8,128)(2,1)} %pack_rows.1), calls=%async_computation | async-start | bytes 1835008 | tf_op jit(solution)/shard_map/all_to_all | solution.py:325
  21.8 0.0 copy-done.1
  21.9 3.1 %collective-permute-start = (bf16[216,1152]{1,0:T(8,128)(2,1)S(1)}, bf16[216,1152]{1,0:T(8,128)(2,1)S(1)}, u32[]{:S(2)}, u32[]{:S(2)}) collective-permute-start(bf16[216,1152]{1,0:T(8,128)(2,1)S(1)} %bitcast.8), channel_id=1, source_target_pairs={{0,1},{1,0},{2,3},{3,2},{4,5},{5,4},{6,7},{7,6},{8,9},{9,8},{10,11... | collective-permute-start | bytes 1493000 | tf_op jit(solution)/shard_map/ppermute | solution.py:315
  25.0 1.5 collective-permute-done.refs_0_.refs_6_.refs_5_
  26.5 19.4 %all-to-all-done.in_ref = bf16[32,112,128]{2,1,0:T(8,128)(2,1)S(1)} async-done(((bf16[32,112,128]{2,1,0:T(8,128)(2,1)}), bf16[32,112,128]{2,1,0:T(8,128)(2,1)S(1)}, u32[]{:S(2)}, u32[]{:S(2)}) %all-to-all-start) | async-done | bytes 917536 | tf_op jit(solution)/shard_map/all_to_all | solution.py:325
  45.9 1.1 unpack_rows.1.refs_0_
  47.0 3.2 %collective-permute-start.1 = (bf16[192,1152]{1,0:T(8,128)(2,1)S(1)}, bf16[192,1152]{1,0:T(8,128)(2,1)S(1)}, u32[]{:S(2)}, u32[]{:S(2)}) collective-permute-start(bf16[192,1152]{1,0:T(8,128)(2,1)S(1)} %unpack_rows.1.refs_0_), channel_id=1, source_target_pairs={{0,2},{1,3},{2,4},{3,5},{4,6},{5,7},{6,8},{7,9},{8,10},{9,11},{10,... | collective-permute-start | bytes 1327112 | tf_op jit(solution)/shard_map/ppermute | solution.py:303
  50.2 3.8 %collective-permute-start.2 = (bf16[192,1152]{1,0:T(8,128)(2,1)S(1)}, bf16[192,1152]{1,0:T(8,128)(2,1)S(1)}, u32[]{:S(2)}, u32[]{:S(2)}) collective-permute-start(bf16[192,1152]{1,0:T(8,128)(2,1)S(1)} %unpack_rows.1.refs_0_), channel_id=1, source_target_pairs={{0,14},{1,15},{2,0},{3,1},{4,2},{5,3},{6,4},{7,5},{8,6},{9,7},{10,... | collective-permute-start | bytes 1327112 | tf_op jit(solution)/shard_map/ppermute | solution.py:303
  54.1 8.9 %collective-permute-done.1.refs_1_ = bf16[192,1152]{1,0:T(8,128)(2,1)S(1)} collective-permute-done((bf16[192,1152]{1,0:T(8,128)(2,1)S(1)}, bf16[192,1152]{1,0:T(8,128)(2,1)S(1)}, u32[]{:S(2)}, u32[]{:S(2)}) %collective-permute-start.1) | collective-permute-done | bytes 442400 | tf_op jit(solution)/shard_map/ppermute | solution.py:303
  63.0 1.9 %collective-permute-start.3 = (bf16[192,1152]{1,0:T(8,128)(2,1)S(1)}, bf16[192,1152]{1,0:T(8,128)(2,1)S(1)}, u32[]{:S(2)}, u32[]{:S(2)}) collective-permute-start(bf16[192,1152]{1,0:T(8,128)(2,1)S(1)} %collective-permute-done.1.refs_1_), channel_id=1, source_target_pairs={{0,2},{1,3},{2,4},{3,5},{4,6},{5,7},{6,8},{7,9},{8,10},{9,11},{10,... | collective-permute-start | bytes 1327112 | tf_op jit(solution)/shard_map/ppermute | solution.py:303
  64.9 0.0 collective-permute-done.2.refs_2_
  64.9 4.6 %collective-permute-start.4 = (bf16[192,1152]{1,0:T(8,128)(2,1)S(1)}, bf16[192,1152]{1,0:T(8,128)(2,1)S(1)}, u32[]{:S(2)}, u32[]{:S(2)}) collective-permute-start(bf16[192,1152]{1,0:T(8,128)(2,1)S(1)} %collective-permute-done.2.refs_2_), channel_id=1, source_target_pairs={{0,14},{1,15},{2,0},{3,1},{4,2},{5,3},{6,4},{7,5},{8,6},{9,7},{10,... | collective-permute-start | bytes 1327112 | tf_op jit(solution)/shard_map/ppermute | solution.py:303
  69.5 7.6 %collective-permute-done.3.refs_3_ = bf16[192,1152]{1,0:T(8,128)(2,1)S(1)} collective-permute-done((bf16[192,1152]{1,0:T(8,128)(2,1)S(1)}, bf16[192,1152]{1,0:T(8,128)(2,1)S(1)}, u32[]{:S(2)}, u32[]{:S(2)}) %collective-permute-start.3) | collective-permute-done | bytes 442400 | tf_op jit(solution)/shard_map/ppermute | solution.py:303
  77.1 1.9 %collective-permute-start.5 = (bf16[192,1152]{1,0:T(8,128)(2,1)S(1)}, bf16[192,1152]{1,0:T(8,128)(2,1)S(1)}, u32[]{:S(2)}, u32[]{:S(2)}) collective-permute-start(bf16[192,1152]{1,0:T(8,128)(2,1)S(1)} %collective-permute-done.3.refs_3_), channel_id=1, source_target_pairs={{0,2},{1,3},{2,4},{3,5},{4,6},{5,7},{6,8},{7,9},{8,10},{9,11},{10,... | collective-permute-start | bytes 1327112 | tf_op jit(solution)/shard_map/ppermute | solution.py:303
  79.0 0.0 collective-permute-done.4.refs_4_
  79.0 4.6 %collective-permute-start.6 = (bf16[192,1152]{1,0:T(8,128)(2,1)S(1)}, bf16[192,1152]{1,0:T(8,128)(2,1)S(1)}, u32[]{:S(2)}, u32[]{:S(2)}) collective-permute-start(bf16[192,1152]{1,0:T(8,128)(2,1)S(1)} %collective-permute-done.4.refs_4_), channel_id=1, source_target_pairs={{0,14},{1,15},{2,0},{3,1},{4,2},{5,3},{6,4},{7,5},{8,6},{9,7},{10,... | collective-permute-start | bytes 1327112 | tf_op jit(solution)/shard_map/ppermute | solution.py:303
  83.6 1.5 qkv_first.1
  85.1 0.0 copy-start.3
  85.1 5.2 %collective-permute-done.5.right_ref.refs_0_ = bf16[192,1152]{1,0:T(8,128)(2,1)S(1)} collective-permute-done((bf16[192,1152]{1,0:T(8,128)(2,1)S(1)}, bf16[192,1152]{1,0:T(8,128)(2,1)S(1)}, u32[]{:S(2)}, u32[]{:S(2)}) %collective-permute-start.5) | collective-permute-done | bytes 442400 | tf_op jit(solution)/shard_map/ppermute | solution.py:303
  90.3 0.9 collective-permute-done.6.left_ref.refs_1_
  91.3 1.9 %collective-permute-start.7 = (bf16[96,1152]{1,0:T(8,128)(2,1)S(1)}, bf16[96,1152]{1,0:T(8,128)(2,1)S(1)}, u32[]{:S(2)}, u32[]{:S(2)}) collective-permute-start(bf16[96,1152]{1,0:T(8,128)(2,1)S(1)} %get-tuple-element.13), channel_id=1, source_target_pairs={{0,2},{1,3},{2,4},{3,5},{4,6},{5,7},{6,8},{7,9},{8,10},{9,11},{10,... | collective-permute-start | bytes 663560 | tf_op jit(solution)/shard_map/ppermute | solution.py:303
  93.2 5.3 %collective-permute-start.8 = (bf16[96,1152]{1,0:T(8,128)(2,1)S(1)}, bf16[96,1152]{1,0:T(8,128)(2,1)S(1)}, u32[]{:S(2)}, u32[]{:S(2)}) collective-permute-start(bf16[96,1152]{1,0:T(8,128)(2,1)S(1)} %get-tuple-element.14), channel_id=1, source_target_pairs={{0,14},{1,15},{2,0},{3,1},{4,2},{5,3},{6,4},{7,5},{8,6},{9,7},{10,... | collective-permute-start | bytes 663560 | tf_op jit(solution)/shard_map/ppermute | solution.py:303
  98.5 4.9 %collective-permute-start.9 = (bf16[5,192,256]{2,1,0:T(8,128)(2,1)S(1)}, bf16[5,192,256]{2,1,0:T(8,128)(2,1)S(1)}, u32[]{:S(2)}, u32[]{:S(2)}) collective-permute-start(bf16[5,192,256]{2,1,0:T(8,128)(2,1)S(1)} %get-tuple-element.12.refs_0_), channel_id=1, source_target_pairs={{0,1},{1,0},{2,3},{3,2},{4,5},{5,4},{6,7},{7,6},{8,9},{9,8},{10,11... | collective-permute-start | bytes 1474568 | tf_op jit(solution)/shard_map/ppermute | solution.py:315
  103.5 0.0 collective-permute-done.7.refs_2_
  103.5 0.0 collective-permute-done.8.refs_3_
  103.5 1.0 qkv_last.1
  104.5 3.4 %collective-permute-start.10 = (bf16[3,192,256]{2,1,0:T(8,128)(2,1)S(1)}, bf16[3,192,256]{2,1,0:T(8,128)(2,1)S(1)}, u32[]{:S(2)}, u32[]{:S(2)}) collective-permute-start(bf16[3,192,256]{2,1,0:T(8,128)(2,1)S(1)} %get-tuple-element.16), channel_id=1, source_target_pairs={{0,1},{1,0},{2,3},{3,2},{4,5},{5,4},{6,7},{7,6},{8,9},{9,8},{10,11... | collective-permute-start | bytes 884744 | tf_op jit(solution)/shard_map/ppermute | solution.py:315
  107.9 0.0 collective-permute-done.9.refs_2_
  107.9 1.2 collective-permute-done.10.refs_3_
  109.1 0.0 copy-done.3
  109.1 9.8 %attend.1 = bf16[16,112,128]{2,1,0:T(8,128)(2,1)S(1)} custom-call(s32[1]{0:T(128)} %bitcast.me_ref, s32[1,3072]{1,0:T(1,128)S(1)} %copy-done.3, bf16[5,192,256]{2,1,0:T(8,128)(2,1)S(1)} %get-tuple-element.11.refs_0_, bf16[3,192,256]{2,1,0:T(8,128)(2,1)S(1)} %get-tuple-element.15.refs_1_, bf16[5,192,256]{2,1,0:T(8,128)(2,1)S(1)} %collective-permute-done.9.refs_2_, ...), custom_call_target="tpu_custom_call" | custom-call | flops 1358954496 | bytes 2043908 | tf_op jit(solution)/shard_map/attend/pallas_call | solution.py:250
  118.9 21.8 %all_to_all.10.in_ref = bf16[16,112,128]{2,1,0:T(8,128)(2,1)S(1)} all-to-all(bf16[16,112,128]{2,1,0:T(8,128)(2,1)S(1)} %attend.1), channel_id=1, replica_groups=mesh['pack'=32,'seq'=16] {'seq'}, dimensions={0} | all-to-all | bytes 917504 | tf_op jit(solution)/shard_map/all_to_all | solution.py:352
  140.7 0.0 all-gather.3.cloned.1.call-done
  140.7 0.0 copy-start
  140.7 1.7 %copy-done = bf16[1152,1152]{1,0:T(8,128)(2,1)S(1)} copy-done((bf16[1152,1152]{1,0:T(8,128)(2,1)S(1)}, bf16[1152,1152]{1,0:T(8,128)(2,1)}, u32[]{:S(2)}) %copy-start) | copy-done | bytes 2654232
  142.4 1.6 %project.1 = bf16[192,1152]{1,0:T(8,128)(2,1)} custom-call(bf16[16,112,128]{2,1,0:T(8,128)(2,1)S(1)} %all_to_all.10.in_ref, bf16[16,72,1152]{2,1,0:T(8,128)(2,1)S(1)} %bitcast.7), custom_call_target="tpu_custom_call" | custom-call | flops 509607936 | bytes 3555328 | tf_op jit(solution)/shard_map/project/pallas_call | solution.py:250
  (1 shorter events, 0.0 us)
Async XLA Ops:
  6.5 134.2 %all-gather.3.cloned.1.call-start = ((), (), s32[]{:S(2)}) async-start(), calls=%async_computation.2 | async-start | bytes 2820096 | tf_op jit(solution)/shard_map/all_gather | solution.py:328
  7.3 1.0 copy-start.2
  8.3 0.7 copy-start.4
  8.9 12.9 %copy-start.1 = (bf16[3,1152,72]{1,2,0:T(8,128)(2,1)S(1)}, bf16[3,1152,72]{1,2,0:T(8,128)(2,1)}, u32[]{:S(2)}) copy-start(bf16[3,1152,72]{1,2,0:T(8,128)(2,1)} %param.8) | copy-start | bytes 1492996
  10.7 35.2 %all-to-all-start = ((bf16[32,112,128]{2,1,0:T(8,128)(2,1)}), bf16[32,112,128]{2,1,0:T(8,128)(2,1)S(1)}, u32[]{:S(2)}, u32[]{:S(2)}) async-start(bf16[32,112,128]{2,1,0:T(8,128)(2,1)} %pack_rows.1), calls=%async_computation | async-start | bytes 1835008 | tf_op jit(solution)/shard_map/all_to_all | solution.py:325
  21.9 4.6 %collective-permute-start = (bf16[216,1152]{1,0:T(8,128)(2,1)S(1)}, bf16[216,1152]{1,0:T(8,128)(2,1)S(1)}, u32[]{:S(2)}, u32[]{:S(2)}) collective-permute-start(bf16[216,1152]{1,0:T(8,128)(2,1)S(1)} %bitcast.8), channel_id=1, source_target_pairs={{0,1},{1,0},{2,3},{3,2},{4,5},{5,4},{6,7},{7,6},{8,9},{9,8},{10,11... | collective-permute-start | bytes 1493000 | tf_op jit(solution)/shard_map/ppermute | solution.py:315
  47.0 16.0 %collective-permute-start.1 = (bf16[192,1152]{1,0:T(8,128)(2,1)S(1)}, bf16[192,1152]{1,0:T(8,128)(2,1)S(1)}, u32[]{:S(2)}, u32[]{:S(2)}) collective-permute-start(bf16[192,1152]{1,0:T(8,128)(2,1)S(1)} %unpack_rows.1.refs_0_), channel_id=1, source_target_pairs={{0,2},{1,3},{2,4},{3,5},{4,6},{5,7},{6,8},{7,9},{8,10},{9,11},{10,... | collective-permute-start | bytes 1327112 | tf_op jit(solution)/shard_map/ppermute | solution.py:303
  50.2 14.7 %collective-permute-start.2 = (bf16[192,1152]{1,0:T(8,128)(2,1)S(1)}, bf16[192,1152]{1,0:T(8,128)(2,1)S(1)}, u32[]{:S(2)}, u32[]{:S(2)}) collective-permute-start(bf16[192,1152]{1,0:T(8,128)(2,1)S(1)} %unpack_rows.1.refs_0_), channel_id=1, source_target_pairs={{0,14},{1,15},{2,0},{3,1},{4,2},{5,3},{6,4},{7,5},{8,6},{9,7},{10,... | collective-permute-start | bytes 1327112 | tf_op jit(solution)/shard_map/ppermute | solution.py:303
  63.0 14.1 %collective-permute-start.3 = (bf16[192,1152]{1,0:T(8,128)(2,1)S(1)}, bf16[192,1152]{1,0:T(8,128)(2,1)S(1)}, u32[]{:S(2)}, u32[]{:S(2)}) collective-permute-start(bf16[192,1152]{1,0:T(8,128)(2,1)S(1)} %collective-permute-done.1.refs_1_), channel_id=1, source_target_pairs={{0,2},{1,3},{2,4},{3,5},{4,6},{5,7},{6,8},{7,9},{8,10},{9,11},{10,... | collective-permute-start | bytes 1327112 | tf_op jit(solution)/shard_map/ppermute | solution.py:303
  64.9 14.1 %collective-permute-start.4 = (bf16[192,1152]{1,0:T(8,128)(2,1)S(1)}, bf16[192,1152]{1,0:T(8,128)(2,1)S(1)}, u32[]{:S(2)}, u32[]{:S(2)}) collective-permute-start(bf16[192,1152]{1,0:T(8,128)(2,1)S(1)} %collective-permute-done.2.refs_2_), channel_id=1, source_target_pairs={{0,14},{1,15},{2,0},{3,1},{4,2},{5,3},{6,4},{7,5},{8,6},{9,7},{10,... | collective-permute-start | bytes 1327112 | tf_op jit(solution)/shard_map/ppermute | solution.py:303
  77.1 13.2 %collective-permute-start.5 = (bf16[192,1152]{1,0:T(8,128)(2,1)S(1)}, bf16[192,1152]{1,0:T(8,128)(2,1)S(1)}, u32[]{:S(2)}, u32[]{:S(2)}) collective-permute-start(bf16[192,1152]{1,0:T(8,128)(2,1)S(1)} %collective-permute-done.3.refs_3_), channel_id=1, source_target_pairs={{0,2},{1,3},{2,4},{3,5},{4,6},{5,7},{6,8},{7,9},{8,10},{9,11},{10,... | collective-permute-start | bytes 1327112 | tf_op jit(solution)/shard_map/ppermute | solution.py:303
  79.0 12.2 %collective-permute-start.6 = (bf16[192,1152]{1,0:T(8,128)(2,1)S(1)}, bf16[192,1152]{1,0:T(8,128)(2,1)S(1)}, u32[]{:S(2)}, u32[]{:S(2)}) collective-permute-start(bf16[192,1152]{1,0:T(8,128)(2,1)S(1)} %collective-permute-done.4.refs_4_), channel_id=1, source_target_pairs={{0,14},{1,15},{2,0},{3,1},{4,2},{5,3},{6,4},{7,5},{8,6},{9,7},{10,... | collective-permute-start | bytes 1327112 | tf_op jit(solution)/shard_map/ppermute | solution.py:303
  85.1 24.0 %copy-start.3 = (s32[1,3072]{1,0:T(1,128)S(1)}, s32[1,3072]{1,0:T(1,128)}, u32[]{:S(2)}) copy-start(s32[1,3072]{1,0:T(1,128)} %doc_ref.1) | copy-start | bytes 36868
  91.3 12.2 %collective-permute-start.7 = (bf16[96,1152]{1,0:T(8,128)(2,1)S(1)}, bf16[96,1152]{1,0:T(8,128)(2,1)S(1)}, u32[]{:S(2)}, u32[]{:S(2)}) collective-permute-start(bf16[96,1152]{1,0:T(8,128)(2,1)S(1)} %get-tuple-element.13), channel_id=1, source_target_pairs={{0,2},{1,3},{2,4},{3,5},{4,6},{5,7},{6,8},{7,9},{8,10},{9,11},{10,... | collective-permute-start | bytes 663560 | tf_op jit(solution)/shard_map/ppermute | solution.py:303
  93.2 10.3 %collective-permute-start.8 = (bf16[96,1152]{1,0:T(8,128)(2,1)S(1)}, bf16[96,1152]{1,0:T(8,128)(2,1)S(1)}, u32[]{:S(2)}, u32[]{:S(2)}) collective-permute-start(bf16[96,1152]{1,0:T(8,128)(2,1)S(1)} %get-tuple-element.14), channel_id=1, source_target_pairs={{0,14},{1,15},{2,0},{3,1},{4,2},{5,3},{6,4},{7,5},{8,6},{9,7},{10,... | collective-permute-start | bytes 663560 | tf_op jit(solution)/shard_map/ppermute | solution.py:303
  98.5 9.4 %collective-permute-start.9 = (bf16[5,192,256]{2,1,0:T(8,128)(2,1)S(1)}, bf16[5,192,256]{2,1,0:T(8,128)(2,1)S(1)}, u32[]{:S(2)}, u32[]{:S(2)}) collective-permute-start(bf16[5,192,256]{2,1,0:T(8,128)(2,1)S(1)} %get-tuple-element.12.refs_0_), channel_id=1, source_target_pairs={{0,1},{1,0},{2,3},{3,2},{4,5},{5,4},{6,7},{7,6},{8,9},{9,8},{10,11... | collective-permute-start | bytes 1474568 | tf_op jit(solution)/shard_map/ppermute | solution.py:315
  104.5 4.6 %collective-permute-start.10 = (bf16[3,192,256]{2,1,0:T(8,128)(2,1)S(1)}, bf16[3,192,256]{2,1,0:T(8,128)(2,1)S(1)}, u32[]{:S(2)}, u32[]{:S(2)}) collective-permute-start(bf16[3,192,256]{2,1,0:T(8,128)(2,1)S(1)} %get-tuple-element.16), channel_id=1, source_target_pairs={{0,1},{1,0},{2,3},{3,2},{4,5},{5,4},{6,7},{7,6},{8,9},{9,8},{10,11... | collective-permute-start | bytes 884744 | tf_op jit(solution)/shard_map/ppermute | solution.py:315
  140.7 1.8 %copy-start = (bf16[1152,1152]{1,0:T(8,128)(2,1)S(1)}, bf16[1152,1152]{1,0:T(8,128)(2,1)}, u32[]{:S(2)}) copy-start(bf16[1152,1152]{1,0:T(8,128)(2,1)} %all-gather.3.cloned.1.call-done) | copy-start | bytes 7962628
Sparse Core Ops, SparseCore 0:
  9.5 46.7 all-gather.2

commit v8 on v7

--- a/solution.py
+++ b/solution.py
@@ -97,7 +97,6 @@
 AROWS = 112
 NEG = -3e38
 BACK = (0, 1, -1, 2, -2, 3, -3, 4)
-LIMIT = pltpu.CompilerParams(vmem_limit_bytes=30 * 2**20)
 
 
 def origin(me, n):
@@ -111,7 +110,7 @@
     *x_refs, mine_w_ref, pair_w_ref, mine_ref, pair_ref = refs
     x = jnp.concatenate([ref[...] for ref in x_refs], axis=0)
     rows = x.shape[0]
-    scale = jnp.where(iota((1, 3 * HD), 1) < HD, 1.0 / math.sqrt(HD), 1.0)
+    scale = jnp.where(iota((1, 3 * HD), 1) < HD, math.log2(math.e) / math.sqrt(HD), 1.0)
     fill = jnp.where(iota((rows, QKV - 3 * HD), 1) < VROWS - HD, 1.0, 0.0)
     for w_ref, out_ref in ((mine_w_ref, mine_ref), (pair_w_ref, pair_ref)):
         qkv = lax.dot_general(x, w_ref[...], NT, preferred_element_type=F32) * scale
@@ -162,13 +161,14 @@
         chunks = functools.reduce(
             jnp.maximum, [b[-1][1] - b[0][0] for _, _, b in tiles]
         )
-        chunks = (chunks + per_k - 1) // per_k
-
-        def one_chunk(c, carry):
+        big = (chunks + per_k // 2 - 1) // per_k
+        small = jnp.where(chunks > big * per_k, 1, 0)
+
+        def one_chunk(width, base, c, carry):
             result = []
             for (_, q, bounds), (high, total) in zip(tiles, carry):
-                begin = bounds[0][0] + c * per_k
-                keys = pl.ds(pl.multiple_of(jnp.minimum(begin, blocks) * BLK, BLK), KT)
+                begin = bounds[0][0] + base + c * (width // BLK)
+                keys = pl.ds(pl.multiple_of(jnp.minimum(begin, blocks) * BLK, BLK), width)
                 scores = lax.dot_general(k_s[keys, :], q, NT, preferred_element_type=F32)
                 columns = []
                 for i, (lo, hi) in enumerate(bounds):
@@ -178,13 +178,13 @@
                             scores[j * BLK : (j + 1) * BLK, i * BLK : (i + 1) * BLK],
                             -jnp.inf,
                         )
-                        for j in range(per_k)
+                        for j in range(width // BLK)
                     ]
                     columns.append(jnp.concatenate(kept, axis=0))
                 scores = jnp.concatenate(columns, axis=1)
                 newer = jnp.maximum(high, jnp.max(scores, axis=0, keepdims=True))
-                expo = jnp.exp(scores - newer).astype(BF)
-                total = total * jnp.exp(high - newer) + jnp.dot(
+                expo = jnp.exp2(scores - newer).astype(BF)
+                total = total * jnp.exp2(high - newer) + jnp.dot(
                     v_s[:, keys], expo, preferred_element_type=F32
                 )
                 result.append((newer, total))
@@ -193,7 +193,11 @@
         carry = tuple(
             (jnp.full((1, QT), NEG, F32), jnp.zeros((VROWS, QT), F32)) for _ in range(SIDE)
         )
-        for (t, _, _), (_, total) in zip(tiles, lax.fori_loop(0, chunks, one_chunk, carry)):
+        carry = lax.fori_loop(0, big, functools.partial(one_chunk, KT, 0), carry)
+        carry = lax.fori_loop(
+            0, small, functools.partial(one_chunk, KT // 2, big * per_k), carry
+        )
+        for (t, _, _), (_, total) in zip(tiles, carry):
             o_s[:, pl.ds(pl.multiple_of(t * QT, QT), QT)] = total / total[HD : HD + 1, :]
         return 0
 
@@ -243,7 +247,7 @@
     return pl.CostEstimate(flops=flops, bytes_accessed=total, transcendentals=0)
 
 
-def local_call(kernel, out_shape, *operands, name, flops, small=0, scratch=(), behind=()):
+def local_call(kernel, out_shape, *operands, name, flops, small=0, scratch=(), behind=(), mib=30):
     smem = pl.BlockSpec(memory_space=pltpu.SMEM)
     vmem = pl.BlockSpec(memory_space=pltpu.VMEM)
     after = [pl.BlockSpec(memory_space=pl.ANY)] * len(behind)
@@ -253,7 +257,7 @@
         in_specs=[smem] * small + [vmem] * (len(operands) - small) + after,
         out_specs=jax.tree.map(lambda _: vmem, out_shape),
         scratch_shapes=scratch,
-        compiler_params=LIMIT,
+        compiler_params=pltpu.CompilerParams(vmem_limit_bytes=mib * 2**20),
         cost_estimate=cost(flops, operands, out_shape),
         name=name,
     )(*operands, *behind)
@@ -321,6 +325,7 @@
         source[0],
         name="pack_rows",
         flops=10**9,
+        mib=56,
     )
     inbox = lax.all_to_all(outbox, "pack", split_axis=0, concat_axis=0, tiled=True)
 

time: 152 us -> 150 us (0.987)
  local copies, waits for them, and re-layouts: 3.44 us -> 1.76 us
    unnamed x10 -> x6, local copies, waits for them, and re-layouts: 3.44 us -> 1.76 us
where the time goes in v8:
time: 150 us; the launch traced here: 149 us
  starting transfers between devices  50.2 us (33%)
  waiting for transfers between devices  44.4 us (30%)
  blocking collectives  22.5 us (15%)
  Pallas kernels  17 us (11%)
  between operations  13.6 us (9%)
  local copies, waits for them, and re-layouts  1.76 us (1%)
    ppermute x8, starting transfers between devices, ring_step(): return (lax.ppermute(right, 'seq', up), lax.ppermute(left, 'seq', down))  27.2 us
    all_to_all x1, blocking collectives, body(): lax.all_to_all(attended, 'seq', split_axis=0, concat_axis=0, tiled=True)  22.5 us
    ppermute x8, waiting for transfers between devices, ring_step(): return (lax.ppermute(right, 'seq', up), lax.ppermute(left, 'seq', down))  21.5 us
    all_to_all x1, waiting for transfers between devices, body(): lax.all_to_all(outbox, 'pack', split_axis=0, concat_axis=0, tiled=True)  19.4 us
    pallas_call x7, Pallas kernels, local_call(): pl.pallas_call(kernel, out_shape=out_shape, in_specs=[smem] * small + [vm...  17 us
    ppermute x3, starting transfers between devices, other_core(): return lax.ppermute(x, 'seq', [(i, i ^ 1) for i in range(n_seq)])  11.9 us
    all_to_all x1, starting transfers between devices, body(): lax.all_to_all(outbox, 'pack', split_axis=0, concat_axis=0, tiled=True)  11.1 us
  transfers between devices with their start and end apart: 13, of which 7 were waited for; matrix products, arithmetic and copies ran while one was open for 0% of the time, Pallas kernels for 10%

profile of v8, /device:TPU:135, one launch (start us, length us, event | category | flops | bytes accessed | tf_op | source)
XLA Modules:
  0.0 149.4 jit_solution(5172419752195558177)
XLA Ops:
  6.5 0.0 all-gather.3.cloned.1.call-start
  6.5 0.7 all-gather.3.cloned.1.call-update
  7.3 0.0 copy-start.1
  7.3 2.9 %pack_rows.1 = bf16[32,112,128]{2,1,0:T(8,128)(2,1)} custom-call(s32[1,192]{1,0:T(1,128)} %dest_ref.1, bf16[192,1152]{1,0:T(8,128)(2,1)} %bitcast.11), custom_call_target="tpu_custom_call" | custom-call | flops 1000000000 | bytes 1360640 | tf_op jit(solution)/shard_map/pack_rows/pallas_call | solution.py:254
  10.1 11.1 %all-to-all-start = ((bf16[32,112,128]{2,1,0:T(8,128)(2,1)}), bf16[32,112,128]{2,1,0:T(8,128)(2,1)S(1)}, u32[]{:S(2)}, u32[]{:S(2)}) async-start(bf16[32,112,128]{2,1,0:T(8,128)(2,1)} %pack_rows.1), calls=%async_computation | async-start | bytes 1835008 | tf_op jit(solution)/shard_map/all_to_all | solution.py:330
  21.2 0.0 copy-done.1
  21.2 3.1 %collective-permute-start = (bf16[216,1152]{1,0:T(8,128)(2,1)S(1)}, bf16[216,1152]{1,0:T(8,128)(2,1)S(1)}, u32[]{:S(2)}, u32[]{:S(2)}) collective-permute-start(bf16[216,1152]{1,0:T(8,128)(2,1)S(1)} %bitcast.8), channel_id=1, source_target_pairs={{0,1},{1,0},{2,3},{3,2},{4,5},{5,4},{6,7},{7,6},{8,9},{9,8},{10,11... | collective-permute-start | bytes 1493000 | tf_op jit(solution)/shard_map/ppermute | solution.py:319
  24.4 1.5 collective-permute-done.refs_0_.refs_6_.refs_5_
  25.9 19.4 %all-to-all-done.in_ref = bf16[32,112,128]{2,1,0:T(8,128)(2,1)S(1)} async-done(((bf16[32,112,128]{2,1,0:T(8,128)(2,1)}), bf16[32,112,128]{2,1,0:T(8,128)(2,1)S(1)}, u32[]{:S(2)}, u32[]{:S(2)}) %all-to-all-start) | async-done | bytes 917536 | tf_op jit(solution)/shard_map/all_to_all | solution.py:330
  45.3 1.1 unpack_rows.1.refs_0_
  46.4 3.2 %collective-permute-start.1 = (bf16[192,1152]{1,0:T(8,128)(2,1)S(1)}, bf16[192,1152]{1,0:T(8,128)(2,1)S(1)}, u32[]{:S(2)}, u32[]{:S(2)}) collective-permute-start(bf16[192,1152]{1,0:T(8,128)(2,1)S(1)} %unpack_rows.1.refs_0_), channel_id=1, source_target_pairs={{0,2},{1,3},{2,4},{3,5},{4,6},{5,7},{6,8},{7,9},{8,10},{9,11},{10,... | collective-permute-start | bytes 1327112 | tf_op jit(solution)/shard_map/ppermute | solution.py:307
  49.6 3.8 %collective-permute-start.2 = (bf16[192,1152]{1,0:T(8,128)(2,1)S(1)}, bf16[192,1152]{1,0:T(8,128)(2,1)S(1)}, u32[]{:S(2)}, u32[]{:S(2)}) collective-permute-start(bf16[192,1152]{1,0:T(8,128)(2,1)S(1)} %unpack_rows.1.refs_0_), channel_id=1, source_target_pairs={{0,14},{1,15},{2,0},{3,1},{4,2},{5,3},{6,4},{7,5},{8,6},{9,7},{10,... | collective-permute-start | bytes 1327112 | tf_op jit(solution)/shard_map/ppermute | solution.py:307
  53.5 8.6 %collective-permute-done.1.refs_1_ = bf16[192,1152]{1,0:T(8,128)(2,1)S(1)} collective-permute-done((bf16[192,1152]{1,0:T(8,128)(2,1)S(1)}, bf16[192,1152]{1,0:T(8,128)(2,1)S(1)}, u32[]{:S(2)}, u32[]{:S(2)}) %collective-permute-start.1) | collective-permute-done | bytes 442400 | tf_op jit(solution)/shard_map/ppermute | solution.py:307
  62.1 1.9 %collective-permute-start.3 = (bf16[192,1152]{1,0:T(8,128)(2,1)S(1)}, bf16[192,1152]{1,0:T(8,128)(2,1)S(1)}, u32[]{:S(2)}, u32[]{:S(2)}) collective-permute-start(bf16[192,1152]{1,0:T(8,128)(2,1)S(1)} %collective-permute-done.1.refs_1_), channel_id=1, source_target_pairs={{0,2},{1,3},{2,4},{3,5},{4,6},{5,7},{6,8},{7,9},{8,10},{9,11},{10,... | collective-permute-start | bytes 1327112 | tf_op jit(solution)/shard_map/ppermute | solution.py:307
  64.0 0.0 collective-permute-done.2.refs_2_
  64.0 4.6 %collective-permute-start.4 = (bf16[192,1152]{1,0:T(8,128)(2,1)S(1)}, bf16[192,1152]{1,0:T(8,128)(2,1)S(1)}, u32[]{:S(2)}, u32[]{:S(2)}) collective-permute-start(bf16[192,1152]{1,0:T(8,128)(2,1)S(1)} %collective-permute-done.2.refs_2_), channel_id=1, source_target_pairs={{0,14},{1,15},{2,0},{3,1},{4,2},{5,3},{6,4},{7,5},{8,6},{9,7},{10,... | collective-permute-start | bytes 1327112 | tf_op jit(solution)/shard_map/ppermute | solution.py:307
  68.6 7.2 %collective-permute-done.3.refs_3_ = bf16[192,1152]{1,0:T(8,128)(2,1)S(1)} collective-permute-done((bf16[192,1152]{1,0:T(8,128)(2,1)S(1)}, bf16[192,1152]{1,0:T(8,128)(2,1)S(1)}, u32[]{:S(2)}, u32[]{:S(2)}) %collective-permute-start.3) | collective-permute-done | bytes 442400 | tf_op jit(solution)/shard_map/ppermute | solution.py:307
  75.8 1.9 %collective-permute-start.5 = (bf16[192,1152]{1,0:T(8,128)(2,1)S(1)}, bf16[192,1152]{1,0:T(8,128)(2,1)S(1)}, u32[]{:S(2)}, u32[]{:S(2)}) collective-permute-start(bf16[192,1152]{1,0:T(8,128)(2,1)S(1)} %collective-permute-done.3.refs_3_), channel_id=1, source_target_pairs={{0,2},{1,3},{2,4},{3,5},{4,6},{5,7},{6,8},{7,9},{8,10},{9,11},{10,... | collective-permute-start | bytes 1327112 | tf_op jit(solution)/shard_map/ppermute | solution.py:307
  77.7 0.0 collective-permute-done.4.refs_4_
  77.7 4.6 %collective-permute-start.6 = (bf16[192,1152]{1,0:T(8,128)(2,1)S(1)}, bf16[192,1152]{1,0:T(8,128)(2,1)S(1)}, u32[]{:S(2)}, u32[]{:S(2)}) collective-permute-start(bf16[192,1152]{1,0:T(8,128)(2,1)S(1)} %collective-permute-done.4.refs_4_), channel_id=1, source_target_pairs={{0,14},{1,15},{2,0},{3,1},{4,2},{5,3},{6,4},{7,5},{8,6},{9,7},{10,... | collective-permute-start | bytes 1327112 | tf_op jit(solution)/shard_map/ppermute | solution.py:307
  82.3 1.5 qkv_first.1
  83.8 0.0 copy-start.2
  83.8 4.8 %collective-permute-done.5.right_ref.refs_0_ = bf16[192,1152]{1,0:T(8,128)(2,1)S(1)} collective-permute-done((bf16[192,1152]{1,0:T(8,128)(2,1)S(1)}, bf16[192,1152]{1,0:T(8,128)(2,1)S(1)}, u32[]{:S(2)}, u32[]{:S(2)}) %collective-permute-start.5) | collective-permute-done | bytes 442400 | tf_op jit(solution)/shard_map/ppermute | solution.py:307
  88.6 0.9 collective-permute-done.6.left_ref.refs_1_
  89.5 2.1 %collective-permute-start.7 = (bf16[96,1152]{1,0:T(8,128)(2,1)S(1)}, bf16[96,1152]{1,0:T(8,128)(2,1)S(1)}, u32[]{:S(2)}, u32[]{:S(2)}) collective-permute-start(bf16[96,1152]{1,0:T(8,128)(2,1)S(1)} %get-tuple-element.13), channel_id=1, source_target_pairs={{0,2},{1,3},{2,4},{3,5},{4,6},{5,7},{6,8},{7,9},{8,10},{9,11},{10,... | collective-permute-start | bytes 663560 | tf_op jit(solution)/shard_map/ppermute | solution.py:307
  91.7 5.1 %collective-permute-start.8 = (bf16[96,1152]{1,0:T(8,128)(2,1)S(1)}, bf16[96,1152]{1,0:T(8,128)(2,1)S(1)}, u32[]{:S(2)}, u32[]{:S(2)}) collective-permute-start(bf16[96,1152]{1,0:T(8,128)(2,1)S(1)} %get-tuple-element.14), channel_id=1, source_target_pairs={{0,14},{1,15},{2,0},{3,1},{4,2},{5,3},{6,4},{7,5},{8,6},{9,7},{10,... | collective-permute-start | bytes 663560 | tf_op jit(solution)/shard_map/ppermute | solution.py:307
  96.8 5.3 %collective-permute-start.9 = (bf16[5,192,256]{2,1,0:T(8,128)(2,1)S(1)}, bf16[5,192,256]{2,1,0:T(8,128)(2,1)S(1)}, u32[]{:S(2)}, u32[]{:S(2)}) collective-permute-start(bf16[5,192,256]{2,1,0:T(8,128)(2,1)S(1)} %get-tuple-element.12.refs_0_), channel_id=1, source_target_pairs={{0,1},{1,0},{2,3},{3,2},{4,5},{5,4},{6,7},{7,6},{8,9},{9,8},{10,11... | collective-permute-start | bytes 1474568 | tf_op jit(solution)/shard_map/ppermute | solution.py:319
  102.1 0.0 collective-permute-done.7.refs_2_
  102.2 0.0 collective-permute-done.8.refs_3_
  102.2 1.0 qkv_last.1
  103.1 3.4 %collective-permute-start.10 = (bf16[3,192,256]{2,1,0:T(8,128)(2,1)S(1)}, bf16[3,192,256]{2,1,0:T(8,128)(2,1)S(1)}, u32[]{:S(2)}, u32[]{:S(2)}) collective-permute-start(bf16[3,192,256]{2,1,0:T(8,128)(2,1)S(1)} %get-tuple-element.16), channel_id=1, source_target_pairs={{0,1},{1,0},{2,3},{3,2},{4,5},{5,4},{6,7},{7,6},{8,9},{9,8},{10,11... | collective-permute-start | bytes 884744 | tf_op jit(solution)/shard_map/ppermute | solution.py:319
  106.6 0.0 collective-permute-done.9.refs_2_
  106.6 1.2 collective-permute-done.10.refs_3_
  107.8 0.0 copy-done.2
  107.8 8.9 %attend.1 = bf16[16,112,128]{2,1,0:T(8,128)(2,1)S(1)} custom-call(s32[1]{0:T(128)} %bitcast.me_ref, s32[1,3072]{1,0:T(1,128)S(1)} %copy-done.2, bf16[5,192,256]{2,1,0:T(8,128)(2,1)S(1)} %get-tuple-element.11.refs_0_, bf16[3,192,256]{2,1,0:T(8,128)(2,1)S(1)} %get-tuple-element.15.refs_1_, bf16[5,192,256]{2,1,0:T(8,128)(2,1)S(1)} %collective-permute-done.9.refs_2_, ...), custom_call_target="tpu_custom_call" | custom-call | flops 1358954496 | bytes 2043908 | tf_op jit(solution)/shard_map/attend/pallas_call | solution.py:254
  116.7 22.5 %all_to_all.10.in_ref = bf16[16,112,128]{2,1,0:T(8,128)(2,1)S(1)} all-to-all(bf16[16,112,128]{2,1,0:T(8,128)(2,1)S(1)} %attend.1), channel_id=1, replica_groups=mesh['pack'=32,'seq'=16] {'seq'}, dimensions={0} | all-to-all | bytes 917504 | tf_op jit(solution)/shard_map/all_to_all | solution.py:357
  139.2 0.0 all-gather.3.cloned.1.call-done
  139.2 0.0 copy-start
  139.2 1.7 %copy-done = bf16[1152,1152]{1,0:T(8,128)(2,1)S(1)} copy-done((bf16[1152,1152]{1,0:T(8,128)(2,1)S(1)}, bf16[1152,1152]{1,0:T(8,128)(2,1)}, u32[]{:S(2)}) %copy-start) | copy-done | bytes 2654232
  140.9 1.6 %project.1 = bf16[192,1152]{1,0:T(8,128)(2,1)} custom-call(bf16[16,112,128]{2,1,0:T(8,128)(2,1)S(1)} %all_to_all.10.in_ref, bf16[16,72,1152]{2,1,0:T(8,128)(2,1)S(1)} %bitcast.7), custom_call_target="tpu_custom_call" | custom-call | flops 509607936 | bytes 3555328 | tf_op jit(solution)/shard_map/project/pallas_call | solution.py:254
  (1 shorter events, 0.0 us)
Async XLA Ops:
  6.5 132.6 %all-gather.3.cloned.1.call-start = ((), (), s32[]{:S(2)}) async-start(), calls=%async_computation.2 | async-start | bytes 2820096 | tf_op jit(solution)/shard_map/all_gather | solution.py:333
  7.3 14.0 %copy-start.1 = (bf16[3,1152,72]{1,2,0:T(8,128)(2,1)S(1)}, bf16[3,1152,72]{1,2,0:T(8,128)(2,1)}, u32[]{:S(2)}) copy-start(bf16[3,1152,72]{1,2,0:T(8,128)(2,1)} %param.8) | copy-start | bytes 1492996
  10.1 35.2 %all-to-all-start = ((bf16[32,112,128]{2,1,0:T(8,128)(2,1)}), bf16[32,112,128]{2,1,0:T(8,128)(2,1)S(1)}, u32[]{:S(2)}, u32[]{:S(2)}) async-start(bf16[32,112,128]{2,1,0:T(8,128)(2,1)} %pack_rows.1), calls=%async_computation | async-start | bytes 1835008 | tf_op jit(solution)/shard_map/all_to_all | solution.py:330
  21.2 4.6 %collective-permute-start = (bf16[216,1152]{1,0:T(8,128)(2,1)S(1)}, bf16[216,1152]{1,0:T(8,128)(2,1)S(1)}, u32[]{:S(2)}, u32[]{:S(2)}) collective-permute-start(bf16[216,1152]{1,0:T(8,128)(2,1)S(1)} %bitcast.8), channel_id=1, source_target_pairs={{0,1},{1,0},{2,3},{3,2},{4,5},{5,4},{6,7},{7,6},{8,9},{9,8},{10,11... | collective-permute-start | bytes 1493000 | tf_op jit(solution)/shard_map/ppermute | solution.py:319
  46.4 15.6 %collective-permute-start.1 = (bf16[192,1152]{1,0:T(8,128)(2,1)S(1)}, bf16[192,1152]{1,0:T(8,128)(2,1)S(1)}, u32[]{:S(2)}, u32[]{:S(2)}) collective-permute-start(bf16[192,1152]{1,0:T(8,128)(2,1)S(1)} %unpack_rows.1.refs_0_), channel_id=1, source_target_pairs={{0,2},{1,3},{2,4},{3,5},{4,6},{5,7},{6,8},{7,9},{8,10},{9,11},{10,... | collective-permute-start | bytes 1327112 | tf_op jit(solution)/shard_map/ppermute | solution.py:307
  49.6 14.3 %collective-permute-start.2 = (bf16[192,1152]{1,0:T(8,128)(2,1)S(1)}, bf16[192,1152]{1,0:T(8,128)(2,1)S(1)}, u32[]{:S(2)}, u32[]{:S(2)}) collective-permute-start(bf16[192,1152]{1,0:T(8,128)(2,1)S(1)} %unpack_rows.1.refs_0_), channel_id=1, source_target_pairs={{0,14},{1,15},{2,0},{3,1},{4,2},{5,3},{6,4},{7,5},{8,6},{9,7},{10,... | collective-permute-start | bytes 1327112 | tf_op jit(solution)/shard_map/ppermute | solution.py:307
  62.1 13.7 %collective-permute-start.3 = (bf16[192,1152]{1,0:T(8,128)(2,1)S(1)}, bf16[192,1152]{1,0:T(8,128)(2,1)S(1)}, u32[]{:S(2)}, u32[]{:S(2)}) collective-permute-start(bf16[192,1152]{1,0:T(8,128)(2,1)S(1)} %collective-permute-done.1.refs_1_), channel_id=1, source_target_pairs={{0,2},{1,3},{2,4},{3,5},{4,6},{5,7},{6,8},{7,9},{8,10},{9,11},{10,... | collective-permute-start | bytes 1327112 | tf_op jit(solution)/shard_map/ppermute | solution.py:307
  64.0 13.7 %collective-permute-start.4 = (bf16[192,1152]{1,0:T(8,128)(2,1)S(1)}, bf16[192,1152]{1,0:T(8,128)(2,1)S(1)}, u32[]{:S(2)}, u32[]{:S(2)}) collective-permute-start(bf16[192,1152]{1,0:T(8,128)(2,1)S(1)} %collective-permute-done.2.refs_2_), channel_id=1, source_target_pairs={{0,14},{1,15},{2,0},{3,1},{4,2},{5,3},{6,4},{7,5},{8,6},{9,7},{10,... | collective-permute-start | bytes 1327112 | tf_op jit(solution)/shard_map/ppermute | solution.py:307
  75.8 12.8 %collective-permute-start.5 = (bf16[192,1152]{1,0:T(8,128)(2,1)S(1)}, bf16[192,1152]{1,0:T(8,128)(2,1)S(1)}, u32[]{:S(2)}, u32[]{:S(2)}) collective-permute-start(bf16[192,1152]{1,0:T(8,128)(2,1)S(1)} %collective-permute-done.3.refs_3_), channel_id=1, source_target_pairs={{0,2},{1,3},{2,4},{3,5},{4,6},{5,7},{6,8},{7,9},{8,10},{9,11},{10,... | collective-permute-start | bytes 1327112 | tf_op jit(solution)/shard_map/ppermute | solution.py:307
  77.7 11.8 %collective-permute-start.6 = (bf16[192,1152]{1,0:T(8,128)(2,1)S(1)}, bf16[192,1152]{1,0:T(8,128)(2,1)S(1)}, u32[]{:S(2)}, u32[]{:S(2)}) collective-permute-start(bf16[192,1152]{1,0:T(8,128)(2,1)S(1)} %collective-permute-done.4.refs_4_), channel_id=1, source_target_pairs={{0,14},{1,15},{2,0},{3,1},{4,2},{5,3},{6,4},{7,5},{8,6},{9,7},{10,... | collective-permute-start | bytes 1327112 | tf_op jit(solution)/shard_map/ppermute | solution.py:307
  83.8 24.0 %copy-start.2 = (s32[1,3072]{1,0:T(1,128)S(1)}, s32[1,3072]{1,0:T(1,128)}, u32[]{:S(2)}) copy-start(s32[1,3072]{1,0:T(1,128)} %doc_ref.1) | copy-start | bytes 36868
  89.5 12.6 %collective-permute-start.7 = (bf16[96,1152]{1,0:T(8,128)(2,1)S(1)}, bf16[96,1152]{1,0:T(8,128)(2,1)S(1)}, u32[]{:S(2)}, u32[]{:S(2)}) collective-permute-start(bf16[96,1152]{1,0:T(8,128)(2,1)S(1)} %get-tuple-element.13), channel_id=1, source_target_pairs={{0,2},{1,3},{2,4},{3,5},{4,6},{5,7},{6,8},{7,9},{8,10},{9,11},{10,... | collective-permute-start | bytes 663560 | tf_op jit(solution)/shard_map/ppermute | solution.py:307
  91.7 10.5 %collective-permute-start.8 = (bf16[96,1152]{1,0:T(8,128)(2,1)S(1)}, bf16[96,1152]{1,0:T(8,128)(2,1)S(1)}, u32[]{:S(2)}, u32[]{:S(2)}) collective-permute-start(bf16[96,1152]{1,0:T(8,128)(2,1)S(1)} %get-tuple-element.14), channel_id=1, source_target_pairs={{0,14},{1,15},{2,0},{3,1},{4,2},{5,3},{6,4},{7,5},{8,6},{9,7},{10,... | collective-permute-start | bytes 663560 | tf_op jit(solution)/shard_map/ppermute | solution.py:307
  96.8 9.8 %collective-permute-start.9 = (bf16[5,192,256]{2,1,0:T(8,128)(2,1)S(1)}, bf16[5,192,256]{2,1,0:T(8,128)(2,1)S(1)}, u32[]{:S(2)}, u32[]{:S(2)}) collective-permute-start(bf16[5,192,256]{2,1,0:T(8,128)(2,1)S(1)} %get-tuple-element.12.refs_0_), channel_id=1, source_target_pairs={{0,1},{1,0},{2,3},{3,2},{4,5},{5,4},{6,7},{7,6},{8,9},{9,8},{10,11... | collective-permute-start | bytes 1474568 | tf_op jit(solution)/shard_map/ppermute | solution.py:319
  103.1 4.6 %collective-permute-start.10 = (bf16[3,192,256]{2,1,0:T(8,128)(2,1)S(1)}, bf16[3,192,256]{2,1,0:T(8,128)(2,1)S(1)}, u32[]{:S(2)}, u32[]{:S(2)}) collective-permute-start(bf16[3,192,256]{2,1,0:T(8,128)(2,1)S(1)} %get-tuple-element.16), channel_id=1, source_target_pairs={{0,1},{1,0},{2,3},{3,2},{4,5},{5,4},{6,7},{7,6},{8,9},{9,8},{10,11... | collective-permute-start | bytes 884744 | tf_op jit(solution)/shard_map/ppermute | solution.py:319
  139.2 1.8 %copy-start = (bf16[1152,1152]{1,0:T(8,128)(2,1)S(1)}, bf16[1152,1152]{1,0:T(8,128)(2,1)}, u32[]{:S(2)}) copy-start(bf16[1152,1152]{1,0:T(8,128)(2,1)} %all-gather.3.cloned.1.call-done) | copy-start | bytes 7962628
Sparse Core Ops, SparseCore 0:
  9.5 46.9 all-gather.2

commit v9 on v8

--- a/solution.py
+++ b/solution.py
@@ -294,11 +294,16 @@
     )
 
 
-def halves_kernel(right_ref, left_ref, *refs):
-    *_, top_ref, bottom_ref = refs
-    half = top_ref.shape[0]
-    top_ref[...] = right_ref[0:half, :]
-    bottom_ref[...] = left_ref[half:, :]
+def pick_kernel(me_ref, right_ref, left_ref, *refs):
+    out_ref = refs[-1]
+
+    @pl.when((me_ref[0] & 1) == 0)
+    def _():
+        out_ref[...] = right_ref[...]
+
+    @pl.when((me_ref[0] & 1) == 1)
+    def _():
+        out_ref[...] = left_ref[...]
 
 
 def ring_step(right, left, n_seq):
@@ -346,11 +351,19 @@
         right, left = ring_step(right, left, n_seq)
         held += [right, left]
     mine, theirs = project_qkv(held[:5], w_t, pair_w, "qkv_first")
-    half = shape((TOK // 2, width), BF)
-    top, bottom = local_call(
-        halves_kernel, (half, half), right, left, behind=(theirs,), name="halves", flops=0
-    )
-    held += ring_step(top, bottom, n_seq)
+    picked = local_call(
+        pick_kernel,
+        shape((TOK, width), BF),
+        me,
+        right,
+        left,
+        small=1,
+        behind=(theirs,),
+        name="pick",
+        flops=0,
+    )
+    ways = [(i, (i + 2 - 4 * (i % 2)) % n_seq) for i in range(n_seq)]
+    held.append(lax.ppermute(picked, "seq", ways))
     last_mine, last_theirs = project_qkv(held[5:], w_t, pair_w, "qkv_last")
     ours = [mine, last_mine, other_core(theirs), other_core(last_theirs)]
     attended = attend_call(me, doc_ids, n_seq, *ours)

time: 150 us -> 156 us (1.040)
  the two profiles are of different devices: /device:TPU:135 before, /device:TPU:67 now
where the time goes in v9:
time: 156 us
  starting transfers between devices  52.8 us (34%)
  waiting for transfers between devices  45.2 us (29%)
  blocking collectives  23.7 us (15%)
  Pallas kernels  18.6 us (12%)
  between operations  13.6 us (9%)
  local copies, waits for them, and re-layouts  1.76 us (1%)
    all_to_all x1, blocking collectives, body(): lax.all_to_all(attended, 'seq', split_axis=0, concat_axis=0, tiled=True)  23.7 us
    ppermute x6, waiting for transfers between devices, ring_step(): return (lax.ppermute(right, 'seq', up), lax.ppermute(left, 'seq', down))  22.9 us
    ppermute x6, starting transfers between devices, ring_step(): return (lax.ppermute(right, 'seq', up), lax.ppermute(left, 'seq', down))  19.9 us
    pallas_call x7, Pallas kernels, local_call(): pl.pallas_call(kernel, out_shape=out_shape, in_specs=[smem] * small + [vm...  18.6 us
    all_to_all x1, waiting for transfers between devices, body(): lax.all_to_all(outbox, 'pack', split_axis=0, concat_axis=0, tiled=True)  18.5 us
    ppermute x3, starting transfers between devices, other_core(): return lax.ppermute(x, 'seq', [(i, i ^ 1) for i in range(n_seq)])  15.7 us
    all_to_all x1, starting transfers between devices, body(): lax.all_to_all(outbox, 'pack', split_axis=0, concat_axis=0, tiled=True)  12 us
    ppermute x1, starting transfers between devices, body(): held.append(lax.ppermute(picked, 'seq', ways))  5.21 us
  transfers between devices with their start and end apart: 12, of which 9 were waited for; matrix products, arithmetic and copies ran while one was open for 0% of the time, Pallas kernels for 9%

profile of v9, /device:TPU:67, one launch (start us, length us, event | category | flops | bytes accessed | tf_op | source)
XLA Modules:
  0.0 155.7 jit_solution(14604423313476051485)
XLA Ops:
  6.5 0.0 copy-start.1
  6.5 2.9 %pack_rows.1 = bf16[32,112,128]{2,1,0:T(8,128)(2,1)} custom-call(s32[1,192]{1,0:T(1,128)} %dest_ref.1, bf16[192,1152]{1,0:T(8,128)(2,1)} %bitcast.11), custom_call_target="tpu_custom_call" | custom-call | flops 1000000000 | bytes 1360640 | tf_op jit(solution)/shard_map/pack_rows/pallas_call | solution.py:254
  9.4 12.0 %all-to-all-start = ((bf16[32,112,128]{2,1,0:T(8,128)(2,1)}), bf16[32,112,128]{2,1,0:T(8,128)(2,1)S(1)}, u32[]{:S(2)}, u32[]{:S(2)}) async-start(bf16[32,112,128]{2,1,0:T(8,128)(2,1)} %pack_rows.1), calls=%async_computation | async-start | bytes 1835008 | tf_op jit(solution)/shard_map/all_to_all | solution.py:335
  21.4 0.0 all-gather.3.cloned.1.call-start
  21.5 0.7 all-gather.3.cloned.1.call-update
  22.2 0.0 copy-done.1
  22.2 3.1 %collective-permute-start = (bf16[216,1152]{1,0:T(8,128)(2,1)S(1)}, bf16[216,1152]{1,0:T(8,128)(2,1)S(1)}, u32[]{:S(2)}, u32[]{:S(2)}) collective-permute-start(bf16[216,1152]{1,0:T(8,128)(2,1)S(1)} %bitcast.8), channel_id=1, source_target_pairs={{0,1},{1,0},{2,3},{3,2},{4,5},{5,4},{6,7},{7,6},{8,9},{9,8},{10,11... | collective-permute-start | bytes 1493000 | tf_op jit(solution)/shard_map/ppermute | solution.py:324
  25.3 1.5 collective-permute-done.refs_0_.refs_6_.refs_4_
  26.8 18.5 %all-to-all-done.in_ref = bf16[32,112,128]{2,1,0:T(8,128)(2,1)S(1)} async-done(((bf16[32,112,128]{2,1,0:T(8,128)(2,1)}), bf16[32,112,128]{2,1,0:T(8,128)(2,1)S(1)}, u32[]{:S(2)}, u32[]{:S(2)}) %all-to-all-start) | async-done | bytes 917536 | tf_op jit(solution)/shard_map/all_to_all | solution.py:335
  45.3 1.1 unpack_rows.1.refs_0_
  46.5 3.2 %collective-permute-start.1 = (bf16[192,1152]{1,0:T(8,128)(2,1)S(1)}, bf16[192,1152]{1,0:T(8,128)(2,1)S(1)}, u32[]{:S(2)}, u32[]{:S(2)}) collective-permute-start(bf16[192,1152]{1,0:T(8,128)(2,1)S(1)} %unpack_rows.1.refs_0_), channel_id=1, source_target_pairs={{0,2},{1,3},{2,4},{3,5},{4,6},{5,7},{6,8},{7,9},{8,10},{9,11},{10,... | collective-permute-start | bytes 1327112 | tf_op jit(solution)/shard_map/ppermute | solution.py:312
  49.7 3.8 %collective-permute-start.2 = (bf16[192,1152]{1,0:T(8,128)(2,1)S(1)}, bf16[192,1152]{1,0:T(8,128)(2,1)S(1)}, u32[]{:S(2)}, u32[]{:S(2)}) collective-permute-start(bf16[192,1152]{1,0:T(8,128)(2,1)S(1)} %unpack_rows.1.refs_0_), channel_id=1, source_target_pairs={{0,14},{1,15},{2,0},{3,1},{4,2},{5,3},{6,4},{7,5},{8,6},{9,7},{10,... | collective-permute-start | bytes 1327112 | tf_op jit(solution)/shard_map/ppermute | solution.py:312
  53.5 13.4 %collective-permute-done.1.refs_1_ = bf16[192,1152]{1,0:T(8,128)(2,1)S(1)} collective-permute-done((bf16[192,1152]{1,0:T(8,128)(2,1)S(1)}, bf16[192,1152]{1,0:T(8,128)(2,1)S(1)}, u32[]{:S(2)}, u32[]{:S(2)}) %collective-permute-start.1) | collective-permute-done | bytes 442400 | tf_op jit(solution)/shard_map/ppermute | solution.py:312
  66.9 2.0 %collective-permute-start.3 = (bf16[192,1152]{1,0:T(8,128)(2,1)S(1)}, bf16[192,1152]{1,0:T(8,128)(2,1)}, u32[]{:S(2)}, u32[]{:S(2)}) collective-permute-start(bf16[192,1152]{1,0:T(8,128)(2,1)S(1)} %collective-permute-done.1.refs_1_), channel_id=1, source_target_pairs={{0,2},{1,3},{2,4},{3,5},{4,6},{5,7},{6,8},{7,9},{8,10},{9,11},{10,... | collective-permute-start | bytes 1327112 | tf_op jit(solution)/shard_map/ppermute | solution.py:312
  69.0 0.1 collective-permute-done.2.refs_2_
  69.0 4.4 %collective-permute-start.4 = (bf16[192,1152]{1,0:T(8,128)(2,1)S(1)}, bf16[192,1152]{1,0:T(8,128)(2,1)}, u32[]{:S(2)}, u32[]{:S(2)}) collective-permute-start(bf16[192,1152]{1,0:T(8,128)(2,1)S(1)} %collective-permute-done.2.refs_2_), channel_id=1, source_target_pairs={{0,14},{1,15},{2,0},{3,1},{4,2},{5,3},{6,4},{7,5},{8,6},{9,7},{10,... | collective-permute-start | bytes 1327112 | tf_op jit(solution)/shard_map/ppermute | solution.py:312
  73.4 5.9 %collective-permute-done.3.refs_3_ = bf16[192,1152]{1,0:T(8,128)(2,1)} collective-permute-done((bf16[192,1152]{1,0:T(8,128)(2,1)S(1)}, bf16[192,1152]{1,0:T(8,128)(2,1)}, u32[]{:S(2)}, u32[]{:S(2)}) %collective-permute-start.3) | collective-permute-done | bytes 442400 | tf_op jit(solution)/shard_map/ppermute | solution.py:312
  79.3 1.9 %collective-permute-start.5 = (bf16[192,1152]{1,0:T(8,128)(2,1)}, bf16[192,1152]{1,0:T(8,128)(2,1)S(1)}, u32[]{:S(2)}, u32[]{:S(2)}) collective-permute-start(bf16[192,1152]{1,0:T(8,128)(2,1)} %collective-permute-done.3.refs_3_), channel_id=1, source_target_pairs={{0,2},{1,3},{2,4},{3,5},{4,6},{5,7},{6,8},{7,9},{8,10},{9,11},{10,... | collective-permute-start | bytes 1327112 | tf_op jit(solution)/shard_map/ppermute | solution.py:312
  81.2 0.0 collective-permute-done.4.refs_4_
  81.2 4.6 %collective-permute-start.6 = (bf16[192,1152]{1,0:T(8,128)(2,1)}, bf16[192,1152]{1,0:T(8,128)(2,1)S(1)}, u32[]{:S(2)}, u32[]{:S(2)}) collective-permute-start(bf16[192,1152]{1,0:T(8,128)(2,1)} %collective-permute-done.4.refs_4_), channel_id=1, source_target_pairs={{0,14},{1,15},{2,0},{3,1},{4,2},{5,3},{6,4},{7,5},{8,6},{9,7},{10,... | collective-permute-start | bytes 1327112 | tf_op jit(solution)/shard_map/ppermute | solution.py:312
  85.8 2.6 %qkv_first.1 = (bf16[5,192,256]{2,1,0:T(8,128)(2,1)S(1)}, bf16[5,192,256]{2,1,0:T(8,128)(2,1)S(1)}) custom-call(bf16[192,1152]{1,0:T(8,128)(2,1)S(1)} %unpack_rows.1.refs_0_, bf16[192,1152]{1,0:T(8,128)(2,1)S(1)} %collective-permute-done.1.refs_1_, bf16[192,1152]{1,0:T(8,128)(2,1)S(1)} %collective-permute-done.2.refs_2_, ...), custom_call_target="tpu_custom_call" | custom-call | flops 955514880 | bytes 4190208 | tf_op jit(solution)/shard_map/qkv_first/pallas_call | solution.py:254
  88.4 0.0 copy-start.2
  88.5 2.5 %collective-permute-done.5.right_ref.refs_0_ = bf16[192,1152]{1,0:T(8,128)(2,1)S(1)} collective-permute-done((bf16[192,1152]{1,0:T(8,128)(2,1)}, bf16[192,1152]{1,0:T(8,128)(2,1)S(1)}, u32[]{:S(2)}, u32[]{:S(2)}) %collective-permute-start.5) | collective-permute-done | bytes 442400 | tf_op jit(solution)/shard_map/ppermute | solution.py:312
  90.9 1.0 collective-permute-done.6.left_ref.refs_1_
  92.0 5.2 %collective-permute-start.7 = (bf16[192,1152]{1,0:T(8,128)(2,1)S(1)}, bf16[192,1152]{1,0:T(8,128)(2,1)S(1)}, u32[]{:S(2)}, u32[]{:S(2)}) collective-permute-start(bf16[192,1152]{1,0:T(8,128)(2,1)S(1)} %pick.1), channel_id=1, source_target_pairs={{0,2},{1,15},{2,4},{3,1},{4,6},{5,3},{6,8},{7,5},{8,10},{9,7},{10,... | collective-permute-start | bytes 1327112 | tf_op jit(solution)/shard_map/ppermute | solution.py:366
  97.2 5.6 %collective-permute-start.8 = (bf16[5,192,256]{2,1,0:T(8,128)(2,1)S(1)}, bf16[5,192,256]{2,1,0:T(8,128)(2,1)S(1)}, u32[]{:S(2)}, u32[]{:S(2)}) collective-permute-start(bf16[5,192,256]{2,1,0:T(8,128)(2,1)S(1)} %get-tuple-element.10.refs_0_), channel_id=1, source_target_pairs={{0,1},{1,0},{2,3},{3,2},{4,5},{5,4},{6,7},{7,6},{8,9},{9,8},{10,11... | collective-permute-start | bytes 1474568 | tf_op jit(solution)/shard_map/ppermute | solution.py:324
  102.8 0.5 collective-permute-done.7.refs_2_
  103.3 1.0 qkv_last.1
  104.3 6.9 %collective-permute-start.9 = (bf16[3,192,256]{2,1,0:T(8,128)(2,1)S(1)}, bf16[3,192,256]{2,1,0:T(8,128)(2,1)S(1)}, u32[]{:S(2)}, u32[]{:S(2)}) collective-permute-start(bf16[3,192,256]{2,1,0:T(8,128)(2,1)S(1)} %get-tuple-element.12), channel_id=1, source_target_pairs={{0,1},{1,0},{2,3},{3,2},{4,5},{5,4},{6,7},{7,6},{8,9},{9,8},{10,11... | collective-permute-start | bytes 884744 | tf_op jit(solution)/shard_map/ppermute | solution.py:324
  111.2 0.0 collective-permute-done.8.refs_2_
  111.2 1.2 collective-permute-done.9.refs_3_
  112.4 0.0 copy-done.2
  112.4 9.4 %attend.1 = bf16[16,112,128]{2,1,0:T(8,128)(2,1)S(1)} custom-call(s32[1]{0:T(128)} %bitcast.me_ref, s32[1,3072]{1,0:T(1,128)S(1)} %copy-done.2, bf16[5,192,256]{2,1,0:T(8,128)(2,1)S(1)} %get-tuple-element.9.refs_0_, bf16[3,192,256]{2,1,0:T(8,128)(2,1)S(1)} %get-tuple-element.11.refs_1_, bf16[5,192,256]{2,1,0:T(8,128)(2,1)S(1)} %collective-permute-done.8.refs_2_, ...), custom_call_target="tpu_custom_call" | custom-call | flops 1358954496 | bytes 2043908 | tf_op jit(solution)/shard_map/attend/pallas_call | solution.py:254
  121.8 23.7 %all_to_all.10.in_ref = bf16[16,112,128]{2,1,0:T(8,128)(2,1)S(1)} all-to-all(bf16[16,112,128]{2,1,0:T(8,128)(2,1)S(1)} %attend.1), channel_id=1, replica_groups=mesh['pack'=32,'seq'=16] {'seq'}, dimensions={0} | all-to-all | bytes 917504 | tf_op jit(solution)/shard_map/all_to_all | solution.py:370
  145.5 0.0 all-gather.3.cloned.1.call-done
  145.5 0.0 copy-start
  145.5 1.7 %copy-done = bf16[1152,1152]{1,0:T(8,128)(2,1)S(1)} copy-done((bf16[1152,1152]{1,0:T(8,128)(2,1)S(1)}, bf16[1152,1152]{1,0:T(8,128)(2,1)}, u32[]{:S(2)}) %copy-start) | copy-done | bytes 2654232
  147.3 1.6 %project.1 = bf16[192,1152]{1,0:T(8,128)(2,1)} custom-call(bf16[16,112,128]{2,1,0:T(8,128)(2,1)S(1)} %all_to_all.10.in_ref, bf16[16,72,1152]{2,1,0:T(8,128)(2,1)S(1)} %bitcast.7), custom_call_target="tpu_custom_call" | custom-call | flops 509607936 | bytes 3555328 | tf_op jit(solution)/shard_map/project/pallas_call | solution.py:254
  (1 shorter events, 0.0 us)
Async XLA Ops:
  6.5 15.6 %copy-start.1 = (bf16[3,1152,72]{1,2,0:T(8,128)(2,1)S(1)}, bf16[3,1152,72]{1,2,0:T(8,128)(2,1)}, u32[]{:S(2)}) copy-start(bf16[3,1152,72]{1,2,0:T(8,128)(2,1)} %param.8) | copy-start | bytes 1492996
  9.4 35.9 %all-to-all-start = ((bf16[32,112,128]{2,1,0:T(8,128)(2,1)}), bf16[32,112,128]{2,1,0:T(8,128)(2,1)S(1)}, u32[]{:S(2)}, u32[]{:S(2)}) async-start(bf16[32,112,128]{2,1,0:T(8,128)(2,1)} %pack_rows.1), calls=%async_computation | async-start | bytes 1835008 | tf_op jit(solution)/shard_map/all_to_all | solution.py:335
  21.4 124.1 %all-gather.3.cloned.1.call-start = ((), (), s32[]{:S(2)}) async-start(), calls=%async_computation.2 | async-start | bytes 2820096 | tf_op jit(solution)/shard_map/all_gather | solution.py:338
  22.2 4.6 %collective-permute-start = (bf16[216,1152]{1,0:T(8,128)(2,1)S(1)}, bf16[216,1152]{1,0:T(8,128)(2,1)S(1)}, u32[]{:S(2)}, u32[]{:S(2)}) collective-permute-start(bf16[216,1152]{1,0:T(8,128)(2,1)S(1)} %bitcast.8), channel_id=1, source_target_pairs={{0,1},{1,0},{2,3},{3,2},{4,5},{5,4},{6,7},{7,6},{8,9},{9,8},{10,11... | collective-permute-start | bytes 1493000 | tf_op jit(solution)/shard_map/ppermute | solution.py:324
  46.5 20.4 %collective-permute-start.1 = (bf16[192,1152]{1,0:T(8,128)(2,1)S(1)}, bf16[192,1152]{1,0:T(8,128)(2,1)S(1)}, u32[]{:S(2)}, u32[]{:S(2)}) collective-permute-start(bf16[192,1152]{1,0:T(8,128)(2,1)S(1)} %unpack_rows.1.refs_0_), channel_id=1, source_target_pairs={{0,2},{1,3},{2,4},{3,5},{4,6},{5,7},{6,8},{7,9},{8,10},{9,11},{10,... | collective-permute-start | bytes 1327112 | tf_op jit(solution)/shard_map/ppermute | solution.py:312
  49.7 19.4 %collective-permute-start.2 = (bf16[192,1152]{1,0:T(8,128)(2,1)S(1)}, bf16[192,1152]{1,0:T(8,128)(2,1)S(1)}, u32[]{:S(2)}, u32[]{:S(2)}) collective-permute-start(bf16[192,1152]{1,0:T(8,128)(2,1)S(1)} %unpack_rows.1.refs_0_), channel_id=1, source_target_pairs={{0,14},{1,15},{2,0},{3,1},{4,2},{5,3},{6,4},{7,5},{8,6},{9,7},{10,... | collective-permute-start | bytes 1327112 | tf_op jit(solution)/shard_map/ppermute | solution.py:312
  66.9 12.4 %collective-permute-start.3 = (bf16[192,1152]{1,0:T(8,128)(2,1)S(1)}, bf16[192,1152]{1,0:T(8,128)(2,1)}, u32[]{:S(2)}, u32[]{:S(2)}) collective-permute-start(bf16[192,1152]{1,0:T(8,128)(2,1)S(1)} %collective-permute-done.1.refs_1_), channel_id=1, source_target_pairs={{0,2},{1,3},{2,4},{3,5},{4,6},{5,7},{6,8},{7,9},{8,10},{9,11},{10,... | collective-permute-start | bytes 1327112 | tf_op jit(solution)/shard_map/ppermute | solution.py:312
  69.0 12.2 %collective-permute-start.4 = (bf16[192,1152]{1,0:T(8,128)(2,1)S(1)}, bf16[192,1152]{1,0:T(8,128)(2,1)}, u32[]{:S(2)}, u32[]{:S(2)}) collective-permute-start(bf16[192,1152]{1,0:T(8,128)(2,1)S(1)} %collective-permute-done.2.refs_2_), channel_id=1, source_target_pairs={{0,14},{1,15},{2,0},{3,1},{4,2},{5,3},{6,4},{7,5},{8,6},{9,7},{10,... | collective-permute-start | bytes 1327112 | tf_op jit(solution)/shard_map/ppermute | solution.py:312
  79.3 11.6 %collective-permute-start.5 = (bf16[192,1152]{1,0:T(8,128)(2,1)}, bf16[192,1152]{1,0:T(8,128)(2,1)S(1)}, u32[]{:S(2)}, u32[]{:S(2)}) collective-permute-start(bf16[192,1152]{1,0:T(8,128)(2,1)} %collective-permute-done.3.refs_3_), channel_id=1, source_target_pairs={{0,2},{1,3},{2,4},{3,5},{4,6},{5,7},{6,8},{7,9},{8,10},{9,11},{10,... | collective-permute-start | bytes 1327112 | tf_op jit(solution)/shard_map/ppermute | solution.py:312
  81.2 10.7 %collective-permute-start.6 = (bf16[192,1152]{1,0:T(8,128)(2,1)}, bf16[192,1152]{1,0:T(8,128)(2,1)S(1)}, u32[]{:S(2)}, u32[]{:S(2)}) collective-permute-start(bf16[192,1152]{1,0:T(8,128)(2,1)} %collective-permute-done.4.refs_4_), channel_id=1, source_target_pairs={{0,14},{1,15},{2,0},{3,1},{4,2},{5,3},{6,4},{7,5},{8,6},{9,7},{10,... | collective-permute-start | bytes 1327112 | tf_op jit(solution)/shard_map/ppermute | solution.py:312
  88.4 23.9 %copy-start.2 = (s32[1,3072]{1,0:T(1,128)S(1)}, s32[1,3072]{1,0:T(1,128)}, u32[]{:S(2)}) copy-start(s32[1,3072]{1,0:T(1,128)} %doc_ref.1) | copy-start | bytes 36868
  92.0 11.3 %collective-permute-start.7 = (bf16[192,1152]{1,0:T(8,128)(2,1)S(1)}, bf16[192,1152]{1,0:T(8,128)(2,1)S(1)}, u32[]{:S(2)}, u32[]{:S(2)}) collective-permute-start(bf16[192,1152]{1,0:T(8,128)(2,1)S(1)} %pick.1), channel_id=1, source_target_pairs={{0,2},{1,15},{2,4},{3,1},{4,6},{5,3},{6,8},{7,5},{8,10},{9,7},{10,... | collective-permute-start | bytes 1327112 | tf_op jit(solution)/shard_map/ppermute | solution.py:366
  97.2 14.0 %collective-permute-start.8 = (bf16[5,192,256]{2,1,0:T(8,128)(2,1)S(1)}, bf16[5,192,256]{2,1,0:T(8,128)(2,1)S(1)}, u32[]{:S(2)}, u32[]{:S(2)}) collective-permute-start(bf16[5,192,256]{2,1,0:T(8,128)(2,1)S(1)} %get-tuple-element.10.refs_0_), channel_id=1, source_target_pairs={{0,1},{1,0},{2,3},{3,2},{4,5},{5,4},{6,7},{7,6},{8,9},{9,8},{10,11... | collective-permute-start | bytes 1474568 | tf_op jit(solution)/shard_map/ppermute | solution.py:324
  104.3 8.1 %collective-permute-start.9 = (bf16[3,192,256]{2,1,0:T(8,128)(2,1)S(1)}, bf16[3,192,256]{2,1,0:T(8,128)(2,1)S(1)}, u32[]{:S(2)}, u32[]{:S(2)}) collective-permute-start(bf16[3,192,256]{2,1,0:T(8,128)(2,1)S(1)} %get-tuple-element.12), channel_id=1, source_target_pairs={{0,1},{1,0},{2,3},{3,2},{4,5},{5,4},{6,7},{7,6},{8,9},{9,8},{10,11... | collective-permute-start | bytes 884744 | tf_op jit(solution)/shard_map/ppermute | solution.py:324
  145.5 1.8 %copy-start = (bf16[1152,1152]{1,0:T(8,128)(2,1)S(1)}, bf16[1152,1152]{1,0:T(8,128)(2,1)}, u32[]{:S(2)}) copy-start(bf16[1152,1152]{1,0:T(8,128)(2,1)} %all-gather.3.cloned.1.call-done) | copy-start | bytes 7962628
Sparse Core Ops, SparseCore 0:
  24.4 46.7 all-gather.2

commit v10 on v9

--- a/solution.py
+++ b/solution.py
@@ -358,7 +358,7 @@
         right,
         left,
         small=1,
-        behind=(theirs,),
+        behind=(theirs, w_all[0, 0:16, 0:LANES]),
         name="pick",
         flops=0,
     )

time: 156 us -> 150 us (0.962)
  the two profiles are of different devices: /device:TPU:67 before, /device:TPU:7 now
where the time goes in v10:
time: 150 us
  starting transfers between devices  54.3 us (36%)
  waiting for transfers between devices  32.2 us (21%)
  Pallas kernels  24.4 us (16%)
  blocking collectives  21.9 us (15%)
  between operations  13.6 us (9%)
  local copies, waits for them, and re-layouts  3.28 us (2%)
    pallas_call x7, Pallas kernels, local_call(): pl.pallas_call(kernel, out_shape=out_shape, in_specs=[smem] * small + [vm...  24.4 us
    all_to_all x1, blocking collectives, body(): lax.all_to_all(attended, 'seq', split_axis=0, concat_axis=0, tiled=True)  21.9 us
    ppermute x6, starting transfers between devices, ring_step(): return (lax.ppermute(right, 'seq', up), lax.ppermute(left, 'seq', down))  20 us
    ppermute x3, starting transfers between devices, other_core(): return lax.ppermute(x, 'seq', [(i, i ^ 1) for i in range(n_seq)])  16.5 us
    all_to_all x1, waiting for transfers between devices, body(): lax.all_to_all(outbox, 'pack', split_axis=0, concat_axis=0, tiled=True)  16.3 us
    all_to_all x1, starting transfers between devices, body(): lax.all_to_all(outbox, 'pack', split_axis=0, concat_axis=0, tiled=True)  12.9 us
    ppermute x6, waiting for transfers between devices, ring_step(): return (lax.ppermute(right, 'seq', up), lax.ppermute(left, 'seq', down))  11.7 us
    ppermute x1, starting transfers between devices, body(): held.append(lax.ppermute(picked, 'seq', ways))  4.92 us
  transfers between devices with their start and end apart: 12, of which 7 were waited for; matrix products, arithmetic and copies ran while one was open for 0% of the time, Pallas kernels for 5%

profile of v10, /device:TPU:7, one launch (start us, length us, event | category | flops | bytes accessed | tf_op | source)
XLA Modules:
  0.0 149.6 jit_solution(4896519930109017105)
XLA Ops:
  6.5 0.0 all-gather.3.cloned.1.call-start
  6.5 0.7 all-gather.3.cloned.1.call-update
  7.3 0.0 copy-start.1
  7.3 2.9 %pack_rows.1 = bf16[32,112,128]{2,1,0:T(8,128)(2,1)} custom-call(s32[1,192]{1,0:T(1,128)} %dest_ref.1, bf16[192,1152]{1,0:T(8,128)(2,1)} %bitcast.14), custom_call_target="tpu_custom_call" | custom-call | flops 1000000000 | bytes 1360640 | tf_op jit(solution)/shard_map/pack_rows/pallas_call | solution.py:254
  10.1 12.9 %all-to-all-start = ((bf16[32,112,128]{2,1,0:T(8,128)(2,1)}), bf16[32,112,128]{2,1,0:T(8,128)(2,1)S(1)}, u32[]{:S(2)}, u32[]{:S(2)}) async-start(bf16[32,112,128]{2,1,0:T(8,128)(2,1)} %pack_rows.1), calls=%async_computation | async-start | bytes 1835008 | tf_op jit(solution)/shard_map/all_to_all | solution.py:335
  23.0 0.0 copy-done.1
  23.0 3.1 %collective-permute-start = (bf16[216,1152]{1,0:T(8,128)(2,1)S(1)}, bf16[216,1152]{1,0:T(8,128)(2,1)S(1)}, u32[]{:S(2)}, u32[]{:S(2)}) collective-permute-start(bf16[216,1152]{1,0:T(8,128)(2,1)S(1)} %bitcast.11), channel_id=1, source_target_pairs={{0,1},{1,0},{2,3},{3,2},{4,5},{5,4},{6,7},{7,6},{8,9},{9,8},{10,11... | collective-permute-start | bytes 1493000 | tf_op jit(solution)/shard_map/ppermute | solution.py:324
  26.2 1.5 collective-permute-done.refs_0_.refs_6_.refs_4_
  27.7 16.3 %all-to-all-done.in_ref = bf16[32,112,128]{2,1,0:T(8,128)(2,1)S(1)} async-done(((bf16[32,112,128]{2,1,0:T(8,128)(2,1)}), bf16[32,112,128]{2,1,0:T(8,128)(2,1)S(1)}, u32[]{:S(2)}, u32[]{:S(2)}) %all-to-all-start) | async-done | bytes 917536 | tf_op jit(solution)/shard_map/all_to_all | solution.py:335
  44.0 1.1 unpack_rows.1.refs_0_
  45.1 3.2 %collective-permute-start.1 = (bf16[192,1152]{1,0:T(8,128)(2,1)S(1)}, bf16[192,1152]{1,0:T(8,128)(2,1)S(1)}, u32[]{:S(2)}, u32[]{:S(2)}) collective-permute-start(bf16[192,1152]{1,0:T(8,128)(2,1)S(1)} %unpack_rows.1.refs_0_), channel_id=1, source_target_pairs={{0,2},{1,3},{2,4},{3,5},{4,6},{5,7},{6,8},{7,9},{8,10},{9,11},{10,... | collective-permute-start | bytes 1327112 | tf_op jit(solution)/shard_map/ppermute | solution.py:312
  48.3 3.8 %collective-permute-start.2 = (bf16[192,1152]{1,0:T(8,128)(2,1)S(1)}, bf16[192,1152]{1,0:T(8,128)(2,1)S(1)}, u32[]{:S(2)}, u32[]{:S(2)}) collective-permute-start(bf16[192,1152]{1,0:T(8,128)(2,1)S(1)} %unpack_rows.1.refs_0_), channel_id=1, source_target_pairs={{0,14},{1,15},{2,0},{3,1},{4,2},{5,3},{6,4},{7,5},{8,6},{9,7},{10,... | collective-permute-start | bytes 1327112 | tf_op jit(solution)/shard_map/ppermute | solution.py:312
  52.1 7.1 %collective-permute-done.1.refs_1_ = bf16[192,1152]{1,0:T(8,128)(2,1)S(1)} collective-permute-done((bf16[192,1152]{1,0:T(8,128)(2,1)S(1)}, bf16[192,1152]{1,0:T(8,128)(2,1)S(1)}, u32[]{:S(2)}, u32[]{:S(2)}) %collective-permute-start.1) | collective-permute-done | bytes 442400 | tf_op jit(solution)/shard_map/ppermute | solution.py:312
  59.2 2.2 %collective-permute-start.3 = (bf16[192,1152]{1,0:T(8,128)(2,1)S(1)}, bf16[192,1152]{1,0:T(8,128)(2,1)}, u32[]{:S(2)}, u32[]{:S(2)}) collective-permute-start(bf16[192,1152]{1,0:T(8,128)(2,1)S(1)} %collective-permute-done.1.refs_1_), channel_id=1, source_target_pairs={{0,2},{1,3},{2,4},{3,5},{4,6},{5,7},{6,8},{7,9},{8,10},{9,11},{10,... | collective-permute-start | bytes 1327112 | tf_op jit(solution)/shard_map/ppermute | solution.py:312
  61.4 0.0 collective-permute-done.2.refs_2_
  61.4 4.3 %collective-permute-start.4 = (bf16[192,1152]{1,0:T(8,128)(2,1)S(1)}, bf16[192,1152]{1,0:T(8,128)(2,1)}, u32[]{:S(2)}, u32[]{:S(2)}) collective-permute-start(bf16[192,1152]{1,0:T(8,128)(2,1)S(1)} %collective-permute-done.2.refs_2_), channel_id=1, source_target_pairs={{0,14},{1,15},{2,0},{3,1},{4,2},{5,3},{6,4},{7,5},{8,6},{9,7},{10,... | collective-permute-start | bytes 1327112 | tf_op jit(solution)/shard_map/ppermute | solution.py:312
  65.7 0.0 copy-start.2
  65.7 0.8 copy-done.2
  66.5 4.2 %collective-permute-done.3.refs_3_ = bf16[192,1152]{1,0:T(8,128)(2,1)} collective-permute-done((bf16[192,1152]{1,0:T(8,128)(2,1)S(1)}, bf16[192,1152]{1,0:T(8,128)(2,1)}, u32[]{:S(2)}, u32[]{:S(2)}) %collective-permute-start.3) | collective-permute-done | bytes 442400 | tf_op jit(solution)/shard_map/ppermute | solution.py:312
  70.7 1.9 %collective-permute-start.5 = (bf16[192,1152]{1,0:T(8,128)(2,1)}, bf16[192,1152]{1,0:T(8,128)(2,1)S(1)}, u32[]{:S(2)}, u32[]{:S(2)}) collective-permute-start(bf16[192,1152]{1,0:T(8,128)(2,1)} %collective-permute-done.3.refs_3_), channel_id=1, source_target_pairs={{0,2},{1,3},{2,4},{3,5},{4,6},{5,7},{6,8},{7,9},{8,10},{9,11},{10,... | collective-permute-start | bytes 1327112 | tf_op jit(solution)/shard_map/ppermute | solution.py:312
  72.6 0.0 collective-permute-done.4.refs_4_
  72.6 4.6 %collective-permute-start.6 = (bf16[192,1152]{1,0:T(8,128)(2,1)}, bf16[192,1152]{1,0:T(8,128)(2,1)S(1)}, u32[]{:S(2)}, u32[]{:S(2)}) collective-permute-start(bf16[192,1152]{1,0:T(8,128)(2,1)} %collective-permute-done.4.refs_4_), channel_id=1, source_target_pairs={{0,14},{1,15},{2,0},{3,1},{4,2},{5,3},{6,4},{7,5},{8,6},{9,7},{10,... | collective-permute-start | bytes 1327112 | tf_op jit(solution)/shard_map/ppermute | solution.py:312
  77.2 0.0 copy-start.3
  77.2 1.0 copy-done.3
  78.2 2.6 %qkv_first.1 = (bf16[5,192,256]{2,1,0:T(8,128)(2,1)S(1)}, bf16[5,192,256]{2,1,0:T(8,128)(2,1)S(1)}) custom-call(bf16[192,1152]{1,0:T(8,128)(2,1)S(1)} %unpack_rows.1.refs_0_, bf16[192,1152]{1,0:T(8,128)(2,1)S(1)} %collective-permute-done.1.refs_1_, bf16[192,1152]{1,0:T(8,128)(2,1)S(1)} %copy-done.3, bf16[192,1152]{1,0:T(8,128)(2,1)} %collective-permute-done.3.refs_3_, ...), custom_call_target="tpu_custom_call" | custom-call | flops 955514880 | bytes 4190208 | tf_op jit(solution)/shard_map/qkv_first/pallas_call | solution.py:254
  80.8 0.0 copy-start.5
  80.8 0.8 copy-done.5
  81.6 0.0 copy-start.4
  81.6 0.0 all-gather.3.cloned.1.call-done
  81.6 0.0 copy-start.6
  81.6 0.7 slice_bitcast_fusion.refs_1_
  82.4 0.0 collective-permute-done.5.right_ref.refs_0_
  82.4 0.4 collective-permute-done.6.left_ref.refs_1_
  82.8 4.9 %collective-permute-start.7 = (bf16[192,1152]{1,0:T(8,128)(2,1)S(1)}, bf16[192,1152]{1,0:T(8,128)(2,1)S(1)}, u32[]{:S(2)}, u32[]{:S(2)}) collective-permute-start(bf16[192,1152]{1,0:T(8,128)(2,1)S(1)} %pick.1), channel_id=1, source_target_pairs={{0,2},{1,15},{2,4},{3,1},{4,6},{5,3},{6,8},{7,5},{8,10},{9,7},{10,... | collective-permute-start | bytes 1327112 | tf_op jit(solution)/shard_map/ppermute | solution.py:366
  87.7 4.3 %collective-permute-start.8 = (bf16[5,192,256]{2,1,0:T(8,128)(2,1)S(1)}, bf16[5,192,256]{2,1,0:T(8,128)(2,1)S(1)}, u32[]{:S(2)}, u32[]{:S(2)}) collective-permute-start(bf16[5,192,256]{2,1,0:T(8,128)(2,1)S(1)} %get-tuple-element.10.refs_0_), channel_id=1, source_target_pairs={{0,1},{1,0},{2,3},{3,2},{4,5},{5,4},{6,7},{7,6},{8,9},{9,8},{10,11... | collective-permute-start | bytes 1474568 | tf_op jit(solution)/shard_map/ppermute | solution.py:324
  92.1 0.9 collective-permute-done.7.refs_2_
  92.9 1.0 qkv_last.1
  93.9 9.0 %collective-permute-start.9 = (bf16[3,192,256]{2,1,0:T(8,128)(2,1)S(1)}, bf16[3,192,256]{2,1,0:T(8,128)(2,1)S(1)}, u32[]{:S(2)}, u32[]{:S(2)}) collective-permute-start(bf16[3,192,256]{2,1,0:T(8,128)(2,1)S(1)} %get-tuple-element.12), channel_id=1, source_target_pairs={{0,1},{1,0},{2,3},{3,2},{4,5},{5,4},{6,7},{7,6},{8,9},{9,8},{10,11... | collective-permute-start | bytes 884744 | tf_op jit(solution)/shard_map/ppermute | solution.py:324
  102.9 0.0 collective-permute-done.8.refs_2_
  102.9 1.2 collective-permute-done.9.refs_3_
  104.1 0.0 copy-done.4
  104.1 0.0 copy-done.6
  104.1 0.0 copy-start
  104.1 15.2 %attend.1 = bf16[16,112,128]{2,1,0:T(8,128)(2,1)S(1)} custom-call(s32[1]{0:T(128)} %bitcast.me_ref, s32[1,3072]{1,0:T(1,128)S(1)} %copy-done.4, bf16[5,192,256]{2,1,0:T(8,128)(2,1)S(1)} %copy-done.6, bf16[3,192,256]{2,1,0:T(8,128)(2,1)S(1)} %get-tuple-element.11.refs_1_, bf16[5,192,256]{2,1,0:T(8,128)(2,1)S(1)} %collective-permute-done.8.refs_2_, ...), custom_call_target="tpu_custom_call" | custom-call | flops 1358954496 | bytes 2043908 | tf_op jit(solution)/shard_map/attend/pallas_call | solution.py:254
  119.3 21.9 %all_to_all.10.in_ref = bf16[16,112,128]{2,1,0:T(8,128)(2,1)S(1)} all-to-all(bf16[16,112,128]{2,1,0:T(8,128)(2,1)S(1)} %attend.1), channel_id=1, replica_groups=mesh['pack'=32,'seq'=16] {'seq'}, dimensions={0} | all-to-all | bytes 917504 | tf_op jit(solution)/shard_map/all_to_all | solution.py:370
  141.2 0.0 copy-done
  141.2 1.6 %project.1 = bf16[192,1152]{1,0:T(8,128)(2,1)} custom-call(bf16[16,112,128]{2,1,0:T(8,128)(2,1)S(1)} %all_to_all.10.in_ref, bf16[16,72,1152]{2,1,0:T(8,128)(2,1)S(1)} %bitcast.10), custom_call_target="tpu_custom_call" | custom-call | flops 509607936 | bytes 3555328 | tf_op jit(solution)/shard_map/project/pallas_call | solution.py:254
  (1 shorter events, 0.0 us)
Async XLA Ops:
  6.5 75.1 %all-gather.3.cloned.1.call-start = ((), (), s32[]{:S(2)}) async-start(), calls=%async_computation.2 | async-start | bytes 2820096 | tf_op jit(solution)/shard_map/all_gather | solution.py:338
  7.3 15.8 %copy-start.1 = (bf16[3,1152,72]{1,2,0:T(8,128)(2,1)S(1)}, bf16[3,1152,72]{1,2,0:T(8,128)(2,1)}, u32[]{:S(2)}) copy-start(bf16[3,1152,72]{1,2,0:T(8,128)(2,1)} %param.8) | copy-start | bytes 1492996
  10.1 33.8 %all-to-all-start = ((bf16[32,112,128]{2,1,0:T(8,128)(2,1)}), bf16[32,112,128]{2,1,0:T(8,128)(2,1)S(1)}, u32[]{:S(2)}, u32[]{:S(2)}) async-start(bf16[32,112,128]{2,1,0:T(8,128)(2,1)} %pack_rows.1), calls=%async_computation | async-start | bytes 1835008 | tf_op jit(solution)/shard_map/all_to_all | solution.py:335
  23.0 4.6 %collective-permute-start = (bf16[216,1152]{1,0:T(8,128)(2,1)S(1)}, bf16[216,1152]{1,0:T(8,128)(2,1)S(1)}, u32[]{:S(2)}, u32[]{:S(2)}) collective-permute-start(bf16[216,1152]{1,0:T(8,128)(2,1)S(1)} %bitcast.11), channel_id=1, source_target_pairs={{0,1},{1,0},{2,3},{3,2},{4,5},{5,4},{6,7},{7,6},{8,9},{9,8},{10,11... | collective-permute-start | bytes 1493000 | tf_op jit(solution)/shard_map/ppermute | solution.py:324
  45.1 14.1 %collective-permute-start.1 = (bf16[192,1152]{1,0:T(8,128)(2,1)S(1)}, bf16[192,1152]{1,0:T(8,128)(2,1)S(1)}, u32[]{:S(2)}, u32[]{:S(2)}) collective-permute-start(bf16[192,1152]{1,0:T(8,128)(2,1)S(1)} %unpack_rows.1.refs_0_), channel_id=1, source_target_pairs={{0,2},{1,3},{2,4},{3,5},{4,6},{5,7},{6,8},{7,9},{8,10},{9,11},{10,... | collective-permute-start | bytes 1327112 | tf_op jit(solution)/shard_map/ppermute | solution.py:312
  48.3 13.1 %collective-permute-start.2 = (bf16[192,1152]{1,0:T(8,128)(2,1)S(1)}, bf16[192,1152]{1,0:T(8,128)(2,1)S(1)}, u32[]{:S(2)}, u32[]{:S(2)}) collective-permute-start(bf16[192,1152]{1,0:T(8,128)(2,1)S(1)} %unpack_rows.1.refs_0_), channel_id=1, source_target_pairs={{0,14},{1,15},{2,0},{3,1},{4,2},{5,3},{6,4},{7,5},{8,6},{9,7},{10,... | collective-permute-start | bytes 1327112 | tf_op jit(solution)/shard_map/ppermute | solution.py:312
  59.2 11.5 %collective-permute-start.3 = (bf16[192,1152]{1,0:T(8,128)(2,1)S(1)}, bf16[192,1152]{1,0:T(8,128)(2,1)}, u32[]{:S(2)}, u32[]{:S(2)}) collective-permute-start(bf16[192,1152]{1,0:T(8,128)(2,1)S(1)} %collective-permute-done.1.refs_1_), channel_id=1, source_target_pairs={{0,2},{1,3},{2,4},{3,5},{4,6},{5,7},{6,8},{7,9},{8,10},{9,11},{10,... | collective-permute-start | bytes 1327112 | tf_op jit(solution)/shard_map/ppermute | solution.py:312
  61.4 11.2 %collective-permute-start.4 = (bf16[192,1152]{1,0:T(8,128)(2,1)S(1)}, bf16[192,1152]{1,0:T(8,128)(2,1)}, u32[]{:S(2)}, u32[]{:S(2)}) collective-permute-start(bf16[192,1152]{1,0:T(8,128)(2,1)S(1)} %collective-permute-done.2.refs_2_), channel_id=1, source_target_pairs={{0,14},{1,15},{2,0},{3,1},{4,2},{5,3},{6,4},{7,5},{8,6},{9,7},{10,... | collective-permute-start | bytes 1327112 | tf_op jit(solution)/shard_map/ppermute | solution.py:312
  65.7 0.8 copy-start.2
  70.7 11.7 %collective-permute-start.5 = (bf16[192,1152]{1,0:T(8,128)(2,1)}, bf16[192,1152]{1,0:T(8,128)(2,1)S(1)}, u32[]{:S(2)}, u32[]{:S(2)}) collective-permute-start(bf16[192,1152]{1,0:T(8,128)(2,1)} %collective-permute-done.3.refs_3_), channel_id=1, source_target_pairs={{0,2},{1,3},{2,4},{3,5},{4,6},{5,7},{6,8},{7,9},{8,10},{9,11},{10,... | collective-permute-start | bytes 1327112 | tf_op jit(solution)/shard_map/ppermute | solution.py:312
  72.6 10.1 %collective-permute-start.6 = (bf16[192,1152]{1,0:T(8,128)(2,1)}, bf16[192,1152]{1,0:T(8,128)(2,1)S(1)}, u32[]{:S(2)}, u32[]{:S(2)}) collective-permute-start(bf16[192,1152]{1,0:T(8,128)(2,1)} %collective-permute-done.4.refs_4_), channel_id=1, source_target_pairs={{0,14},{1,15},{2,0},{3,1},{4,2},{5,3},{6,4},{7,5},{8,6},{9,7},{10,... | collective-permute-start | bytes 1327112 | tf_op jit(solution)/shard_map/ppermute | solution.py:312
  77.2 1.0 copy-start.3
  80.8 0.8 copy-start.5
  81.6 22.4 %copy-start.4 = (s32[1,3072]{1,0:T(1,128)S(1)}, s32[1,3072]{1,0:T(1,128)}, u32[]{:S(2)}) copy-start(s32[1,3072]{1,0:T(1,128)} %doc_ref.1) | copy-start | bytes 36868
  81.6 22.4 %copy-start.6 = (bf16[5,192,256]{2,1,0:T(8,128)(2,1)S(1)}, bf16[5,192,256]{2,1,0:T(8,128)(2,1)}, u32[]{:S(2)}) copy-start(bf16[5,192,256]{2,1,0:T(8,128)(2,1)} %copy-done.5) | copy-start | bytes 1474564
  82.8 10.2 %collective-permute-start.7 = (bf16[192,1152]{1,0:T(8,128)(2,1)S(1)}, bf16[192,1152]{1,0:T(8,128)(2,1)S(1)}, u32[]{:S(2)}, u32[]{:S(2)}) collective-permute-start(bf16[192,1152]{1,0:T(8,128)(2,1)S(1)} %pick.1), channel_id=1, source_target_pairs={{0,2},{1,15},{2,4},{3,1},{4,6},{5,3},{6,8},{7,5},{8,10},{9,7},{10,... | collective-permute-start | bytes 1327112 | tf_op jit(solution)/shard_map/ppermute | solution.py:366
  87.7 15.2 %collective-permute-start.8 = (bf16[5,192,256]{2,1,0:T(8,128)(2,1)S(1)}, bf16[5,192,256]{2,1,0:T(8,128)(2,1)S(1)}, u32[]{:S(2)}, u32[]{:S(2)}) collective-permute-start(bf16[5,192,256]{2,1,0:T(8,128)(2,1)S(1)} %get-tuple-element.10.refs_0_), channel_id=1, source_target_pairs={{0,1},{1,0},{2,3},{3,2},{4,5},{5,4},{6,7},{7,6},{8,9},{9,8},{10,11... | collective-permute-start | bytes 1474568 | tf_op jit(solution)/shard_map/ppermute | solution.py:324
  93.9 10.2 %collective-permute-start.9 = (bf16[3,192,256]{2,1,0:T(8,128)(2,1)S(1)}, bf16[3,192,256]{2,1,0:T(8,128)(2,1)S(1)}, u32[]{:S(2)}, u32[]{:S(2)}) collective-permute-start(bf16[3,192,256]{2,1,0:T(8,128)(2,1)S(1)} %get-tuple-element.12), channel_id=1, source_target_pairs={{0,1},{1,0},{2,3},{3,2},{4,5},{5,4},{6,7},{7,6},{8,9},{9,8},{10,11... | collective-permute-start | bytes 884744 | tf_op jit(solution)/shard_map/ppermute | solution.py:324
  104.1 37.1 %copy-start = (bf16[1152,1152]{1,0:T(8,128)(2,1)S(1)}, bf16[1152,1152]{1,0:T(8,128)(2,1)}, u32[]{:S(2)}) copy-start(bf16[1152,1152]{1,0:T(8,128)(2,1)} %all-gather.3.cloned.1.call-done) | copy-start | bytes 7962628
Sparse Core Ops, SparseCore 0:
  9.5 48.3 all-gather.2

commit v11 on v9

--- a/solution.py
+++ b/solution.py
@@ -106,8 +106,10 @@
     return 2 * chip + (core if n < chips else 1 - core)
 
 
-def qkv_kernel(*refs):
-    *x_refs, mine_w_ref, pair_w_ref, mine_ref, pair_ref = refs
+def qkv_kernel(count, *refs):
+    x_refs = refs[:count]
+    mine_w_ref, pair_w_ref = refs[count : count + 2]
+    mine_ref, pair_ref = refs[-2:]
     x = jnp.concatenate([ref[...] for ref in x_refs], axis=0)
     rows = x.shape[0]
     scale = jnp.where(iota((1, 3 * HD), 1) < HD, math.log2(math.e) / math.sqrt(HD), 1.0)
@@ -263,12 +265,19 @@
     )(*operands, *behind)
 
 
-def project_qkv(blocks, mine_w, pair_w, name):
+def project_qkv(blocks, mine_w, pair_w, name, behind=()):
     rows = sum(x.shape[0] for x in blocks)
     out = jax.ShapeDtypeStruct((rows // TOK, TOK, QKV), BF)
     flops = 2 * rows * mine_w.shape[1] * 6 * HD
     return local_call(
-        qkv_kernel, (out, out), *blocks, mine_w, pair_w, name=name, flops=flops
+        functools.partial(qkv_kernel, len(blocks)),
+        (out, out),
+        *blocks,
+        mine_w,
+        pair_w,
+        name=name,
+        flops=flops,
+        behind=behind,
     )
 
 
@@ -350,7 +359,9 @@
     for _ in range(3):
         right, left = ring_step(right, left, n_seq)
         held += [right, left]
-    mine, theirs = project_qkv(held[:5], w_t, pair_w, "qkv_first")
+    mine, theirs = project_qkv(
+        held[:5], w_t, pair_w, "qkv_first", behind=(w_all[0, 0:16, 0:LANES],)
+    )
     picked = local_call(
         pick_kernel,
         shape((TOK, width), BF),

time: 156 us -> 149 us (0.955)
  waiting for transfers between devices: 45.2 us -> 40.3 us
  Pallas kernels: 18.6 us -> 21.8 us
  blocking collectives: 23.7 us -> 21 us
    ppermute x6, waiting for transfers between devices: 22.9 us -> 15.6 us  [ring_step(): return (lax.ppermute(right, 'seq', up), lax.ppermute(left, 'seq', down))]
    pallas_call x7, Pallas kernels: 18.6 us -> 21.8 us  [local_call(): pl.pallas_call(kernel, out_shape=out_shape, in_specs=[smem] * small + [vm...]
    all_to_all x1, blocking collectives: 23.7 us -> 21 us  [body(): lax.all_to_all(attended, 'seq', split_axis=0, concat_axis=0, tiled=True)]
    unnamed x6, local copies, waits for them, and re-layouts: 1.76 us -> 0.01 us
  transfers between devices with their start and end apart: 12 -> 12, of which waited for: 9 -> 8; matrix products, arithmetic and copies ran while one was open for 0% -> 0% of each run, Pallas kernels for 9% -> 5%
where the time goes in v11:
time: 149 us
  starting transfers between devices  51.5 us (35%)
  waiting for transfers between devices  40.3 us (27%)
  Pallas kernels  21.8 us (15%)
  blocking collectives  21 us (14%)
  between operations  13.6 us (9%)
    pallas_call x7, Pallas kernels, local_call(): pl.pallas_call(kernel, out_shape=out_shape, in_specs=[smem] * small + [vm...  21.8 us
    all_to_all x1, blocking collectives, body(): lax.all_to_all(attended, 'seq', split_axis=0, concat_axis=0, tiled=True)  21 us
    ppermute x6, starting transfers between devices, ring_step(): return (lax.ppermute(right, 'seq', up), lax.ppermute(left, 'seq', down))  20 us
    all_to_all x1, waiting for transfers between devices, body(): lax.all_to_all(outbox, 'pack', split_axis=0, concat_axis=0, tiled=True)  19.3 us
    ppermute x6, waiting for transfers between devices, ring_step(): return (lax.ppermute(right, 'seq', up), lax.ppermute(left, 'seq', down))  15.6 us
    ppermute x3, starting transfers between devices, other_core(): return lax.ppermute(x, 'seq', [(i, i ^ 1) for i in range(n_seq)])  14.3 us
    all_to_all x1, starting transfers between devices, body(): lax.all_to_all(outbox, 'pack', split_axis=0, concat_axis=0, tiled=True)  12 us
    ppermute x1, starting transfers between devices, body(): held.append(lax.ppermute(picked, 'seq', ways))  5.21 us
  transfers between devices with their start and end apart: 12, of which 8 were waited for; matrix products, arithmetic and copies ran while one was open for 0% of the time, Pallas kernels for 5%

profile of v11, /device:TPU:67, one launch (start us, length us, event | category | flops | bytes accessed | tf_op | source)
XLA Modules:
  0.0 148.8 jit_solution(4118137898206627733)
XLA Ops:
  6.5 0.0 all-gather.3.cloned.1.call-start
  6.5 0.7 all-gather.3.cloned.1.call-update
  7.3 0.0 copy-start.1
  7.3 2.9 %pack_rows.1 = bf16[32,112,128]{2,1,0:T(8,128)(2,1)} custom-call(s32[1,192]{1,0:T(1,128)} %dest_ref.1, bf16[192,1152]{1,0:T(8,128)(2,1)} %bitcast.14), custom_call_target="tpu_custom_call" | custom-call | flops 1000000000 | bytes 1360640 | tf_op jit(solution)/shard_map/pack_rows/pallas_call | solution.py:256
  10.1 12.0 %all-to-all-start = ((bf16[32,112,128]{2,1,0:T(8,128)(2,1)}), bf16[32,112,128]{2,1,0:T(8,128)(2,1)S(1)}, u32[]{:S(2)}, u32[]{:S(2)}) async-start(bf16[32,112,128]{2,1,0:T(8,128)(2,1)} %pack_rows.1), calls=%async_computation | async-start | bytes 1835008 | tf_op jit(solution)/shard_map/all_to_all | solution.py:344
  22.1 0.0 copy-done.1
  22.2 3.1 %collective-permute-start = (bf16[216,1152]{1,0:T(8,128)(2,1)S(1)}, bf16[216,1152]{1,0:T(8,128)(2,1)S(1)}, u32[]{:S(2)}, u32[]{:S(2)}) collective-permute-start(bf16[216,1152]{1,0:T(8,128)(2,1)S(1)} %bitcast.11), channel_id=1, source_target_pairs={{0,1},{1,0},{2,3},{3,2},{4,5},{5,4},{6,7},{7,6},{8,9},{9,8},{10,11... | collective-permute-start | bytes 1493000 | tf_op jit(solution)/shard_map/ppermute | solution.py:333
  25.3 1.5 collective-permute-done.refs_0_.refs_6_.refs_4_
  26.8 19.3 %all-to-all-done.in_ref = bf16[32,112,128]{2,1,0:T(8,128)(2,1)S(1)} async-done(((bf16[32,112,128]{2,1,0:T(8,128)(2,1)}), bf16[32,112,128]{2,1,0:T(8,128)(2,1)S(1)}, u32[]{:S(2)}, u32[]{:S(2)}) %all-to-all-start) | async-done | bytes 917536 | tf_op jit(solution)/shard_map/all_to_all | solution.py:344
  46.1 1.1 unpack_rows.1.refs_0_
  47.2 3.2 %collective-permute-start.1 = (bf16[192,1152]{1,0:T(8,128)(2,1)S(1)}, bf16[192,1152]{1,0:T(8,128)(2,1)S(1)}, u32[]{:S(2)}, u32[]{:S(2)}) collective-permute-start(bf16[192,1152]{1,0:T(8,128)(2,1)S(1)} %unpack_rows.1.refs_0_), channel_id=1, source_target_pairs={{0,2},{1,3},{2,4},{3,5},{4,6},{5,7},{6,8},{7,9},{8,10},{9,11},{10,... | collective-permute-start | bytes 1327112 | tf_op jit(solution)/shard_map/ppermute | solution.py:321
  50.4 3.8 %collective-permute-start.2 = (bf16[192,1152]{1,0:T(8,128)(2,1)S(1)}, bf16[192,1152]{1,0:T(8,128)(2,1)S(1)}, u32[]{:S(2)}, u32[]{:S(2)}) collective-permute-start(bf16[192,1152]{1,0:T(8,128)(2,1)S(1)} %unpack_rows.1.refs_0_), channel_id=1, source_target_pairs={{0,14},{1,15},{2,0},{3,1},{4,2},{5,3},{6,4},{7,5},{8,6},{9,7},{10,... | collective-permute-start | bytes 1327112 | tf_op jit(solution)/shard_map/ppermute | solution.py:321
  54.2 7.1 %collective-permute-done.1.refs_1_ = bf16[192,1152]{1,0:T(8,128)(2,1)S(1)} collective-permute-done((bf16[192,1152]{1,0:T(8,128)(2,1)S(1)}, bf16[192,1152]{1,0:T(8,128)(2,1)S(1)}, u32[]{:S(2)}, u32[]{:S(2)}) %collective-permute-start.1) | collective-permute-done | bytes 442400 | tf_op jit(solution)/shard_map/ppermute | solution.py:321
  61.3 1.9 %collective-permute-start.3 = (bf16[192,1152]{1,0:T(8,128)(2,1)S(1)}, bf16[192,1152]{1,0:T(8,128)(2,1)}, u32[]{:S(2)}, u32[]{:S(2)}) collective-permute-start(bf16[192,1152]{1,0:T(8,128)(2,1)S(1)} %collective-permute-done.1.refs_1_), channel_id=1, source_target_pairs={{0,2},{1,3},{2,4},{3,5},{4,6},{5,7},{6,8},{7,9},{8,10},{9,11},{10,... | collective-permute-start | bytes 1327112 | tf_op jit(solution)/shard_map/ppermute | solution.py:321
  63.3 0.0 collective-permute-done.2.refs_2_
  63.3 4.6 %collective-permute-start.4 = (bf16[192,1152]{1,0:T(8,128)(2,1)S(1)}, bf16[192,1152]{1,0:T(8,128)(2,1)}, u32[]{:S(2)}, u32[]{:S(2)}) collective-permute-start(bf16[192,1152]{1,0:T(8,128)(2,1)S(1)} %collective-permute-done.2.refs_2_), channel_id=1, source_target_pairs={{0,14},{1,15},{2,0},{3,1},{4,2},{5,3},{6,4},{7,5},{8,6},{9,7},{10,... | collective-permute-start | bytes 1327112 | tf_op jit(solution)/shard_map/ppermute | solution.py:321
  67.8 5.8 %collective-permute-done.3.refs_3_ = bf16[192,1152]{1,0:T(8,128)(2,1)} collective-permute-done((bf16[192,1152]{1,0:T(8,128)(2,1)S(1)}, bf16[192,1152]{1,0:T(8,128)(2,1)}, u32[]{:S(2)}, u32[]{:S(2)}) %collective-permute-start.3) | collective-permute-done | bytes 442400 | tf_op jit(solution)/shard_map/ppermute | solution.py:321
  73.7 1.9 %collective-permute-start.5 = (bf16[192,1152]{1,0:T(8,128)(2,1)}, bf16[192,1152]{1,0:T(8,128)(2,1)S(1)}, u32[]{:S(2)}, u32[]{:S(2)}) collective-permute-start(bf16[192,1152]{1,0:T(8,128)(2,1)} %collective-permute-done.3.refs_3_), channel_id=1, source_target_pairs={{0,2},{1,3},{2,4},{3,5},{4,6},{5,7},{6,8},{7,9},{8,10},{9,11},{10,... | collective-permute-start | bytes 1327112 | tf_op jit(solution)/shard_map/ppermute | solution.py:321
  75.6 0.0 collective-permute-done.4.refs_4_
  75.6 4.6 %collective-permute-start.6 = (bf16[192,1152]{1,0:T(8,128)(2,1)}, bf16[192,1152]{1,0:T(8,128)(2,1)S(1)}, u32[]{:S(2)}, u32[]{:S(2)}) collective-permute-start(bf16[192,1152]{1,0:T(8,128)(2,1)} %collective-permute-done.4.refs_4_), channel_id=1, source_target_pairs={{0,14},{1,15},{2,0},{3,1},{4,2},{5,3},{6,4},{7,5},{8,6},{9,7},{10,... | collective-permute-start | bytes 1327112 | tf_op jit(solution)/shard_map/ppermute | solution.py:321
  80.2 0.0 all-gather.3.cloned.1.call-done
  80.2 0.7 slice_bitcast_fusion.refs_7_
  80.9 2.6 %qkv_first.1 = (bf16[5,192,256]{2,1,0:T(8,128)(2,1)S(1)}, bf16[5,192,256]{2,1,0:T(8,128)(2,1)S(1)}) custom-call(bf16[192,1152]{1,0:T(8,128)(2,1)S(1)} %unpack_rows.1.refs_0_, bf16[192,1152]{1,0:T(8,128)(2,1)S(1)} %collective-permute-done.1.refs_1_, bf16[192,1152]{1,0:T(8,128)(2,1)S(1)} %collective-permute-done.2.refs_2_, ...), custom_call_target="tpu_custom_call" | custom-call | flops 955514880 | bytes 4190208 | tf_op jit(solution)/shard_map/qkv_first/pallas_call | solution.py:256
  83.5 0.0 copy-start.2
  83.5 1.7 %collective-permute-done.5.right_ref.refs_0_ = bf16[192,1152]{1,0:T(8,128)(2,1)S(1)} collective-permute-done((bf16[192,1152]{1,0:T(8,128)(2,1)}, bf16[192,1152]{1,0:T(8,128)(2,1)S(1)}, u32[]{:S(2)}, u32[]{:S(2)}) %collective-permute-start.5) | collective-permute-done | bytes 442400 | tf_op jit(solution)/shard_map/ppermute | solution.py:321
  85.2 1.0 collective-permute-done.6.left_ref.refs_1_
  86.3 5.2 %collective-permute-start.7 = (bf16[192,1152]{1,0:T(8,128)(2,1)S(1)}, bf16[192,1152]{1,0:T(8,128)(2,1)S(1)}, u32[]{:S(2)}, u32[]{:S(2)}) collective-permute-start(bf16[192,1152]{1,0:T(8,128)(2,1)S(1)} %pick.1), channel_id=1, source_target_pairs={{0,2},{1,15},{2,4},{3,1},{4,6},{5,3},{6,8},{7,5},{8,10},{9,7},{10,... | collective-permute-start | bytes 1327112 | tf_op jit(solution)/shard_map/ppermute | solution.py:377
  91.5 3.3 %collective-permute-start.8 = (bf16[5,192,256]{2,1,0:T(8,128)(2,1)S(1)}, bf16[5,192,256]{2,1,0:T(8,128)(2,1)S(1)}, u32[]{:S(2)}, u32[]{:S(2)}) collective-permute-start(bf16[5,192,256]{2,1,0:T(8,128)(2,1)S(1)} %get-tuple-element.10.refs_0_), channel_id=1, source_target_pairs={{0,1},{1,0},{2,3},{3,2},{4,5},{5,4},{6,7},{7,6},{8,9},{9,8},{10,11... | collective-permute-start | bytes 1474568 | tf_op jit(solution)/shard_map/ppermute | solution.py:333
  94.8 2.0 %collective-permute-done.7.refs_2_ = bf16[192,1152]{1,0:T(8,128)(2,1)S(1)} collective-permute-done((bf16[192,1152]{1,0:T(8,128)(2,1)S(1)}, bf16[192,1152]{1,0:T(8,128)(2,1)S(1)}, u32[]{:S(2)}, u32[]{:S(2)}) %collective-permute-start.7) | collective-permute-done | bytes 442400 | tf_op jit(solution)/shard_map/ppermute | solution.py:377
  96.7 1.0 qkv_last.1
  97.7 7.9 %collective-permute-start.9 = (bf16[3,192,256]{2,1,0:T(8,128)(2,1)S(1)}, bf16[3,192,256]{2,1,0:T(8,128)(2,1)S(1)}, u32[]{:S(2)}, u32[]{:S(2)}) collective-permute-start(bf16[3,192,256]{2,1,0:T(8,128)(2,1)S(1)} %get-tuple-element.12), channel_id=1, source_target_pairs={{0,1},{1,0},{2,3},{3,2},{4,5},{5,4},{6,7},{7,6},{8,9},{9,8},{10,11... | collective-permute-start | bytes 884744 | tf_op jit(solution)/shard_map/ppermute | solution.py:333
  105.6 0.0 collective-permute-done.8.refs_2_
  105.6 1.2 collective-permute-done.9.refs_3_
  106.8 0.0 copy-done.2
  106.8 0.0 copy-start
  106.8 12.5 %attend.1 = bf16[16,112,128]{2,1,0:T(8,128)(2,1)S(1)} custom-call(s32[1]{0:T(128)} %bitcast.me_ref, s32[1,3072]{1,0:T(1,128)S(1)} %copy-done.2, bf16[5,192,256]{2,1,0:T(8,128)(2,1)S(1)} %get-tuple-element.9.refs_0_, bf16[3,192,256]{2,1,0:T(8,128)(2,1)S(1)} %get-tuple-element.11.refs_1_, bf16[5,192,256]{2,1,0:T(8,128)(2,1)S(1)} %collective-permute-done.8.refs_2_, ...), custom_call_target="tpu_custom_call" | custom-call | flops 1358954496 | bytes 2043908 | tf_op jit(solution)/shard_map/attend/pallas_call | solution.py:256
  119.3 21.0 %all_to_all.10.in_ref = bf16[16,112,128]{2,1,0:T(8,128)(2,1)S(1)} all-to-all(bf16[16,112,128]{2,1,0:T(8,128)(2,1)S(1)} %attend.1), channel_id=1, replica_groups=mesh['pack'=32,'seq'=16] {'seq'}, dimensions={0} | all-to-all | bytes 917504 | tf_op jit(solution)/shard_map/all_to_all | solution.py:381
  140.3 0.0 copy-done
  140.3 1.6 %project.1 = bf16[192,1152]{1,0:T(8,128)(2,1)} custom-call(bf16[16,112,128]{2,1,0:T(8,128)(2,1)S(1)} %all_to_all.10.in_ref, bf16[16,72,1152]{2,1,0:T(8,128)(2,1)S(1)} %bitcast.10), custom_call_target="tpu_custom_call" | custom-call | flops 509607936 | bytes 3555328 | tf_op jit(solution)/shard_map/project/pallas_call | solution.py:256
  (1 shorter events, 0.0 us)
Async XLA Ops:
  6.5 73.7 %all-gather.3.cloned.1.call-start = ((), (), s32[]{:S(2)}) async-start(), calls=%async_computation.2 | async-start | bytes 2820096 | tf_op jit(solution)/shard_map/all_gather | solution.py:347
  7.3 14.9 %copy-start.1 = (bf16[3,1152,72]{1,2,0:T(8,128)(2,1)S(1)}, bf16[3,1152,72]{1,2,0:T(8,128)(2,1)}, u32[]{:S(2)}) copy-start(bf16[3,1152,72]{1,2,0:T(8,128)(2,1)} %param.8) | copy-start | bytes 1492996
  10.1 35.9 %all-to-all-start = ((bf16[32,112,128]{2,1,0:T(8,128)(2,1)}), bf16[32,112,128]{2,1,0:T(8,128)(2,1)S(1)}, u32[]{:S(2)}, u32[]{:S(2)}) async-start(bf16[32,112,128]{2,1,0:T(8,128)(2,1)} %pack_rows.1), calls=%async_computation | async-start | bytes 1835008 | tf_op jit(solution)/shard_map/all_to_all | solution.py:344
  22.2 4.6 %collective-permute-start = (bf16[216,1152]{1,0:T(8,128)(2,1)S(1)}, bf16[216,1152]{1,0:T(8,128)(2,1)S(1)}, u32[]{:S(2)}, u32[]{:S(2)}) collective-permute-start(bf16[216,1152]{1,0:T(8,128)(2,1)S(1)} %bitcast.11), channel_id=1, source_target_pairs={{0,1},{1,0},{2,3},{3,2},{4,5},{5,4},{6,7},{7,6},{8,9},{9,8},{10,11... | collective-permute-start | bytes 1493000 | tf_op jit(solution)/shard_map/ppermute | solution.py:333
  47.2 14.1 %collective-permute-start.1 = (bf16[192,1152]{1,0:T(8,128)(2,1)S(1)}, bf16[192,1152]{1,0:T(8,128)(2,1)S(1)}, u32[]{:S(2)}, u32[]{:S(2)}) collective-permute-start(bf16[192,1152]{1,0:T(8,128)(2,1)S(1)} %unpack_rows.1.refs_0_), channel_id=1, source_target_pairs={{0,2},{1,3},{2,4},{3,5},{4,6},{5,7},{6,8},{7,9},{8,10},{9,11},{10,... | collective-permute-start | bytes 1327112 | tf_op jit(solution)/shard_map/ppermute | solution.py:321
  50.4 12.8 %collective-permute-start.2 = (bf16[192,1152]{1,0:T(8,128)(2,1)S(1)}, bf16[192,1152]{1,0:T(8,128)(2,1)S(1)}, u32[]{:S(2)}, u32[]{:S(2)}) collective-permute-start(bf16[192,1152]{1,0:T(8,128)(2,1)S(1)} %unpack_rows.1.refs_0_), channel_id=1, source_target_pairs={{0,14},{1,15},{2,0},{3,1},{4,2},{5,3},{6,4},{7,5},{8,6},{9,7},{10,... | collective-permute-start | bytes 1327112 | tf_op jit(solution)/shard_map/ppermute | solution.py:321
  61.3 12.3 %collective-permute-start.3 = (bf16[192,1152]{1,0:T(8,128)(2,1)S(1)}, bf16[192,1152]{1,0:T(8,128)(2,1)}, u32[]{:S(2)}, u32[]{:S(2)}) collective-permute-start(bf16[192,1152]{1,0:T(8,128)(2,1)S(1)} %collective-permute-done.1.refs_1_), channel_id=1, source_target_pairs={{0,2},{1,3},{2,4},{3,5},{4,6},{5,7},{6,8},{7,9},{8,10},{9,11},{10,... | collective-permute-start | bytes 1327112 | tf_op jit(solution)/shard_map/ppermute | solution.py:321
  63.3 12.3 %collective-permute-start.4 = (bf16[192,1152]{1,0:T(8,128)(2,1)S(1)}, bf16[192,1152]{1,0:T(8,128)(2,1)}, u32[]{:S(2)}, u32[]{:S(2)}) collective-permute-start(bf16[192,1152]{1,0:T(8,128)(2,1)S(1)} %collective-permute-done.2.refs_2_), channel_id=1, source_target_pairs={{0,14},{1,15},{2,0},{3,1},{4,2},{5,3},{6,4},{7,5},{8,6},{9,7},{10,... | collective-permute-start | bytes 1327112 | tf_op jit(solution)/shard_map/ppermute | solution.py:321
  73.7 11.5 %collective-permute-start.5 = (bf16[192,1152]{1,0:T(8,128)(2,1)}, bf16[192,1152]{1,0:T(8,128)(2,1)S(1)}, u32[]{:S(2)}, u32[]{:S(2)}) collective-permute-start(bf16[192,1152]{1,0:T(8,128)(2,1)} %collective-permute-done.3.refs_3_), channel_id=1, source_target_pairs={{0,2},{1,3},{2,4},{3,5},{4,6},{5,7},{6,8},{7,9},{8,10},{9,11},{10,... | collective-permute-start | bytes 1327112 | tf_op jit(solution)/shard_map/ppermute | solution.py:321
  75.6 10.6 %collective-permute-start.6 = (bf16[192,1152]{1,0:T(8,128)(2,1)}, bf16[192,1152]{1,0:T(8,128)(2,1)S(1)}, u32[]{:S(2)}, u32[]{:S(2)}) collective-permute-start(bf16[192,1152]{1,0:T(8,128)(2,1)} %collective-permute-done.4.refs_4_), channel_id=1, source_target_pairs={{0,14},{1,15},{2,0},{3,1},{4,2},{5,3},{6,4},{7,5},{8,6},{9,7},{10,... | collective-permute-start | bytes 1327112 | tf_op jit(solution)/shard_map/ppermute | solution.py:321
  83.5 23.2 %copy-start.2 = (s32[1,3072]{1,0:T(1,128)S(1)}, s32[1,3072]{1,0:T(1,128)}, u32[]{:S(2)}) copy-start(s32[1,3072]{1,0:T(1,128)} %doc_ref.1) | copy-start | bytes 36868
  86.3 10.4 %collective-permute-start.7 = (bf16[192,1152]{1,0:T(8,128)(2,1)S(1)}, bf16[192,1152]{1,0:T(8,128)(2,1)S(1)}, u32[]{:S(2)}, u32[]{:S(2)}) collective-permute-start(bf16[192,1152]{1,0:T(8,128)(2,1)S(1)} %pick.1), channel_id=1, source_target_pairs={{0,2},{1,15},{2,4},{3,1},{4,6},{5,3},{6,8},{7,5},{8,10},{9,7},{10,... | collective-permute-start | bytes 1327112 | tf_op jit(solution)/shard_map/ppermute | solution.py:377
  91.5 14.1 %collective-permute-start.8 = (bf16[5,192,256]{2,1,0:T(8,128)(2,1)S(1)}, bf16[5,192,256]{2,1,0:T(8,128)(2,1)S(1)}, u32[]{:S(2)}, u32[]{:S(2)}) collective-permute-start(bf16[5,192,256]{2,1,0:T(8,128)(2,1)S(1)} %get-tuple-element.10.refs_0_), channel_id=1, source_target_pairs={{0,1},{1,0},{2,3},{3,2},{4,5},{5,4},{6,7},{7,6},{8,9},{9,8},{10,11... | collective-permute-start | bytes 1474568 | tf_op jit(solution)/shard_map/ppermute | solution.py:333
  97.7 9.1 %collective-permute-start.9 = (bf16[3,192,256]{2,1,0:T(8,128)(2,1)S(1)}, bf16[3,192,256]{2,1,0:T(8,128)(2,1)S(1)}, u32[]{:S(2)}, u32[]{:S(2)}) collective-permute-start(bf16[3,192,256]{2,1,0:T(8,128)(2,1)S(1)} %get-tuple-element.12), channel_id=1, source_target_pairs={{0,1},{1,0},{2,3},{3,2},{4,5},{5,4},{6,7},{7,6},{8,9},{9,8},{10,11... | collective-permute-start | bytes 884744 | tf_op jit(solution)/shard_map/ppermute | solution.py:333
  106.8 33.5 %copy-start = (bf16[1152,1152]{1,0:T(8,128)(2,1)S(1)}, bf16[1152,1152]{1,0:T(8,128)(2,1)}, u32[]{:S(2)}) copy-start(bf16[1152,1152]{1,0:T(8,128)(2,1)} %all-gather.3.cloned.1.call-done) | copy-start | bytes 7962628
Sparse Core Ops, SparseCore 0:
  9.5 47.4 all-gather.2
